TPU v7x, 256 devices: a whole 4x4x8 slice. The times are simulated.
256 devices in a mesh: row: 16 (over y, z_lo), col: 8 (over x, z_hi), depth: 2 (over core).
Axes of the slice: x: 4, y: 4, z: 8 (z_hi: 2, z_lo: 4; z = z_hi * 4 + z_lo), core: 2. Of those that a mesh axis runs over, the one named last changes fastest.
Arguments:
- pair: bfloat16 [512, 512, 128], P('row', ('col', 'depth')), may hold values from -6 to 6
- grad_out: bfloat16 [512, 512, 128], P('row', ('col', 'depth')), may hold values from -6 to 6
- pair_mask: int32 [512, 512], P('row', ('col', 'depth')), may hold values 0 or 1
- ln_in_gain: float32 [128], replicated, may hold values from 0.5 to 1.5
- ln_in_bias: float32 [128], replicated, may hold values from -3 to 3
- in_proj: bfloat16 [128, 512], replicated, may hold values from -0.5 to 0.5
- w_gate: bfloat16 [128, 128], replicated, may hold values from -0.5 to 0.5
- inner_norm_gain: float32 [128], replicated, may hold values from 0.5 to 1.5
- inner_norm_bias: float32 [128], replicated, may hold values from -3 to 3
- w_out: bfloat16 [128, 128], replicated, may hold values from -0.5 to 0.5
Outputs:
- grad_pair: bfloat16 [512, 512, 128], P('row', ('col', 'depth'))
- grad_in_proj: float32 [128, 512], replicated
- grad_w_gate: float32 [128, 128], replicated
- grad_w_out: float32 [128, 128], replicated
- grad_ln_in: float32 [2, 128], replicated
- inner_norm_gradients: float32 [2, 128], replicated
All inputs are finite; a program needn't handle non-finite values. No bound on the sum of `pair_mask` on one device may be relied on, other than what follows from the above.
Results may differ from a plain program's by a relative error of at most 0.02.
Values may be sent and summed in bfloat16 or wider, within the bound.
No kernel may reach another device: no remote copies, remote signals or barrier semaphores. Data moves between devices by JAX's collectives and lax.ppermute only.
A program may use at most 64 MiB of HBM per device.

v0:
```python
import jax
import jax.numpy as jnp
from jax import lax
from jax.sharding import PartitionSpec as P


def broadcast(x, axis, root):
    mine = lax.axis_index(axis) == root
    return lax.psum(jnp.where(mine, x, jnp.zeros_like(x)), axis)


def layer_norm_forward(value, gain, bias):
    centre = value - jnp.mean(value, axis=-1, keepdims=True)
    inverse = lax.rsqrt(jnp.mean(centre * centre, axis=-1, keepdims=True) + 1e-05)
    scaled = centre * inverse
    return (scaled * gain + bias, scaled, inverse)


def layer_norm_backward(grad, scaled, inverse, gain):
    tangent = grad * gain
    first = jnp.mean(tangent, axis=-1, keepdims=True)
    second = jnp.mean(tangent * scaled, axis=-1, keepdims=True)
    return inverse * (tangent - first - scaled * second)


def per_device(
    pair,
    grad_out,
    pair_mask,
    ln_in_gain,
    ln_in_bias,
    in_proj,
    w_gate,
    inner_norm_gain,
    inner_norm_bias,
    w_out,
):
    tile_rows, width, chans = pair.shape
    hidden_width = w_out.shape[0]
    cells = tile_rows * width
    ratio = lax.axis_size("row") // lax.axis_size("col")
    col_index = lax.axis_index("col")
    row_index = lax.axis_index("row")
    zf = pair.astype(jnp.float32).reshape(cells, chans)
    zn, zhat, zinv = layer_norm_forward(zf, ln_in_gain, ln_in_bias)
    normed = zn.astype(jnp.bfloat16)
    proj = jnp.dot(normed, in_proj, preferred_element_type=jnp.float32)
    maskf = pair_mask.astype(jnp.float32).reshape(cells, 1)
    a_val = proj[:, :hidden_width]
    sig_a = jax.nn.sigmoid(proj[:, hidden_width : 2 * hidden_width])
    b_val = proj[:, 2 * hidden_width : 3 * hidden_width]
    sig_b = jax.nn.sigmoid(proj[:, 3 * hidden_width :])
    left = (sig_a * a_val * maskf).astype(jnp.bfloat16).reshape(tile_rows, width, hidden_width)
    right = (sig_b * b_val * maskf).astype(jnp.bfloat16).reshape(tile_rows, width, hidden_width)
    left_slab = lax.all_gather(left, "col", axis=1, tiled=True)
    right_slab = lax.all_gather(right, "col", axis=1, tiled=True)
    right_parts = [broadcast(right_slab, "row", col_index * ratio + half) for half in range(ratio)]
    right_panel = jnp.concatenate(right_parts, axis=0)
    partial_inner = jnp.einsum(
        "ikh,jkh->ijh", left_slab, right_panel, preferred_element_type=jnp.float32
    )
    inner_product = (
        lax.psum_scatter(
            partial_inner.astype(jnp.bfloat16), "depth", scatter_dimension=1, tiled=True
        )
        .astype(jnp.float32)
        .reshape(cells, hidden_width)
    )
    normalised_input, centred_scaled_input, inverse_deviation = layer_norm_forward(
        inner_product, inner_norm_gain, inner_norm_bias
    )
    xnorm = normalised_input.astype(jnp.bfloat16)
    outp = jnp.dot(xnorm, w_out, preferred_element_type=jnp.float32)
    gate = jax.nn.sigmoid(jnp.dot(normed, w_gate, preferred_element_type=jnp.float32))
    upstream = grad_out.astype(jnp.float32).reshape(cells, chans)
    d_out_proj = (upstream * gate).astype(jnp.bfloat16)
    d_gate_pre = (upstream * outp * gate * (1.0 - gate)).astype(jnp.bfloat16)
    normed_input_grad = jnp.dot(d_out_proj, w_out.T, preferred_element_type=jnp.float32)
    local_w_out = jnp.einsum("pa,pb->ab", xnorm, d_out_proj, preferred_element_type=jnp.float32)
    local_inner_norm = jnp.stack(
        [
            jnp.sum(normed_input_grad * centred_scaled_input, axis=0),
            jnp.sum(normed_input_grad, axis=0),
        ]
    )
    input_gradient = (
        layer_norm_backward(
            normed_input_grad, centred_scaled_input, inverse_deviation, inner_norm_gain
        )
        .astype(jnp.bfloat16)
        .reshape(tile_rows, width, hidden_width)
    )
    grad_strip = lax.all_gather(input_gradient, "depth", axis=1, tiled=True)
    right_cols = lax.all_gather(right, "row", axis=0, tiled=True)
    grad_rows = lax.all_gather(input_gradient, ("col", "depth"), axis=1, tiled=True)
    grad_a = jnp.einsum("ijh,jkh->ikh", grad_rows, right_cols, preferred_element_type=jnp.float32)
    partial_b = jnp.einsum(
        "ijh,ikh->jkh", grad_strip, left_slab, preferred_element_type=jnp.float32
    )
    summed_b = lax.psum_scatter(
        partial_b.astype(jnp.bfloat16), "row", scatter_dimension=1, tiled=True
    )
    column_b = lax.all_gather(summed_b, "row", axis=1, tiled=True)
    own_rows = lax.dynamic_slice_in_dim(column_b, row_index % ratio * tile_rows, tile_rows, 0)
    owner_rows = broadcast(own_rows, "col", row_index // ratio)
    grad_b = lax.dynamic_slice_in_dim(owner_rows, col_index * width, width, 1)
    grad_af = grad_a.reshape(cells, hidden_width)
    grad_bf = grad_b.astype(jnp.float32).reshape(cells, hidden_width)
    d_proj = jnp.concatenate(
        [
            grad_af * sig_a * maskf,
            grad_af * a_val * maskf * sig_a * (1.0 - sig_a),
            grad_bf * sig_b * maskf,
            grad_bf * b_val * maskf * sig_b * (1.0 - sig_b),
        ],
        axis=1,
    ).astype(jnp.bfloat16)
    local_in_proj = jnp.einsum("pc,pf->cf", normed, d_proj, preferred_element_type=jnp.float32)
    local_gate = jnp.einsum("pc,pf->cf", normed, d_gate_pre, preferred_element_type=jnp.float32)
    d_normed = jnp.dot(d_proj, in_proj.T, preferred_element_type=jnp.float32) + jnp.dot(
        d_gate_pre, w_gate.T, preferred_element_type=jnp.float32
    )
    local_ln_in = jnp.stack([jnp.sum(d_normed * zhat, axis=0), jnp.sum(d_normed, axis=0)])
    grad_pair = (
        layer_norm_backward(d_normed, zhat, zinv, ln_in_gain)
        .astype(jnp.bfloat16)
        .reshape(tile_rows, width, chans)
    )
    grad_in_proj, grad_w_gate, grad_w_out, grad_ln_in, inner_norm_gradients = lax.psum(
        (local_in_proj, local_gate, local_w_out, local_ln_in, local_inner_norm),
        ("row", "col", "depth"),
    )
    return (grad_pair, grad_in_proj, grad_w_gate, grad_w_out, grad_ln_in, inner_norm_gradients)


def solution(mesh):
    return jax.shard_map(
        per_device,
        mesh=mesh,
        in_specs=(
            P("row", ("col", "depth"), None),
            P("row", ("col", "depth"), None),
            P("row", ("col", "depth")),
            P(),
            P(),
            P(),
            P(),
            P(),
            P(),
            P(),
        ),
        out_specs=(P("row", ("col", "depth"), None), P(), P(), P(), P(), P()),
        check_vma=False,
    )
```

profile of v0, /device:TPU:1, one launch (start us, length us, event | category | flops | bytes accessed | tf_op | source)
XLA Modules:
  0.0 1338.6 jit_solution(16126976695107174041)
XLA Ops:
  7.2 1.2 convert_reduce_fusion
  8.4 1.3 multiply_reduce_fusion.5
  10.7 1.3 add_convert_fusion.1
  12.8 0.8 copy.48
  13.7 0.8 copy.51
  14.6 77.9 %all-gather.8.cloned.1.call-done = bf16[32,256,128]{2,0,1:T(8,128)(2,1)} async-done(((bf16[32,32,128]{2,0,1:T(8,128)(2,1)}), bf16[32,256,128]{2,0,1:T(8,128)(2,1)}) %all-gather.8.cloned.1.call-update) | async-done | bytes 2097168 | tf_op jit(solution)/shard_map/all_gather | solution.py:56
  92.4 4.6 broadcast_select_fusion.1
  97.1 70.3 %all-gather.10.cloned.1.call-done = bf16[32,256,128]{2,0,1:T(8,128)(2,1)} async-done(((bf16[32,32,128]{2,0,1:T(8,128)(2,1)}), bf16[32,256,128]{2,0,1:T(8,128)(2,1)}) %all-gather.10.cloned.1.call-update) | async-done | bytes 2097168 | tf_op jit(solution)/shard_map/all_gather | solution.py:55
  167.4 4.9 copy.53
  172.3 199.0 %all-reduce.11.cloned.1.call-done = (bf16[32,256,128]{2,1,0:T(8,128)(2,1)}, bf16[32,256,128]{2,1,0:T(8,128)(2,1)}) async-done(((bf16[32,256,128]{2,1,0:T(8,128)(2,1)}, bf16[32,256,128]{2,1,0:T(8,128)(2,1)}), (bf16[32,256,128]{2,1,0:T(8,128)(2,1)}, bf16[32,256,128]{2,1,0:T(8,128)(2,1)})) %all-reduce.11.cloned.1.call-update) | async-done | bytes 4194320 | tf_op jit(solution)/shard_map/psum | solution.py:9
  371.4 4.5 pad_maximum_fusion
  375.9 6.8 copy.52
  382.7 4.1 fusion
  386.8 2.3 copy.54
  389.2 2.1 fusion.13
  391.3 9.5 reduce-scatter.3.cloned.1.call-done
  400.8 1.2 convert_reduce_fusion.1
  402.1 1.3 multiply_reduce_fusion.4
  404.2 2.2 multiply_reduce_fusion
  406.3 2.7 multiply_convert_fusion.1
  409.0 2.7 copy.60
  411.7 3.6 all_gather.22
  415.3 3.2 convert_bitcast_fusion
  418.5 7.4 copy.62
  426.0 100.4 %reduce-scatter.5.cloned.1.call-done = bf16[64,16,128]{2,0,1:T(8,128)(2,1)} async-done(((bf16[64,256,128]{2,0,1:T(8,128)(2,1)}), bf16[64,16,128]{2,0,1:T(8,128)(2,1)}) %reduce-scatter.5.cloned.1.call-update) | async-done | bytes 262160 | tf_op jit(solution)/shard_map/reduce_scatter | solution.py:100
  528.1 102.4 %all-gather.14.cloned.1.call-done = bf16[64,256,128]{2,0,1:T(8,128)(2,1)} async-done(((bf16[64,16,128]{2,0,1:T(8,128)(2,1)}), bf16[64,256,128]{2,0,1:T(8,128)(2,1)}) %all-gather.14.cloned.1.call-update) | async-done | bytes 4194320 | tf_op jit(solution)/shard_map/all_gather | solution.py:103
  630.5 2.0 constant_dynamic-slice_fusion.1
  632.4 2.3 copy_select_fusion
  634.8 96.8 %all-gather.6.cloned.1.call-done = bf16[512,32,128]{2,1,0:T(8,128)(2,1)} async-done(((bf16[32,32,128]{2,1,0:T(8,128)(2,1)}), bf16[512,32,128]{2,1,0:T(8,128)(2,1)}) %all-gather.6.cloned.1.call-update) | async-done | bytes 4194320 | tf_op jit(solution)/shard_map/all_gather | solution.py:94
  731.6 8.5 copy.57
  740.9 0.9 fusion.34
  741.8 1.2 fusion.6
  743.0 0.9 fusion.33
  743.9 1.0 fusion.32
  744.9 65.4 %all-gather.12.cloned.1.call-done = bf16[32,512,128]{2,0,1:T(8,128)(2,1)} async-done(((bf16[32,32,128]{2,0,1:T(8,128)(2,1)}), bf16[32,512,128]{2,0,1:T(8,128)(2,1)}) %all-gather.12.cloned.1.call-update) | async-done | bytes 4194320 | tf_op jit(solution)/shard_map/all_gather | solution.py:95
  810.4 8.6 copy.58
  819.0 6.2 convolution_bitcast_fusion
  825.2 2.8 copy.59
  828.0 174.3 %all-reduce.7.cloned.1.call-done = bf16[32,256,128]{2,1,0:T(8,128)(2,1)} async-done(((bf16[32,256,128]{2,1,0:T(8,128)(2,1)}), bf16[32,256,128]{2,1,0:T(8,128)(2,1)}) %all-reduce.7.cloned.1.call-update) | async-done | bytes 2097168 | tf_op jit(solution)/shard_map/psum | solution.py:9
  1002.3 1.0 constant_dynamic-slice_fusion
  1004.7 1.0 fusion.28
  1005.7 1.8 multiply_reduce_fusion.1
  1007.5 74.2 %all-reduce = (f32[2,128]{1,0:T(2,128)}, f32[2,128]{1,0:T(2,128)}) all-reduce(f32[2,128]{1,0:T(2,128)S(1)} %pad_maximum_fusion.4, f32[2,128]{1,0:T(2,128)S(1)} %pad_maximum_fusion.5), channel_id=1, replica_groups=mesh['row'=16,'col'=8,'depth'=2] {'row','col','depth'}, use_global_device_ids=true, to_apply=%region_18.19 | all-reduce | flops 512 | bytes 4096 | tf_op jit(solution)/shard_map/psum | solution.py:129
  1081.8 1.3 multiply_convert_fusion
  1083.1 244.0 %all-reduce.9.cloned.1.call-done = (f32[128,512]{1,0:T(8,128)}, f32[128,128]{1,0:T(8,128)}, f32[128,128]{1,0:T(8,128)}) async-done(((f32[128,512]{1,0:T(8,128)}, f32[128,128]{1,0:T(8,128)}, f32[128,128]{1,0:T(8,128)}), (f32[128,512]{1,0:T(8,128)}, f32[128,128]{1,0:T(8,128)}, f32[128,128]{1,0:T(8,128)})) %all-reduce.9.cloned.1.call-update) | async-done | bytes 393232 | tf_op jit(solution)/shard_map/psum | solution.py:129
  1327.1 1.7 copy.80
  1328.8 1.5 copy.81
  1330.3 1.5 copy.82
  (71 shorter events, 6.6 us)
Async XLA Ops:
  7.2 4.9 copy-start
  7.2 85.3 %all-gather.8.cloned.1.call-start = ((), (), s32[]{:S(2)}) async-start(), calls=%async_computation.3 | async-start | bytes 2359296 | tf_op jit(solution)/shard_map/all_gather | solution.py:56
  12.8 84.3 %copy-start.3 = (bf16[1024,128]{1,0:T(8,128)(2,1)}, bf16[1024,128]{1,0:T(8,128)(2,1)S(1)}, u32[]{:S(2)}) copy-start(bf16[1024,128]{1,0:T(8,128)(2,1)S(1)} %get-tuple-element.28) | copy-start | bytes 786436
  13.6 153.8 %all-gather.10.cloned.1.call-start = ((), (), s32[]{:S(2)}) async-start(), calls=%async_computation.4 | async-start | bytes 2359296 | tf_op jit(solution)/shard_map/all_gather | solution.py:55
  14.5 356.9 %all-reduce.11.cloned.1.call-start = ((), (), s32[]{:S(2)}) async-start(), calls=%async_computation.11 | async-start | bytes 8388608 | tf_op jit(solution)/shard_map/psum | solution.py:9
  97.1 303.8 %reduce-scatter.3.cloned.1.call-start = ((), (), s32[]{:S(2)}) async-start(), calls=%async_computation.5 | async-start | bytes 786432 | tf_op jit(solution)/shard_map/reduce_scatter | solution.py:63
  389.2 137.2 %reduce-scatter.5.cloned.1.call-start = ((), (), s32[]{:S(2)}) async-start(), calls=%async_computation.7 | async-start | bytes 4456448 | tf_op jit(solution)/shard_map/reduce_scatter | solution.py:100
  391.3 17.7 %copy-start.12 = (bf16[1024,128]{1,0:T(8,128)(2,1)}, bf16[1024,128]{1,0:T(8,128)(2,1)S(1)}, u32[]{:S(2)}) copy-start(bf16[1024,128]{1,0:T(8,128)(2,1)S(1)} %get-tuple-element.33) | copy-start | bytes 786436
  400.8 5.5 copy-start.5
  411.7 3.6 copy-start.1
  425.9 101.3 %copy-start.4 = (bf16[1024,128]{1,0:T(8,128)(2,1)S(1)}, bf16[1024,128]{1,0:T(8,128)(2,1)}, u32[]{:S(2)}) copy-start(bf16[1024,128]{1,0:T(8,128)(2,1)} %get-tuple-element.31) | copy-start | bytes 786436
  425.9 204.5 %all-gather.14.cloned.1.call-start = ((), (), s32[]{:S(2)}) async-start(), calls=%async_computation.8 | async-start | bytes 4456448 | tf_op jit(solution)/shard_map/all_gather | solution.py:103
  526.3 205.3 %all-gather.6.cloned.1.call-start = ((), (), s32[]{:S(2)}) async-start(), calls=%async_computation.2 | async-start | bytes 4456448 | tf_op jit(solution)/shard_map/all_gather | solution.py:94
  527.1 283.3 %all-gather.12.cloned.1.call-start = ((), (), s32[]{:S(2)}) async-start(), calls=%async_computation.6 | async-start | bytes 4456448 | tf_op jit(solution)/shard_map/all_gather | solution.py:95
  528.0 474.3 %all-reduce.7.cloned.1.call-start = ((), (), s32[]{:S(2)}) async-start(), calls=%async_computation.9 | async-start | bytes 4194304 | tf_op jit(solution)/shard_map/psum | solution.py:9
  634.8 692.4 %all-reduce.9.cloned.1.call-start = ((), (), s32[]{:S(2)}) async-start(), calls=%async_computation.10 | async-start | bytes 786432 | tf_op jit(solution)/shard_map/psum | solution.py:129
  634.8 106.1 %copy-start.6 = (bf16[1024,128]{1,0:T(8,128)(2,1)S(1)}, bf16[1024,128]{1,0:T(8,128)(2,1)}, u32[]{:S(2)}) copy-start(bf16[1024,128]{1,0:T(8,128)(2,1)} %get-tuple-element.32) | copy-start | bytes 786436
  634.8 106.0 %copy-start.13 = (bf16[1024,128]{1,0:T(8,128)(2,1)S(1)}, bf16[1024,128]{1,0:T(8,128)(2,1)}, u32[]{:S(2)}) copy-start(bf16[1024,128]{1,0:T(8,128)(2,1)} %copy-done.12) | copy-start | bytes 786436
  634.8 106.9 %copy-start.8 = (f32[1024,128]{1,0:T(8,128)S(1)}, f32[1024,128]{1,0:T(8,128)}, u32[]{:S(2)}) copy-start(f32[1024,128]{1,0:T(8,128)} %get-tuple-element.34) | copy-start | bytes 1572868
  740.2 3.7 copy-start.14
  1003.8 0.7 copy-start.9
  1003.8 0.8 copy-start.10
  1003.8 0.9 copy-start.11
  1003.8 1.9 copy-start.2
  1003.8 1.9 copy-start.7
  1003.9 1.9 copy-start.15
Sparse Core Ops, SparseCore 0:
  13.7 78.6 all-gather.7
  95.6 71.7 all-gather.9
  170.1 201.2 all-reduce.10
  389.3 11.4 reduce-scatter.2
  426.0 100.2 reduce-scatter.4
  528.1 102.3 all-gather.13
  632.4 99.2 all-gather.5
  735.2 75.0 all-gather.11
  813.2 189.0 all-reduce.6
  1081.9 245.1 all-reduce.8
where the time goes:
time: 1340 us
  waiting for transfers between devices  1140 us (85%)
  blocking collectives  77.9 us (6%)
  local copies, waits for them, and re-layouts  55.9 us (4%)
  matrix products  25 us (2%)
  other arithmetic  24 us (2%)
  between operations  14.5 us (1%)
    psum x2, waiting for transfers between devices, broadcast(): return lax.psum(jnp.where(mine, x, jnp.zeros_like(x)), axis)  373 us
    psum x1, waiting for transfers between devices, per_device(): lax.psum((local_in_proj, local_gate, local_w_out, local_ln_in, local_inne...  244 us
    all_gather x1, waiting for transfers between devices, per_device(): column_b = lax.all_gather(summed_b, 'row', axis=1, tiled=True)  102 us
    reduce_scatter x1, waiting for transfers between devices, per_device(): lax.psum_scatter(partial_b.astype(jnp.bfloat16), 'row', scatter_dimension...  100 us
    all_gather x1, waiting for transfers between devices, per_device(): right_cols = lax.all_gather(right, 'row', axis=0, tiled=True)  96.8 us
    all_gather x1, waiting for transfers between devices, per_device(): right_slab = lax.all_gather(right, 'col', axis=1, tiled=True)  77.9 us
    psum x1, blocking collectives, per_device(): lax.psum((local_in_proj, local_gate, local_w_out, local_ln_in, local_inne...  74.2 us
    all_gather x1, waiting for transfers between devices, per_device(): left_slab = lax.all_gather(left, 'col', axis=1, tiled=True)  70.3 us
  transfers between devices with their start and end apart: 10, of which 10 were waited for; matrix products, arithmetic and copies ran while one was open for 4% of the time, Pallas kernels for 0%

commit v1 on v0

v1 whole, which is shorter than its diff:
```python
import jax
import jax.numpy as jnp
from jax import lax
from jax.experimental import pallas as pl
from jax.experimental.pallas import tpu as pltpu
from jax.sharding import PartitionSpec as P

F32 = jnp.float32
BF16 = jnp.bfloat16
PLANE = ("row", "col")
T = 32
CH = 128
CELLS = T * T
SUB = 8
GROUPS = T // SUB


def call(kernel, out_shapes, *args, scratch=(), flops=2_000_000, smem=()):
    specs = [
        pl.BlockSpec(memory_space=pltpu.SMEM) if i in smem else pl.BlockSpec(memory_space=pltpu.VMEM)
        for i in range(len(args))
    ]
    moved = sum(a.size * a.dtype.itemsize for a in args)
    moved += sum(o.size * o.dtype.itemsize for o in out_shapes)
    return pl.pallas_call(
        kernel,
        out_shape=out_shapes,
        in_specs=specs,
        out_specs=[pl.BlockSpec(memory_space=pltpu.VMEM) for _ in out_shapes],
        scratch_shapes=list(scratch),
        compiler_params=pltpu.CompilerParams(vmem_limit_bytes=40 * 1024 * 1024),
        cost_estimate=pl.CostEstimate(flops=flops, bytes_accessed=moved, transcendentals=0),
    )(*args)


def struct(shape, dtype):
    return jax.ShapeDtypeStruct(shape, dtype)


def column(row):
    return jnp.transpose(jnp.broadcast_to(row, (CH, CH)))[:, :1]


def dot(a, b, ca, cb):
    return lax.dot_general(a, b, (((ca,), (cb,)), ((), ())), preferred_element_type=F32)


def channel_major(ref):
    chunks = []
    for s in range(SUB):
        block = jnp.concatenate([ref[SUB * g + s] for g in range(GROUPS)], axis=0)
        chunks.append(jnp.transpose(block.astype(F32)))
    return jnp.concatenate(chunks, axis=1)


def to_tiles(value, scratch, first, stride):
    for s in range(SUB):
        scratch[pl.ds(first + s, CH, stride=stride), :] = value[:, s * CH : (s + 1) * CH]


def from_tiles(scratch, first, stride):
    return jnp.concatenate(
        [scratch[pl.ds(first + s, CH, stride=stride), :] for s in range(SUB)], axis=1
    )


def norm(value):
    centre = value - jnp.mean(value, axis=0, keepdims=True)
    inverse = lax.rsqrt(jnp.mean(centre * centre, axis=0, keepdims=True) + 1e-05)
    return centre * inverse, inverse


def norm_back(grad, scaled, inverse, gain):
    tangent = grad * gain
    first = jnp.mean(tangent, axis=0, keepdims=True)
    second = jnp.mean(tangent * scaled, axis=0, keepdims=True)
    return inverse * (tangent - first - scaled * second)


def swap_groups(parts):
    a, b, c, d = parts
    axis = a.ndim - 1
    lane = lax.broadcasted_iota(jnp.int32, a.shape, axis)
    low = lane < 64
    even = (lane & 32) == 0
    a, c = jnp.where(low, a, pltpu.roll(c, 64, axis)), jnp.where(low, pltpu.roll(a, 64, axis), c)
    b, d = jnp.where(low, b, pltpu.roll(d, 64, axis)), jnp.where(low, pltpu.roll(b, 64, axis), d)
    a, b = jnp.where(even, a, pltpu.roll(b, 32, axis)), jnp.where(even, pltpu.roll(a, 96, axis), b)
    c, d = jnp.where(even, c, pltpu.roll(d, 32, axis)), jnp.where(even, pltpu.roll(c, 96, axis), d)
    return a, b, c, d


def to_matrix(tiles):
    blocks = tiles.shape[0]
    halves = []
    for half in range(2):
        parts = [tiles[:, half * 4 + part].astype(F32) for part in range(4)]
        rows = jnp.stack(swap_groups(parts), axis=1)
        halves.append(rows.reshape(blocks * T, CH))
    return jnp.concatenate(halves, axis=1)


def from_matrix(matrix):
    blocks = matrix.shape[0] // T
    parts = []
    for half in range(2):
        rows = matrix[:, half * CH : (half + 1) * CH].reshape(blocks, GROUPS, SUB, CH)
        parts += list(swap_groups([rows[:, g] for g in range(GROUPS)]))
    return jnp.stack(parts, axis=1)


def factors_kernel(pair, mask, gain, bias, in_proj, send, normed, zhat, zinv, coef, scratch):
    scaled, inverse = norm(channel_major(pair))
    zhat[...] = scaled
    zinv[...] = inverse
    value = (scaled * column(gain[...]) + column(bias[...])).astype(BF16)
    normed[...] = value
    proj = dot(in_proj[...], value, 0, 0)
    flags = mask[...].astype(F32)
    tile = jnp.concatenate([flags[SUB * g : SUB * (g + 1)] for g in range(GROUPS)], axis=1)
    m = jnp.concatenate([tile[s : s + 1] for s in range(SUB)], axis=1)
    for side in range(2):
        val = proj[2 * side * CH : (2 * side + 1) * CH]
        sig = jax.nn.sigmoid(proj[(2 * side + 1) * CH : (2 * side + 2) * CH])
        gated = sig * m
        factor = gated * val
        to_tiles(factor, scratch, side * SUB, 2 * SUB)
        coef[2 * side * CH : (2 * side + 1) * CH] = gated
        coef[(2 * side + 1) * CH : (2 * side + 2) * CH] = factor * (1.0 - sig)
    send[...] = scratch[...].reshape(CH, 2 * SUB, CH).astype(BF16)


def gate_kernel(grad_out, normed, w_gate, w_out, d_out_proj, d_xnorm, slope):
    upstream = channel_major(grad_out)
    gate = jax.nn.sigmoid(dot(w_gate[...], normed[...], 0, 0))
    moved = upstream * gate
    slope[...] = moved * (1.0 - gate)
    rounded = moved.astype(BF16)
    d_out_proj[...] = rounded
    d_xnorm[...] = dot(w_out[...], rounded, 1, 0)


def product_kernel(parity, own, other, send, left_own, right_own):
    rows = lax.bitwise_and(parity[0], 1)
    left_a = to_matrix(own[:, :, :, :SUB].reshape(16, 8, SUB, CH)).astype(BF16)
    left_b = to_matrix(other[:, :, :, :SUB].reshape(16, 8, SUB, CH)).astype(BF16)
    right_a = to_matrix(own[:, :, :, SUB:].reshape(16, 8, SUB, CH)).astype(BF16)
    left_own[...] = left_a
    right_own[...] = right_a
    mine = to_matrix(own[:, pl.ds(rows, 1), :, SUB:].reshape(8, 8, SUB, CH)).astype(BF16)
    theirs = to_matrix(other[:, pl.ds(rows, 1), :, SUB:].reshape(8, 8, SUB, CH)).astype(BF16)
    x = dot(left_a, mine, 1, 1) + dot(left_b, theirs, 1, 1)
    send[...] = from_matrix(x).reshape(CH, SUB, CH).astype(BF16)


def inner_kernel(recv, d_xnorm, gain, send, xhat, scratch):
    scratch[...] = recv[...].astype(F32).reshape(CELLS, CH)
    scaled, inverse = norm(from_tiles(scratch, 0, SUB))
    xhat[...] = scaled
    to_tiles(norm_back(d_xnorm[...], scaled, inverse, column(gain[...])), scratch, 0, SUB)
    send[...] = scratch[...].reshape(CH, SUB, CH).astype(BF16)


def sums(first, second, place):
    lane = lax.broadcasted_iota(jnp.int32, (CH, CH), 1)
    a = jnp.sum(first, axis=1, keepdims=True)
    b = jnp.sum(second, axis=1, keepdims=True)
    return jnp.where(lane == place, a, jnp.where(lane == place + 1, b, 0.0))


def output_kernel(
    xhat, d_xnorm, slope, d_out_proj, normed, gain, bias, w_out, w_gate, g_gate, g_out, inner, partial
):
    scaled = xhat[...]
    xnorm = (scaled * column(gain[...]) + column(bias[...])).astype(BF16)
    outp = dot(w_out[...], xnorm, 0, 0)
    d_gate_pre = (slope[...] * outp).astype(BF16)
    g_out[...] = dot(xnorm, d_out_proj[...], 1, 1)
    g_gate[...] = dot(normed[...], d_gate_pre, 1, 1)
    partial[...] = dot(w_gate[...], d_gate_pre, 1, 0)
    grad = d_xnorm[...]
    inner[...] = sums(grad * scaled, grad, 2)


def back_kernel(parity, own, other, left, right, send):
    flip = lax.bitwise_and(parity[0], 1) == 1
    mine = to_matrix(own[...].reshape(16, 8, SUB, CH)).astype(BF16)
    theirs = to_matrix(other[...].reshape(16, 8, SUB, CH)).astype(BF16)
    even = jnp.where(flip, theirs, mine)
    odd = jnp.where(flip, mine, theirs)
    pairs = right[...].reshape(8, 2, T, 2 * CH)
    da = dot(even, pairs[:, 0].reshape(8 * T, 2 * CH), 1, 0)
    da += dot(odd, pairs[:, 1].reshape(8 * T, 2 * CH), 1, 0)
    db_even = dot(even, left[...], 0, 0).reshape(8, T, 2 * CH)
    db_odd = dot(odd, left[...], 0, 0).reshape(8, T, 2 * CH)
    db = jnp.stack([db_even, db_odd], axis=1).reshape(16 * T, 2 * CH)
    both = jnp.concatenate([from_matrix(da), from_matrix(db)], axis=2)
    send[...] = both.reshape(CH, 2 * SUB, CH).astype(BF16)


def project_kernel(
    recv, coef, normed, zhat, partial, in_proj, g_gate, g_out, inner, send, d_normed, scratch, packed
):
    scratch[...] = recv[...].astype(F32).reshape(2 * CELLS, CH)
    da = from_tiles(scratch, 0, 2 * SUB)
    db = from_tiles(scratch, SUB, 2 * SUB)
    d_proj = jnp.concatenate(
        [
            (da * coef[0:CH]).astype(BF16),
            (da * coef[CH : 2 * CH]).astype(BF16),
            (db * coef[2 * CH : 3 * CH]).astype(BF16),
            (db * coef[3 * CH :]).astype(BF16),
        ],
        axis=0,
    )
    g_in = dot(normed[...], d_proj, 1, 1)
    grad = dot(in_proj[...], d_proj, 1, 0) + partial[...]
    d_normed[...] = grad
    for part in range(4):
        packed[pl.ds(part, CH, stride=SUB), :] = g_in[:, part * CH : (part + 1) * CH]
    packed[pl.ds(4, CH, stride=SUB), :] = g_gate[...]
    packed[pl.ds(5, CH, stride=SUB), :] = g_out[...]
    packed[pl.ds(6, CH, stride=SUB), :] = inner[...] + sums(grad * zhat[...], grad, 0)
    packed[pl.ds(7, CH, stride=SUB), :] = jnp.zeros((CH, CH), F32)
    send[...] = packed[...].reshape(CH, SUB, CH)


def pair_kernel(d_normed, zhat, zinv, gain, out):
    grad = norm_back(d_normed[...], zhat[...], zinv[...], column(gain[...]))
    for s in range(SUB):
        block = jnp.transpose(grad[:, s * CH : (s + 1) * CH]).astype(BF16)
        for g in range(GROUPS):
            out[SUB * g + s] = block[g * T : (g + 1) * T]


def total_kernel(recv, send):
    total = jnp.sum(recv[...], axis=0, keepdims=True)
    send[...] = jnp.broadcast_to(total, (CH, SUB, CH))


def unpack_kernel(own, other, g_in, g_gate, g_out, ln_in, inner, scratch):
    scratch[...] = (own[...] + other[...]).reshape(CELLS, CH)
    for part in range(4):
        g_in[:, part * CH : (part + 1) * CH] = scratch[pl.ds(part, CH, stride=SUB), :]
    g_gate[...] = scratch[pl.ds(4, CH, stride=SUB), :]
    g_out[...] = scratch[pl.ds(5, CH, stride=SUB), :]
    norms = jnp.transpose(scratch[pl.ds(6, CH, stride=SUB), :])
    ln_in[...] = norms[0:2]
    inner[...] = norms[2:4]


def swap_cores(value):
    return lax.ppermute(value, "depth", [(0, 1), (1, 0)])


def exchange(value):
    return lax.all_to_all(value, PLANE, 0, 0, tiled=True)


def per_device(
    pair,
    grad_out,
    pair_mask,
    ln_in_gain,
    ln_in_bias,
    in_proj,
    w_gate,
    inner_norm_gain,
    inner_norm_bias,
    w_out,
):
    parity = lax.axis_index("depth").astype(jnp.int32).reshape(1)
    in_gain = ln_in_gain.reshape(1, CH)
    in_bias = ln_in_bias.reshape(1, CH)
    x_gain = inner_norm_gain.reshape(1, CH)
    x_bias = inner_norm_bias.reshape(1, CH)
    one = struct((CH, SUB, CH), BF16)
    two = struct((CH, 2 * SUB, CH), BF16)
    wide = struct((CH, CELLS), F32)
    square = struct((CH, CH), F32)

    factors, normed, zhat, zinv, coef = call(
        factors_kernel,
        [two, struct((CH, CELLS), BF16), wide, struct((1, CELLS), F32), struct((4 * CH, CELLS), F32)],
        pair,
        pair_mask,
        in_gain,
        in_bias,
        in_proj,
        scratch=[pltpu.VMEM((2 * CELLS, CH), F32)],
    )
    factors = exchange(factors)
    d_out_proj, d_xnorm, slope = call(
        gate_kernel,
        [struct((CH, CELLS), BF16), wide, wide],
        grad_out,
        normed,
        w_gate,
        w_out,
        flops=500_000_000,
    )
    theirs = swap_cores(factors)
    x_send, left, right = call(
        product_kernel,
        [one, struct((16 * T, 2 * CH), BF16), struct((16 * T, 2 * CH), BF16)],
        parity,
        factors.reshape(8, 2, 8, 2 * SUB, CH),
        theirs.reshape(8, 2, 8, 2 * SUB, CH),
        smem=(0,),
    )
    x_recv = exchange(x_send)
    dx_send, xhat = call(
        inner_kernel,
        [one, wide],
        x_recv,
        d_xnorm,
        x_gain,
        scratch=[pltpu.VMEM((CELLS, CH), F32)],
    )
    dx = exchange(dx_send)
    g_gate, g_out, inner, partial = call(
        output_kernel,
        [square, square, square, wide],
        xhat,
        d_xnorm,
        slope,
        d_out_proj,
        normed,
        x_gain,
        x_bias,
        w_out,
        w_gate,
        flops=500_000_000,
    )
    (back_send,) = call(back_kernel, [two], parity, dx, swap_cores(dx), left, right, smem=(0,))
    back = exchange(back_send)
    weights, d_normed = call(
        project_kernel,
        [struct((CH, SUB, CH), F32), wide],
        back,
        coef,
        normed,
        zhat,
        partial,
        in_proj,
        g_gate,
        g_out,
        inner,
        scratch=[pltpu.VMEM((2 * CELLS, CH), F32), pltpu.VMEM((CELLS, CH), F32)],
    )
    weights = exchange(weights)
    (grad_pair,) = call(
        pair_kernel,
        [struct((T, T, CH), BF16)],
        d_normed,
        zhat,
        zinv,
        in_gain,
        flops=500_000_000,
    )
    (totals,) = call(total_kernel, [struct((CH, SUB, CH), F32)], weights)
    totals = exchange(totals)
    g_in, g_gate, g_out, ln_in, inner = call(
        unpack_kernel,
        [struct((CH, 4 * CH), F32), square, square, struct((2, CH), F32), struct((2, CH), F32)],
        totals,
        swap_cores(totals),
        scratch=[pltpu.VMEM((CELLS, CH), F32)],
    )
    return grad_pair, g_in, g_gate, g_out, ln_in, inner


def solution(mesh):
    cells = P("row", ("col", "depth"), None)
    return jax.shard_map(
        per_device,
        mesh=mesh,
        in_specs=(cells, cells, P("row", ("col", "depth"))) + (P(),) * 7,
        out_specs=(cells,) + (P(),) * 5,
        check_vma=False,
    )
```

time: 1340 us -> 183 us (0.14)
  waiting for transfers between devices: 1140 us -> 23.3 us
  local copies, waits for them, and re-layouts: 55.9 us -> 22.1 us
  matrix products: 25 us -> 0 us
  blocking collectives: 77.9 us -> 102 us
  other arithmetic: 24 us -> 0 us
  starting transfers between devices: 0.41 us -> 24 us
  between operations: 14.5 us -> 0.81 us
    psum x3 -> x0, waiting for transfers between devices: 617 us -> none  [the longest x2 373 us: broadcast(): return lax.psum(jnp.where(mine, x, jnp.zeros_like(x)), axis)]
    all_gather x5 -> x0, waiting for transfers between devices: 413 us -> none  [the longest x1 102 us: per_device(): column_b = lax.all_gather(summed_b, 'row', axis=1, tiled=True)]
    reduce_scatter x2 -> x0, waiting for transfers between devices: 110 us -> none  [the longest x1 100 us: per_device(): lax.psum_scatter(partial_b.astype(jnp.bfloat16), 'row', scatter_dimension...]
    all_to_all x0 -> x4, blocking collectives: none -> 102 us  [exchange(): return lax.all_to_all(value, PLANE, 0, 0, tiled=True)]
    psum x1 -> x0, blocking collectives: 74.2 us -> none  [per_device(): lax.psum((local_in_proj, local_gate, local_w_out, local_ln_in, local_inne...]
    dot_general x12 -> x0, matrix products: 25 us -> none  [the longest x1 6.21 us: per_device(): jnp.einsum('ijh,jkh->ikh', grad_rows, right_cols, preferred_element_type=...]
    all_gather x3 -> x0, local copies, waits for them, and re-layouts: 22.1 us -> none  [the longest x1 8.59 us: per_device(): lax.all_gather(input_gradient, ('col', 'depth'), axis=1, tiled=True)]
    all_to_all x0 -> x2, waiting for transfers between devices: none -> 20.2 us  [exchange(): return lax.all_to_all(value, PLANE, 0, 0, tiled=True)]
  transfers between devices with their start and end apart: 10 -> 5, of which waited for: 10 -> 5; matrix products, arithmetic and copies ran while one was open for 4% -> 0% of each run, Pallas kernels for 0% -> 1%
where the time goes in v1:
time: 183 us; the launch traced here: 182 us
  blocking collectives  102 us (56%)
  starting transfers between devices  24 us (13%)
  waiting for transfers between devices  23.3 us (13%)
  local copies, waits for them, and re-layouts  22.1 us (12%)
  Pallas kernels  9.66 us (5%)
    all_to_all x4, blocking collectives, exchange(): return lax.all_to_all(value, PLANE, 0, 0, tiled=True)  102 us
    unnamed x70, local copies, waits for them, and re-layouts  22.1 us
    all_to_all x2, waiting for transfers between devices, exchange(): return lax.all_to_all(value, PLANE, 0, 0, tiled=True)  20.2 us
    all_to_all x2, starting transfers between devices, exchange(): return lax.all_to_all(value, PLANE, 0, 0, tiled=True)  13.1 us
    ppermute x3, starting transfers between devices, swap_cores(): return lax.ppermute(value, 'depth', [(0, 1), (1, 0)])  10.9 us
    pallas_call x10, Pallas kernels, call(): pl.pallas_call(kernel, out_shape=out_shapes, in_specs=specs, out_specs=[p...  9.66 us
  transfers between devices with their start and end apart: 5, of which 5 were waited for; matrix products, arithmetic and copies ran while one was open for 0% of the time, Pallas kernels for 1%

profile of v1, /device:TPU:1, one launch (start us, length us, event | category | flops | bytes accessed | tf_op | source)
XLA Modules:
  0.0 181.6 jit_solution(4062718707458572698)
XLA Ops:
  0.6 0.9 copy-done
  1.5 0.9 copy-done.10
  2.5 0.7 copy-done.28
  3.2 0.7 copy-done.30
  3.9 0.7 copy-done.31
  4.5 1.0 shard_map.145
  5.5 0.8 copy-done.6
  6.3 33.7 %all_to_all.30 = bf16[128,16,128]{2,1,0:T(8,128)(2,1)S(1)} all-to-all(bf16[128,16,128]{2,1,0:T(8,128)(2,1)S(1)} %get-tuple-element.30), channel_id=1, replica_groups=mesh['row'=16,'col'=8,'depth'=2] {'row','col'}, dimensions={0} | all-to-all | bytes 1048576 | tf_op jit(solution)/shard_map/all_to_all | solution.py:257
  40.0 3.0 %collective-permute-start = (bf16[128,16,128]{2,1,0:T(8,128)(2,1)S(1)}, bf16[128,16,128]{2,1,0:T(8,128)(2,1)S(1)}, u32[]{:S(2)}, u32[]{:S(2)}) collective-permute-start(bf16[128,16,128]{2,1,0:T(8,128)(2,1)S(1)} %all_to_all.30), channel_id=1, source_target_pairs={{0,1},{1,0},{2,3},{3,2},{4,5},{5,4},{6,7},{7,6},{8,9},{9,8},{10,11... | collective-permute-start | bytes 1572872 | tf_op jit(solution)/shard_map/ppermute | solution.py:253
  43.0 1.5 collective-permute-done
  44.5 1.7 shard_map.146
  46.2 0.7 copy-done.11
  46.9 0.7 copy-done.12
  47.6 0.7 copy-done.14
  48.4 6.7 %all-to-all-start.1 = ((bf16[128,8,128]{2,1,0:T(8,128)(2,1)}), bf16[128,8,128]{2,1,0:T(8,128)(2,1)S(1)}, u32[]{:S(2)}, u32[]{:S(2)}) async-start(bf16[128,8,128]{2,1,0:T(8,128)(2,1)} %copy-done.11), calls=%async_computation.1 | async-start | bytes 524288 | tf_op jit(solution)/shard_map/all_to_all | solution.py:257
  55.1 0.9 copy-done.34
  56.6 0.8 copy-done.2
  57.4 0.7 copy-done.16
  58.1 10.1 %all-to-all-done.1.recv = bf16[128,8,128]{2,1,0:T(8,128)(2,1)S(1)} async-done(((bf16[128,8,128]{2,1,0:T(8,128)(2,1)}), bf16[128,8,128]{2,1,0:T(8,128)(2,1)S(1)}, u32[]{:S(2)}, u32[]{:S(2)}) %all-to-all-start.1) | async-done | bytes 262176 | tf_op jit(solution)/shard_map/all_to_all | solution.py:257
  68.2 0.5 shard_map.148
  68.7 18.9 %all_to_all.31.own = bf16[128,8,128]{2,1,0:T(8,128)(2,1)S(1)} all-to-all(bf16[128,8,128]{2,1,0:T(8,128)(2,1)S(1)} %get-tuple-element.34), channel_id=1, replica_groups=mesh['row'=16,'col'=8,'depth'=2] {'row','col'}, dimensions={0} | all-to-all | bytes 524288 | tf_op jit(solution)/shard_map/all_to_all | solution.py:257
  87.6 3.6 %collective-permute-start.1 = (bf16[128,8,128]{2,1,0:T(8,128)(2,1)S(1)}, bf16[128,8,128]{2,1,0:T(8,128)(2,1)S(1)}, u32[]{:S(2)}, u32[]{:S(2)}) collective-permute-start(bf16[128,8,128]{2,1,0:T(8,128)(2,1)S(1)} %all_to_all.31.own), channel_id=1, source_target_pairs={{0,1},{1,0},{2,3},{3,2},{4,5},{5,4},{6,7},{7,6},{8,9},{9,8},{10,11... | collective-permute-start | bytes 786440 | tf_op jit(solution)/shard_map/ppermute | solution.py:253
  91.2 1.2 collective-permute-done.1.other
  92.3 0.9 copy-done.15
  93.3 2.2 %shard_map.149 = bf16[128,16,128]{2,1,0:T(8,128)(2,1)} custom-call(s32[1]{0:T(128)} %bitcast.parity, bf16[128,8,128]{2,1,0:T(8,128)(2,1)S(1)} %all_to_all.31.own, bf16[128,8,128]{2,1,0:T(8,128)(2,1)S(1)} %collective-permute-done.1.other, bf16[512,256]{1,0:T(8,128)(2,1)S(1)} %copy-done.13, bf16[512,256]{1,0:T(8,128)(2,1)S(1)} %copy-done.15), custom_call_target="tpu_custom_call" | custom-call | flops 2000000 | bytes 1572868 | tf_op jit(solution)/shard_map/pallas_call | solution.py:25
  95.5 6.3 %all-to-all-start.3 = ((bf16[128,16,128]{2,1,0:T(8,128)(2,1)}), bf16[128,16,128]{2,1,0:T(8,128)(2,1)S(1)}, u32[]{:S(2)}, u32[]{:S(2)}) async-start(bf16[128,16,128]{2,1,0:T(8,128)(2,1)} %shard_map.149), calls=%async_computation.3 | async-start | bytes 1048576 | tf_op jit(solution)/shard_map/all_to_all | solution.py:257
  101.9 1.0 copy-done.3
  102.9 1.0 copy-done.5
  103.9 0.9 copy-done.17
  104.9 0.8 copy-done.25
  105.6 0.8 copy-done.27
  106.4 0.7 shard_map.150
  107.1 0.8 copy-done.8
  107.9 0.6 copy-done.18
  108.5 0.6 copy-done.20
  109.1 0.6 copy-done.22
  109.8 10.1 %all-to-all-done.3.recv = bf16[128,16,128]{2,1,0:T(8,128)(2,1)S(1)} async-done(((bf16[128,16,128]{2,1,0:T(8,128)(2,1)}), bf16[128,16,128]{2,1,0:T(8,128)(2,1)S(1)}, u32[]{:S(2)}, u32[]{:S(2)}) %all-to-all-start.3) | async-done | bytes 524320 | tf_op jit(solution)/shard_map/all_to_all | solution.py:257
  119.9 1.0 copy-done.7
  120.9 1.0 copy-done.9
  122.0 0.8 copy-done.19
  122.8 0.8 copy-done.21
  123.6 0.8 copy-done.23
  124.5 1.0 shard_map.151
  125.5 24.5 %all_to_all.32.recv = f32[128,8,128]{2,1,0:T(8,128)S(1)} all-to-all(f32[128,8,128]{2,1,0:T(8,128)S(1)} %get-tuple-element.48), channel_id=1, replica_groups=mesh['row'=16,'col'=8,'depth'=2] {'row','col'}, dimensions={0} | all-to-all | bytes 1048576 | tf_op jit(solution)/shard_map/all_to_all | solution.py:257
  150.2 24.6 %all_to_all.33.own = f32[128,8,128]{2,1,0:T(8,128)S(1)} all-to-all(f32[128,8,128]{2,1,0:T(8,128)S(1)} %shard_map.153), channel_id=1, replica_groups=mesh['row'=16,'col'=8,'depth'=2] {'row','col'}, dimensions={0} | all-to-all | bytes 1048576 | tf_op jit(solution)/shard_map/all_to_all | solution.py:257
  174.8 4.3 %collective-permute-start.2 = (f32[128,8,128]{2,1,0:T(8,128)S(1)}, f32[128,8,128]{2,1,0:T(8,128)S(1)}, u32[]{:S(2)}, u32[]{:S(2)}) collective-permute-start(f32[128,8,128]{2,1,0:T(8,128)S(1)} %all_to_all.33.own), channel_id=1, source_target_pairs={{0,1},{1,0},{2,3},{3,2},{4,5},{5,4},{6,7},{7,6},{8,9},{9,8},{10,11... | collective-permute-start | bytes 1572872 | tf_op jit(solution)/shard_map/ppermute | solution.py:253
  179.2 1.1 shard_map.152
  180.7 0.9 shard_map.154
  (46 shorter events, 1.2 us)
Async XLA Ops:
  0.6 0.9 copy-start
  1.5 0.9 copy-start.10
  2.5 0.7 copy-start.28
  3.2 0.7 copy-start.30
  3.9 0.7 copy-start.31
  4.5 50.6 %copy-start.24 = (bf16[128,128]{1,0:T(8,128)(2,1)S(1)}, bf16[128,128]{1,0:T(8,128)(2,1)}, u32[]{:S(2)}) copy-start(bf16[128,128]{1,0:T(8,128)(2,1)} %w_gate.3) | copy-start | bytes 98308
  4.5 50.6 %copy-start.26 = (bf16[128,128]{1,0:T(8,128)(2,1)S(1)}, bf16[128,128]{1,0:T(8,128)(2,1)}, u32[]{:S(2)}) copy-start(bf16[128,128]{1,0:T(8,128)(2,1)} %w_out.3) | copy-start | bytes 98308
  5.5 0.8 copy-start.6
  6.3 61.9 %copy-start.29 = (f32[128]{0:T(128)S(1)}, f32[128]{0:T(128)}, u32[]{:S(2)}) copy-start(f32[128]{0:T(128)} %param.17) | copy-start | bytes 1540
  40.0 4.5 %collective-permute-start = (bf16[128,16,128]{2,1,0:T(8,128)(2,1)S(1)}, bf16[128,16,128]{2,1,0:T(8,128)(2,1)S(1)}, u32[]{:S(2)}, u32[]{:S(2)}) collective-permute-start(bf16[128,16,128]{2,1,0:T(8,128)(2,1)S(1)} %all_to_all.30), channel_id=1, source_target_pairs={{0,1},{1,0},{2,3},{3,2},{4,5},{5,4},{6,7},{7,6},{8,9},{9,8},{10,11... | collective-permute-start | bytes 1572872 | tf_op jit(solution)/shard_map/ppermute | solution.py:253
  46.2 0.7 copy-start.11
  46.9 0.7 copy-start.12
  47.6 0.7 copy-start.14
  48.4 44.0 %copy-start.13 = (bf16[512,256]{1,0:T(8,128)(2,1)S(1)}, bf16[512,256]{1,0:T(8,128)(2,1)}, u32[]{:S(2)}) copy-start(bf16[512,256]{1,0:T(8,128)(2,1)} %copy-done.12) | copy-start | bytes 786436
  48.4 19.8 %all-to-all-start.1 = ((bf16[128,8,128]{2,1,0:T(8,128)(2,1)}), bf16[128,8,128]{2,1,0:T(8,128)(2,1)S(1)}, u32[]{:S(2)}, u32[]{:S(2)}) async-start(bf16[128,8,128]{2,1,0:T(8,128)(2,1)} %copy-done.11), calls=%async_computation.1 | async-start | bytes 524288 | tf_op jit(solution)/shard_map/all_to_all | solution.py:257
  55.1 1.0 copy-start.34
  56.6 0.8 copy-start.2
  57.4 0.7 copy-start.16
  58.1 43.7 %copy-start.33 = (f32[128]{0:T(128)S(1)}, f32[128]{0:T(128)}, u32[]{:S(2)}) copy-start(f32[128]{0:T(128)} %param.18) | copy-start | bytes 1540
  68.7 23.6 %copy-start.4 = (f32[128,1024]{1,0:T(8,128)}, f32[128,1024]{1,0:T(8,128)S(1)}, u32[]{:S(2)}) copy-start(f32[128,1024]{1,0:T(8,128)S(1)} %get-tuple-element.39.xhat) | copy-start | bytes 1572868
  87.6 4.8 %collective-permute-start.1 = (bf16[128,8,128]{2,1,0:T(8,128)(2,1)S(1)}, bf16[128,8,128]{2,1,0:T(8,128)(2,1)S(1)}, u32[]{:S(2)}, u32[]{:S(2)}) collective-permute-start(bf16[128,8,128]{2,1,0:T(8,128)(2,1)S(1)} %all_to_all.31.own), channel_id=1, source_target_pairs={{0,1},{1,0},{2,3},{3,2},{4,5},{5,4},{6,7},{7,6},{8,9},{9,8},{10,11... | collective-permute-start | bytes 786440 | tf_op jit(solution)/shard_map/ppermute | solution.py:253
  92.3 1.0 copy-start.15
  93.3 26.6 %copy-start.1 = (bf16[128,512]{1,0:T(8,128)(2,1)S(1)}, bf16[128,512]{1,0:T(8,128)(2,1)}, u32[]{:S(2)}) copy-start(bf16[128,512]{1,0:T(8,128)(2,1)} %in_proj.3) | copy-start | bytes 393220
  95.5 24.4 %all-to-all-start.3 = ((bf16[128,16,128]{2,1,0:T(8,128)(2,1)}), bf16[128,16,128]{2,1,0:T(8,128)(2,1)S(1)}, u32[]{:S(2)}, u32[]{:S(2)}) async-start(bf16[128,16,128]{2,1,0:T(8,128)(2,1)} %shard_map.149), calls=%async_computation.3 | async-start | bytes 1048576 | tf_op jit(solution)/shard_map/all_to_all | solution.py:257
  101.8 1.0 copy-start.3
  102.9 1.0 copy-start.5
  103.9 0.9 copy-start.17
  104.9 0.8 copy-start.25
  105.6 0.8 copy-start.27
  107.1 0.8 copy-start.8
  107.9 0.6 copy-start.18
  108.5 0.6 copy-start.20
  109.1 0.6 copy-start.22
  119.9 1.0 copy-start.7
  120.9 1.0 copy-start.9
  122.0 0.8 copy-start.19
  122.8 0.8 copy-start.21
  123.6 0.8 copy-start.23
  125.5 53.7 %copy-start.32 = (f32[128]{0:T(128)S(1)}, f32[128]{0:T(128)}, u32[]{:S(2)}) copy-start(f32[128]{0:T(128)} %param.13) | copy-start | bytes 1540
  174.8 5.9 %collective-permute-start.2 = (f32[128,8,128]{2,1,0:T(8,128)S(1)}, f32[128,8,128]{2,1,0:T(8,128)S(1)}, u32[]{:S(2)}, u32[]{:S(2)}) collective-permute-start(f32[128,8,128]{2,1,0:T(8,128)S(1)} %all_to_all.33.own), channel_id=1, source_target_pairs={{0,1},{1,0},{2,3},{3,2},{4,5},{5,4},{6,7},{7,6},{8,9},{9,8},{10,11... | collective-permute-start | bytes 1572872 | tf_op jit(solution)/shard_map/ppermute | solution.py:253

commit v2 on v1

v2 whole, which is shorter than its diff:
```python
import jax
import jax.numpy as jnp
from jax import lax
from jax.experimental import pallas as pl
from jax.experimental.pallas import tpu as pltpu
from jax.sharding import PartitionSpec as P

F32 = jnp.float32
BF16 = jnp.bfloat16
PLANE = ("row", "col")
T = 32
CH = 128
CELLS = T * T
SUB = 8
GROUPS = T // SUB
HALF = SUB // 2


def call(kernel, outs, *args, scratch=(), flops=2_000_000, spaces=None, fetched=()):
    spaces = spaces or {}
    fetched = tuple(fetched)
    count = len(args)
    specs = [
        pl.BlockSpec(memory_space=pltpu.HBM if i in fetched else spaces.get(i, pltpu.VMEM))
        for i in range(count)
    ]
    moved = sum(a.size * a.dtype.itemsize for a in args)
    moved += sum(o.size * o.dtype.itemsize for o in outs)
    args = [
        pltpu.with_memory_space_constraint(a, pltpu.HBM) if i in fetched else a
        for i, a in enumerate(args)
    ]

    def body(*refs):
        if not fetched:
            return kernel(*refs)
        local = refs[len(refs) - 1 - len(fetched) : -1]
        refs, sems = refs[: len(refs) - 1 - len(fetched)], refs[-1]
        inputs = list(refs[:count])
        copies = [
            pltpu.make_async_copy(inputs[i], target, sems.at[place])
            for place, (i, target) in enumerate(zip(fetched, local))
        ]
        for copy in copies:
            copy.start()
        for copy in copies:
            copy.wait()
        for i, target in zip(fetched, local):
            inputs[i] = target
        return kernel(*inputs, *refs[count:])

    extra = [pltpu.VMEM(args[i].shape, args[i].dtype) for i in fetched]
    if fetched:
        extra.append(pltpu.SemaphoreType.DMA((len(fetched),)))
    return pl.pallas_call(
        body,
        out_shape=outs,
        in_specs=specs,
        out_specs=[pl.BlockSpec(memory_space=pltpu.VMEM) for _ in outs],
        scratch_shapes=list(scratch) + extra,
        compiler_params=pltpu.CompilerParams(vmem_limit_bytes=32 * 1024 * 1024),
        cost_estimate=pl.CostEstimate(flops=flops, bytes_accessed=moved, transcendentals=0),
    )(*args)


def struct(shape, dtype):
    return jax.ShapeDtypeStruct(shape, dtype)


def column(row):
    return jnp.transpose(jnp.broadcast_to(row, (CH, CH)))[:, :1]


def dot(a, b, ca, cb):
    return lax.dot_general(a, b, (((ca,), (cb,)), ((), ())), preferred_element_type=F32)


def channel_major(ref):
    chunks = []
    for s in range(SUB):
        block = jnp.concatenate([ref[SUB * g + s] for g in range(GROUPS)], axis=0)
        chunks.append(jnp.transpose(block.astype(F32)))
    return jnp.concatenate(chunks, axis=1)


def to_tiles(value, scratch, first, stride):
    for s in range(SUB):
        scratch[pl.ds(first + s, CH, stride=stride), :] = value[:, s * CH : (s + 1) * CH]


def from_tiles(scratch, first, stride):
    return jnp.concatenate(
        [scratch[pl.ds(first + s, CH, stride=stride), :] for s in range(SUB)], axis=1
    )


def norm(value):
    centre = value - jnp.mean(value, axis=0, keepdims=True)
    inverse = lax.rsqrt(jnp.mean(centre * centre, axis=0, keepdims=True) + 1e-05)
    return centre * inverse, inverse


def norm_back(tangent, scaled, inverse):
    first = jnp.mean(tangent, axis=0, keepdims=True)
    second = jnp.mean(tangent * scaled, axis=0, keepdims=True)
    return inverse * (tangent - first - scaled * second)


def swap_groups(parts):
    a, b, c, d = parts
    axis = a.ndim - 1
    lane = lax.broadcasted_iota(jnp.int32, a.shape, axis)
    low = lane < 64
    even = (lane & 32) == 0
    a, c = jnp.where(low, a, pltpu.roll(c, 64, axis)), jnp.where(low, pltpu.roll(a, 64, axis), c)
    b, d = jnp.where(low, b, pltpu.roll(d, 64, axis)), jnp.where(low, pltpu.roll(b, 64, axis), d)
    a, b = jnp.where(even, a, pltpu.roll(b, 32, axis)), jnp.where(even, pltpu.roll(a, 96, axis), b)
    c, d = jnp.where(even, c, pltpu.roll(d, 32, axis)), jnp.where(even, pltpu.roll(c, 96, axis), d)
    return a, b, c, d


def to_matrix(tiles):
    blocks = tiles.shape[0]
    halves = []
    for half in range(2):
        parts = [tiles[:, half * 4 + part].astype(F32) for part in range(4)]
        rows = jnp.stack(swap_groups(parts), axis=1)
        halves.append(rows.reshape(blocks * T, CH))
    return jnp.concatenate(halves, axis=1)


def from_matrix(matrix):
    blocks = matrix.shape[0] // T
    parts = []
    for half in range(2):
        rows = matrix[:, half * CH : (half + 1) * CH].reshape(blocks, GROUPS, SUB, CH)
        parts += list(swap_groups([rows[:, g] for g in range(GROUPS)]))
    return jnp.stack(parts, axis=1)


def normalise(pair, gain, bias):
    scaled, inverse = norm(channel_major(pair))
    return scaled, inverse, (scaled * column(gain[...]) + column(bias[...])).astype(BF16)


def factors_of(normed, mask, in_proj):
    proj = dot(in_proj[...], normed, 0, 0)
    flags = mask[...].astype(F32)
    tile = jnp.concatenate([flags[SUB * g : SUB * (g + 1)] for g in range(GROUPS)], axis=1)
    m = jnp.concatenate([tile[s : s + 1] for s in range(SUB)], axis=1)
    sides = []
    for side in range(2):
        val = proj[2 * side * CH : (2 * side + 1) * CH]
        sig = jax.nn.sigmoid(proj[(2 * side + 1) * CH : (2 * side + 2) * CH])
        gated = sig * m
        sides.append((gated, gated * val, 1.0 - sig))
    return sides


def factors_kernel(pair, mask, gain, bias, in_proj, send, scratch):
    normed = normalise(pair, gain, bias)[2]
    for side, (_, factor, _) in enumerate(factors_of(normed, mask, in_proj)):
        to_tiles(factor, scratch, side * SUB, 2 * SUB)
    send[...] = scratch[...].reshape(CH, 2 * SUB, CH).astype(BF16)


def gated_grad(grad_out, normed, w_gate):
    gate = jax.nn.sigmoid(dot(w_gate[...], normed, 0, 0))
    moved = channel_major(grad_out) * gate
    return moved.astype(BF16), moved * (1.0 - gate)


def tangent_kernel(pair, grad_out, gain, bias, x_gain, w_gate, w_out, tangent):
    normed = normalise(pair, gain, bias)[2]
    d_out_proj, _ = gated_grad(grad_out, normed, w_gate)
    tangent[...] = dot(w_out[...], d_out_proj, 1, 0) * column(x_gain[...])


def product_rows(tiles, mine):
    return to_matrix(tiles[:, pl.ds(mine, 1), :, SUB:].reshape(8, 8, SUB, CH)).astype(BF16)


def product_own_kernel(parity, own, left_out, right_out, partial):
    mine = lax.bitwise_and(parity[0], 1)
    left = to_matrix(own[:, :, :, :SUB].reshape(16, 8, SUB, CH)).astype(BF16)
    left_out[...] = left
    right_out[...] = to_matrix(own[:, :, :, SUB:].reshape(16, 8, SUB, CH)).astype(BF16)
    partial[...] = dot(left, product_rows(own, mine), 1, 1)


def product_kernel(parity, other, partial, send):
    mine = lax.bitwise_and(parity[0], 1)
    left = to_matrix(other[:, :, :, :SUB].reshape(16, 8, SUB, CH)).astype(BF16)
    x = partial[...] + dot(left, product_rows(other, mine), 1, 1)
    send[...] = from_matrix(x).reshape(CH, SUB, CH).astype(BF16)


def inner_kernel(recv, tangent, send, scratch):
    scratch[...] = recv[...].astype(F32).reshape(CELLS, CH)
    scaled, inverse = norm(from_tiles(scratch, 0, SUB))
    to_tiles(norm_back(tangent[...], scaled, inverse), scratch, 0, SUB)
    send[...] = scratch[...].reshape(CH, SUB, CH).astype(BF16)


def sums(first, second, place):
    lane = lax.broadcasted_iota(jnp.int32, (CH, CH), 1)
    a = jnp.sum(first, axis=1, keepdims=True)
    b = jnp.sum(second, axis=1, keepdims=True)
    return jnp.where(lane == place, a, jnp.where(lane == place + 1, b, 0.0))


def output_kernel(
    pair,
    grad_out,
    mask,
    gain,
    bias,
    x_gain,
    x_bias,
    in_proj,
    w_gate,
    w_out,
    x_recv,
    after,
    coef,
    normed_out,
    zhat,
    partial,
    early,
    scratch,
):
    scaled, _, normed = normalise(pair, gain, bias)
    zhat[...] = scaled.astype(BF16)
    normed_out[...] = normed
    for side, (gated, factor, rest) in enumerate(factors_of(normed, mask, in_proj)):
        coef[2 * side * CH : (2 * side + 1) * CH] = gated.astype(BF16)
        coef[(2 * side + 1) * CH : (2 * side + 2) * CH] = (factor * rest).astype(BF16)
    d_out_proj, slope = gated_grad(grad_out, normed, w_gate)
    d_xnorm = dot(w_out[...], d_out_proj, 1, 0)
    scratch[...] = x_recv[...].astype(F32).reshape(CELLS, CH)
    xhat, _ = norm(from_tiles(scratch, 0, SUB))
    xnorm = (xhat * column(x_gain[...]) + column(x_bias[...])).astype(BF16)
    d_gate_pre = (slope * dot(w_out[...], xnorm, 0, 0)).astype(BF16)
    early[0:CH] = dot(normed, d_gate_pre, 1, 1)
    early[CH : 2 * CH] = dot(xnorm, d_out_proj, 1, 1)
    early[2 * CH :] = sums(d_xnorm * xhat, d_xnorm, 2)
    partial[...] = dot(w_gate[...], d_gate_pre, 1, 0)


def back_kernel(dx, left, right, send):
    pairs = right[...].reshape(8, 2, T, 2 * CH)
    da = None
    dbs = []
    for half in range(2):
        grad = to_matrix(dx[half].reshape(16, 8, SUB, CH)).astype(BF16)
        term = dot(grad, pairs[:, half].reshape(8 * T, 2 * CH), 1, 0)
        da = term if da is None else da + term
        dbs.append(dot(grad, left[...], 0, 0).reshape(8, T, 2 * CH))
    db = jnp.stack(dbs, axis=1).reshape(16 * T, 2 * CH)
    send[:, :SUB] = from_matrix(da).reshape(CH, SUB, CH).astype(BF16)
    send[:, SUB:] = from_matrix(db).reshape(CH, SUB, CH).astype(BF16)


def project_kernel(recv, in_proj, coef, normed, zhat, partial, early, send, d_normed, scratch, packed):
    scratch[...] = recv[...].astype(F32).reshape(2 * CELLS, CH)
    da = from_tiles(scratch, 0, 2 * SUB)
    db = from_tiles(scratch, SUB, 2 * SUB)
    d_proj = jnp.concatenate(
        [
            (grad * coef[part * CH : (part + 1) * CH].astype(F32)).astype(BF16)
            for part, grad in enumerate((da, da, db, db))
        ],
        axis=0,
    )
    g_in = dot(normed[...], d_proj, 1, 1)
    grad = dot(in_proj[...], d_proj, 1, 0) + partial[...]
    d_normed[...] = grad
    for part in range(4):
        packed[pl.ds(part, CH, stride=SUB), :] = g_in[:, part * CH : (part + 1) * CH]
    packed[pl.ds(4, CH, stride=SUB), :] = early[0:CH]
    packed[pl.ds(5, CH, stride=SUB), :] = early[CH : 2 * CH]
    packed[pl.ds(6, CH, stride=SUB), :] = early[2 * CH :] + sums(
        grad * zhat[...].astype(F32), grad, 0
    )
    packed[pl.ds(7, CH, stride=SUB), :] = jnp.zeros((CH, CH), F32)
    send[...] = packed[...].reshape(CH, SUB, CH).astype(BF16)


def pair_kernel(d_normed, pair, gain, out):
    scaled, inverse = norm(channel_major(pair))
    grad = norm_back(d_normed[...] * column(gain[...]), scaled, inverse)
    for s in range(SUB):
        block = jnp.transpose(grad[:, s * CH : (s + 1) * CH]).astype(BF16)
        for g in range(GROUPS):
            out[SUB * g + s] = block[g * T : (g + 1) * T]


def total_kernel(recv, after, send):
    total = jnp.sum(recv[...].astype(F32), axis=0, keepdims=True)
    total = total + pltpu.roll(total, HALF, 1)
    send[...] = jnp.broadcast_to(total, (CH // 2, SUB, CH)).astype(BF16)


def unpack_kernel(totals, g_in, g_gate, g_out, ln_in, inner, scratch):
    scratch[...] = totals[...].astype(F32).reshape(CELLS, CH)
    for part in range(HALF):
        g_in[:, part * CH : (part + 1) * CH] = scratch[pl.ds(part, CH, stride=HALF), :]
    g_gate[...] = scratch[pl.ds(CELLS // 2, CH, stride=HALF), :]
    g_out[...] = scratch[pl.ds(CELLS // 2 + 1, CH, stride=HALF), :]
    norms = jnp.transpose(scratch[pl.ds(CELLS // 2 + 2, CH, stride=HALF), :])
    ln_in[...] = norms[0:2]
    inner[...] = norms[2:4]


def swap_cores(value):
    return lax.ppermute(value, "depth", [(0, 1), (1, 0)])


def both_cores(value):
    return lax.all_gather(value, "depth", axis=0, tiled=False)


def exchange(value, axes=PLANE):
    return lax.all_to_all(value, axes, 0, 0, tiled=True)


def per_device(
    pair,
    grad_out,
    pair_mask,
    ln_in_gain,
    ln_in_bias,
    in_proj,
    w_gate,
    inner_norm_gain,
    inner_norm_bias,
    w_out,
):
    parity = lax.axis_index("depth").astype(jnp.int32).reshape(1)
    in_gain = ln_in_gain.reshape(1, CH)
    in_bias = ln_in_bias.reshape(1, CH)
    x_gain = inner_norm_gain.reshape(1, CH)
    x_bias = inner_norm_bias.reshape(1, CH)
    one = struct((CH, SUB, CH), BF16)
    two = struct((CH, 2 * SUB, CH), BF16)
    square = struct((CH, CH), F32)
    matrix = struct((16 * T, 2 * CH), BF16)
    wide = struct((CH, CELLS), F32)
    narrow = struct((CH, CELLS), BF16)
    tiles = pltpu.VMEM((CELLS, CH), F32)
    pairs_of_tiles = pltpu.VMEM((2 * CELLS, CH), F32)

    (factors,) = call(
        factors_kernel,
        [two],
        pair,
        pair_mask,
        in_gain,
        in_bias,
        in_proj,
        scratch=[pairs_of_tiles],
        fetched=range(5),
    )
    factors = exchange(factors).reshape(8, 2, 8, 2 * SUB, CH)
    left, right, partial = call(
        product_own_kernel,
        [matrix, matrix, struct((16 * T, 2 * CH), F32)],
        parity,
        factors,
        spaces={0: pltpu.SMEM},
    )
    (x_send,) = call(
        product_kernel, [one], parity, swap_cores(factors), partial, spaces={0: pltpu.SMEM}
    )
    x_recv = exchange(x_send)
    (tangent,) = call(
        tangent_kernel,
        [wide],
        pair,
        grad_out,
        in_gain,
        in_bias,
        x_gain,
        w_gate,
        w_out,
        flops=500_000_000,
        fetched=range(7),
    )
    (dx_send,) = call(inner_kernel, [one], x_recv, tangent, scratch=[tiles])
    (back_send,) = call(back_kernel, [two], both_cores(exchange(dx_send)), left, right)
    back = exchange(back_send)
    coef, normed, zhat, partial, early = call(
        output_kernel,
        [struct((4 * CH, CELLS), BF16), narrow, narrow, wide, struct((3 * CH, CH), F32)],
        pair,
        grad_out,
        pair_mask,
        in_gain,
        in_bias,
        x_gain,
        x_bias,
        in_proj,
        w_gate,
        w_out,
        x_recv,
        back_send,
        scratch=[tiles],
        flops=500_000_000,
        fetched=range(10),
        spaces={11: pl.ANY},
    )
    weights, d_normed = call(
        project_kernel,
        [one, wide],
        back,
        in_proj,
        coef,
        normed,
        zhat,
        partial,
        early,
        scratch=[pairs_of_tiles, tiles],
    )
    weights = exchange(weights.reshape(2 * CH, HALF, CH), ("row", "col", "depth"))
    (grad_pair,) = call(
        pair_kernel,
        [struct((T, T, CH), BF16)],
        d_normed,
        pair,
        in_gain,
        flops=500_000_000,
        fetched=(1, 2),
    )
    (totals,) = call(
        total_kernel,
        [struct((CH // 2, SUB, CH), BF16)],
        weights.reshape(CH, SUB, CH),
        grad_pair,
        spaces={1: pl.ANY},
    )
    totals = exchange(totals.reshape(CH, HALF, CH))
    g_in, g_gate, g_out, ln_in, inner = call(
        unpack_kernel,
        [struct((CH, 4 * CH), F32), square, square, struct((2, CH), F32), struct((2, CH), F32)],
        both_cores(totals.reshape(CH // 2, SUB, CH)),
        scratch=[tiles],
    )
    return grad_pair, g_in, g_gate, g_out, ln_in, inner


def solution(mesh):
    cells = P("row", ("col", "depth"), None)
    return jax.shard_map(
        per_device,
        mesh=mesh,
        in_specs=(cells, cells, P("row", ("col", "depth"))) + (P(),) * 7,
        out_specs=(cells,) + (P(),) * 5,
        check_vma=False,
    )
```

time: 183 us -> 162 us (0.89)
  blocking collectives: 102 us -> 77.9 us
  local copies, waits for them, and re-layouts: 22.1 us -> 1.75 us
  waiting for transfers between devices: 23.3 us -> 40.9 us
  Pallas kernels: 9.66 us -> 16.7 us
    all_to_all x4 -> x3, blocking collectives: 102 us -> 68.9 us  [exchange(): return lax.all_to_all(value, axes, 0, 0, tiled=True)]
    unnamed x70 -> x8, local copies, waits for them, and re-layouts: 22.1 us -> 1.75 us
    all_to_all x2 -> x3, waiting for transfers between devices: 20.2 us -> 40.2 us  [exchange(): return lax.all_to_all(value, axes, 0, 0, tiled=True)]
    all_gather x0 -> x2, blocking collectives: none -> 9 us  [both_cores(): return lax.all_gather(value, 'depth', axis=0, tiled=False)]
    ppermute x3 -> x1, starting transfers between devices: 10.9 us -> 2.98 us  [swap_cores(): return lax.ppermute(value, 'depth', [(0, 1), (1, 0)])]
    all_to_all x2 -> x3, starting transfers between devices: 13.1 us -> 20.5 us  [exchange(): return lax.all_to_all(value, axes, 0, 0, tiled=True)]
    pallas_call x10 -> x11, Pallas kernels: 9.66 us -> 16.7 us  [call(): pl.pallas_call(body, out_shape=outs, in_specs=specs, out_specs=[pl.BlockS...]
    ppermute x3 -> x1, waiting for transfers between devices: 3.13 us -> 0.73 us  [swap_cores(): return lax.ppermute(value, 'depth', [(0, 1), (1, 0)])]
  transfers between devices with their start and end apart: 5 -> 4, of which waited for: 5 -> 4; matrix products, arithmetic and copies ran while one was open for 0% -> 0% of each run, Pallas kernels for 1% -> 5%
where the time goes in v2:
time: 162 us; the launch traced here: 161 us
  blocking collectives  77.9 us (48%)
  waiting for transfers between devices  40.9 us (25%)
  starting transfers between devices  23.4 us (14%)
  Pallas kernels  16.7 us (10%)
  local copies, waits for them, and re-layouts  1.75 us (1%)
    all_to_all x3, blocking collectives, exchange(): return lax.all_to_all(value, axes, 0, 0, tiled=True)  68.9 us
    all_to_all x3, waiting for transfers between devices, exchange(): return lax.all_to_all(value, axes, 0, 0, tiled=True)  40.2 us
    all_to_all x3, starting transfers between devices, exchange(): return lax.all_to_all(value, axes, 0, 0, tiled=True)  20.5 us
    pallas_call x11, Pallas kernels, call(): pl.pallas_call(body, out_shape=outs, in_specs=specs, out_specs=[pl.BlockS...  16.7 us
    all_gather x2, blocking collectives, both_cores(): return lax.all_gather(value, 'depth', axis=0, tiled=False)  9 us
  transfers between devices with their start and end apart: 4, of which 4 were waited for; matrix products, arithmetic and copies ran while one was open for 0% of the time, Pallas kernels for 5%

profile of v2, /device:TPU:1, one launch (start us, length us, event | category | flops | bytes accessed | tf_op | source)
XLA Modules:
  0.0 161.4 jit_solution(17390700411600728456)
XLA Ops:
  0.6 2.0 %shard_map.145 = bf16[128,16,128]{2,1,0:T(8,128)(2,1)S(1)} custom-call(bf16[32,32,128]{2,1,0:T(8,128)(2,1)} %refs_1_.9, s32[32,32]{1,0:T(8,128)} %refs_2_.1, f32[1,128]{1,0:T(1,128)} %bitcast.20, f32[1,128]{1,0:T(1,128)} %bitcast.17, bf16[128,512]{1,0:T(8,128)(2,1)} %refs_1_.8), custom_call_target="tpu_custom_call" | custom-call | flops 2000000 | bytes 922624 | tf_op jit(solution)/shard_map/pallas_call | solution.py:55
  2.6 33.6 %all_to_all.30 = bf16[128,16,128]{2,1,0:T(8,128)(2,1)S(1)} all-to-all(bf16[128,16,128]{2,1,0:T(8,128)(2,1)S(1)} %shard_map.145), channel_id=1, replica_groups=mesh['row'=16,'col'=8,'depth'=2] {'row','col'}, dimensions={0} | all-to-all | bytes 1048576 | tf_op jit(solution)/shard_map/all_to_all | solution.py:324
  36.2 3.0 %collective-permute-start = (bf16[8,2,8,16,128]{4,3,2,1,0:T(8,128)(2,1)S(1)}, bf16[8,2,8,16,128]{4,3,2,1,0:T(8,128)(2,1)S(1)}, u32[]{:S(2)}, u32[]{:S(2)}) collective-permute-start(bf16[8,2,8,16,128]{4,3,2,1,0:T(8,128)(2,1)S(1)} %bitcast.12), channel_id=1, source_target_pairs={{0,1},{1,0},{2,3},{3,2},{4,5},{5,4},{6,7},{7,6},{8,9},{9,8},{10,11... | collective-permute-start | bytes 1572872 | tf_op jit(solution)/shard_map/ppermute | solution.py:316
  39.2 0.8 shard_map.146
  40.0 0.7 collective-permute-done.refs_1_
  40.7 1.6 shard_map.147
  42.3 6.6 %all-to-all-start.1 = ((bf16[128,8,128]{2,1,0:T(8,128)(2,1)}), bf16[128,8,128]{2,1,0:T(8,128)(2,1)S(1)}, u32[]{:S(2)}, u32[]{:S(2)}) async-start(bf16[128,8,128]{2,1,0:T(8,128)(2,1)} %shard_map.147), calls=%async_computation.1 | async-start | bytes 524288 | tf_op jit(solution)/shard_map/all_to_all | solution.py:324
  48.9 1.8 %shard_map.148.refs_1_ = f32[128,1024]{1,0:T(8,128)S(1)} custom-call(bf16[32,32,128]{2,1,0:T(8,128)(2,1)} %refs_1_.9, bf16[32,32,128]{2,1,0:T(8,128)(2,1)} %refs_1_.7, f32[1,128]{1,0:T(1,128)} %bitcast.21, f32[1,128]{1,0:T(1,128)} %bitcast.18, f32[1,128]{1,0:T(1,128)} %bitcast.24, bf16[128,128]{1,0:T(8,128)(2,1)} %refs_8_.1, bf16[128,128]{1,0:T(8,128)(2,1)} %refs_9_.1), custom_call_target="tpu_custom_call" | custom-call | flops 500000000 | bytes 1115648 | tf_op jit(solution)/shard_map/pallas_call | solution.py:55
  50.7 11.3 %all-to-all-done.1.refs_0_.refs_10_ = bf16[128,8,128]{2,1,0:T(8,128)(2,1)S(1)} async-done(((bf16[128,8,128]{2,1,0:T(8,128)(2,1)}), bf16[128,8,128]{2,1,0:T(8,128)(2,1)S(1)}, u32[]{:S(2)}, u32[]{:S(2)}) %all-to-all-start.1) | async-done | bytes 262176 | tf_op jit(solution)/shard_map/all_to_all | solution.py:324
  62.0 0.5 shard_map.149
  62.5 18.9 %all_to_all.31 = bf16[128,8,128]{2,1,0:T(8,128)(2,1)S(1)} all-to-all(bf16[128,8,128]{2,1,0:T(8,128)(2,1)S(1)} %shard_map.149), channel_id=1, replica_groups=mesh['row'=16,'col'=8,'depth'=2] {'row','col'}, dimensions={0} | all-to-all | bytes 524288 | tf_op jit(solution)/shard_map/all_to_all | solution.py:324
  81.4 5.4 %all-gather = bf16[256,8,128]{2,1,0:T(8,128)(2,1)S(1)} all-gather(bf16[128,8,128]{2,1,0:T(8,128)(2,1)S(1)} %all_to_all.31), channel_id=2, replica_groups=mesh['row'=16,'col'=8,'depth'=2] {'depth'}, dimensions={0}, use_global_device_ids=true | all-gather | bytes 786432 | tf_op jit(solution)/shard_map/all_gather | solution.py:320
  86.8 2.4 %shard_map.150.refs_11_ = bf16[128,16,128]{2,1,0:T(8,128)(2,1)} custom-call(bf16[2,128,8,128]{3,2,1,0:T(8,128)(2,1)S(1)} %bitcast.11, bf16[512,256]{1,0:T(8,128)(2,1)S(1)} %get-tuple-element.22.refs_1_, bf16[512,256]{1,0:T(8,128)(2,1)S(1)} %get-tuple-element.23.refs_2_), custom_call_target="tpu_custom_call" | custom-call | flops 2000000 | bytes 1572864 | tf_op jit(solution)/shard_map/pallas_call | solution.py:55
  89.1 6.4 %all-to-all-start.3 = ((bf16[128,16,128]{2,1,0:T(8,128)(2,1)}), bf16[128,16,128]{2,1,0:T(8,128)(2,1)S(1)}, u32[]{:S(2)}, u32[]{:S(2)}) async-start(bf16[128,16,128]{2,1,0:T(8,128)(2,1)} %shard_map.150.refs_11_), calls=%async_computation.3 | async-start | bytes 1048576 | tf_op jit(solution)/shard_map/all_to_all | solution.py:324
  95.5 0.0 copy-start
  95.5 2.9 %shard_map.151 = (bf16[512,1024]{1,0:T(8,128)(2,1)S(1)}, bf16[128,1024]{1,0:T(8,128)(2,1)S(1)}, bf16[128,1024]{1,0:T(8,128)(2,1)S(1)}, f32[128,1024]{1,0:T(8,128)S(1)}, f32[384,128]{1,0:T(8,128)S(1)}) custom-call(bf16[32,32,128]{2,1,0:T(8,128)(2,1)} %refs_1_.9, bf16[32,32,128]{2,1,0:T(8,128)(2,1)} %refs_1_.7, s32[32,32]{1,0:T(8,128)} %refs_2_.1, ...), custom_call_target="tpu_custom_call" | custom-call | flops 500000000 | bytes 3807232 | tf_op jit(solution)/shard_map/pallas_call | solution.py:55
  98.4 15.2 %all-to-all-done.3.refs_0_ = bf16[128,16,128]{2,1,0:T(8,128)(2,1)S(1)} async-done(((bf16[128,16,128]{2,1,0:T(8,128)(2,1)}), bf16[128,16,128]{2,1,0:T(8,128)(2,1)S(1)}, u32[]{:S(2)}, u32[]{:S(2)}) %all-to-all-start.3) | async-done | bytes 524320 | tf_op jit(solution)/shard_map/all_to_all | solution.py:324
  113.7 0.0 copy-done
  113.7 1.6 %shard_map.152 = (bf16[128,8,128]{2,1,0:T(8,128)(2,1)}, f32[128,1024]{1,0:T(8,128)S(1)}) custom-call(bf16[128,16,128]{2,1,0:T(8,128)(2,1)S(1)} %all-to-all-done.3.refs_0_, bf16[128,512]{1,0:T(8,128)(2,1)S(1)} %copy-done, bf16[512,1024]{1,0:T(8,128)(2,1)S(1)} %get-tuple-element.24.refs_2_, bf16[128,1024]{1,0:T(8,128)(2,1)S(1)} %get-tuple-element.25.refs_3_, ...), custom_call_target="tpu_custom_call" | custom-call | flops 2000000 | bytes 3735552 | tf_op jit(solution)/shard_map/pallas_call | solution.py:55
  115.3 0.0 copy-start.2
  115.3 0.8 copy-done.2
  116.1 0.0 copy-start.3
  116.1 7.5 %all-to-all-start.4 = ((bf16[256,4,128]{2,1,0:T(4,128)(2,1)}), bf16[256,4,128]{2,1,0:T(4,128)(2,1)S(1)}, u32[]{:S(2)}, u32[]{:S(2)}) async-start(bf16[256,4,128]{2,1,0:T(4,128)(2,1)} %bitcast.7), calls=%async_computation.4 | async-start | bytes 524288 | tf_op jit(solution)/shard_map/all_to_all | solution.py:324
  123.6 0.0 copy-done.3
  123.6 2.2 %shard_map.153.refs_1_ = bf16[32,32,128]{2,1,0:T(8,128)(2,1)} custom-call(f32[128,1024]{1,0:T(8,128)S(1)} %copy-done.3, bf16[32,32,128]{2,1,0:T(8,128)(2,1)} %refs_1_.9, f32[1,128]{1,0:T(1,128)} %bitcast.23), custom_call_target="tpu_custom_call" | custom-call | flops 500000000 | bytes 1049088 | tf_op jit(solution)/shard_map/pallas_call | solution.py:55
  125.8 13.7 %all-to-all-done.4 = bf16[256,4,128]{2,1,0:T(4,128)(2,1)S(1)} async-done(((bf16[256,4,128]{2,1,0:T(4,128)(2,1)}), bf16[256,4,128]{2,1,0:T(4,128)(2,1)S(1)}, u32[]{:S(2)}, u32[]{:S(2)}) %all-to-all-start.4) | async-done | bytes 262176 | tf_op jit(solution)/shard_map/all_to_all | solution.py:324
  139.5 0.0 copy-start.1
  139.5 0.9 copy-done.1
  140.4 0.1 shard_map.154
  140.6 16.4 %all_to_all.32 = bf16[128,4,128]{2,1,0:T(4,128)(2,1)S(1)} all-to-all(bf16[128,4,128]{2,1,0:T(4,128)(2,1)S(1)} %bitcast.15), channel_id=1, replica_groups=mesh['row'=16,'col'=8,'depth'=2] {'row','col'}, dimensions={0} | all-to-all | bytes 262144 | tf_op jit(solution)/shard_map/all_to_all | solution.py:324
  157.0 3.6 %all_gather.11.refs_0_ = bf16[2,64,8,128]{3,2,1,0:T(8,128)(2,1)S(1)} all-gather(bf16[1,64,8,128]{3,2,1,0:T(8,128)(2,1)S(1)} %bitcast.16), channel_id=1, replica_groups=mesh['row'=16,'col'=8,'depth'=2] {'depth'}, dimensions={0}, use_global_device_ids=true | all-gather | bytes 393216 | tf_op jit(solution)/shard_map/all_gather | solution.py:320
  160.6 0.8 shard_map.155
Async XLA Ops:
  36.2 4.5 %collective-permute-start = (bf16[8,2,8,16,128]{4,3,2,1,0:T(8,128)(2,1)S(1)}, bf16[8,2,8,16,128]{4,3,2,1,0:T(8,128)(2,1)S(1)}, u32[]{:S(2)}, u32[]{:S(2)}) collective-permute-start(bf16[8,2,8,16,128]{4,3,2,1,0:T(8,128)(2,1)S(1)} %bitcast.12), channel_id=1, source_target_pairs={{0,1},{1,0},{2,3},{3,2},{4,5},{5,4},{6,7},{7,6},{8,9},{9,8},{10,11... | collective-permute-start | bytes 1572872 | tf_op jit(solution)/shard_map/ppermute | solution.py:316
  42.3 19.7 %all-to-all-start.1 = ((bf16[128,8,128]{2,1,0:T(8,128)(2,1)}), bf16[128,8,128]{2,1,0:T(8,128)(2,1)S(1)}, u32[]{:S(2)}, u32[]{:S(2)}) async-start(bf16[128,8,128]{2,1,0:T(8,128)(2,1)} %shard_map.147), calls=%async_computation.1 | async-start | bytes 524288 | tf_op jit(solution)/shard_map/all_to_all | solution.py:324
  89.1 24.5 %all-to-all-start.3 = ((bf16[128,16,128]{2,1,0:T(8,128)(2,1)}), bf16[128,16,128]{2,1,0:T(8,128)(2,1)S(1)}, u32[]{:S(2)}, u32[]{:S(2)}) async-start(bf16[128,16,128]{2,1,0:T(8,128)(2,1)} %shard_map.150.refs_11_), calls=%async_computation.3 | async-start | bytes 1048576 | tf_op jit(solution)/shard_map/all_to_all | solution.py:324
  95.5 18.2 %copy-start = (bf16[128,512]{1,0:T(8,128)(2,1)S(1)}, bf16[128,512]{1,0:T(8,128)(2,1)}, u32[]{:S(2)}) copy-start(bf16[128,512]{1,0:T(8,128)(2,1)} %refs_1_.8) | copy-start | bytes 393220
  115.3 0.8 copy-start.2
  116.1 7.5 %copy-start.3 = (f32[128,1024]{1,0:T(8,128)S(1)}, f32[128,1024]{1,0:T(8,128)}, u32[]{:S(2)}) copy-start(f32[128,1024]{1,0:T(8,128)} %copy-done.2) | copy-start | bytes 1572868
  116.1 23.4 %all-to-all-start.4 = ((bf16[256,4,128]{2,1,0:T(4,128)(2,1)}), bf16[256,4,128]{2,1,0:T(4,128)(2,1)S(1)}, u32[]{:S(2)}, u32[]{:S(2)}) async-start(bf16[256,4,128]{2,1,0:T(4,128)(2,1)} %bitcast.7), calls=%async_computation.4 | async-start | bytes 524288 | tf_op jit(solution)/shard_map/all_to_all | solution.py:324
  139.5 1.0 copy-start.1

commit v3 on v2

--- a/solution.py
+++ b/solution.py
@@ -3,31 +3,40 @@
 from jax import lax
 from jax.experimental import pallas as pl
 from jax.experimental.pallas import tpu as pltpu
+from jax.sharding import Mesh
 from jax.sharding import PartitionSpec as P
 
 F32 = jnp.float32
 BF16 = jnp.bfloat16
-PLANE = ("row", "col")
 T = 32
 CH = 128
 CELLS = T * T
 SUB = 8
 GROUPS = T // SUB
-HALF = SUB // 2
-
-
-def call(kernel, outs, *args, scratch=(), flops=2_000_000, spaces=None, fetched=()):
+ROW = ("y", "z_lo")
+COL = ("x", "z_hi")
+SIZES = (4, 4, 4, 2, 2)
+PLANE = ("z_lo", "y") + COL
+FLAT = ("depth", "y", "x")
+UPRIGHT = ("z_lo", "z_hi")
+PARTS = 32
+PEERS = 8
+PART = CELLS // PARTS
+
+
+def call(kernel, outs, *args, scratch=(), flops=2_000_000, spaces=None, fetched=(), hbm=(), hbm_outs=()):
     spaces = spaces or {}
     fetched = tuple(fetched)
+    hbm = fetched + tuple(hbm)
     count = len(args)
     specs = [
-        pl.BlockSpec(memory_space=pltpu.HBM if i in fetched else spaces.get(i, pltpu.VMEM))
+        pl.BlockSpec(memory_space=pltpu.HBM if i in hbm else spaces.get(i, pltpu.VMEM))
         for i in range(count)
     ]
     moved = sum(a.size * a.dtype.itemsize for a in args)
     moved += sum(o.size * o.dtype.itemsize for o in outs)
     args = [
-        pltpu.with_memory_space_constraint(a, pltpu.HBM) if i in fetched else a
+        pltpu.with_memory_space_constraint(a, pltpu.HBM) if i in hbm else a
         for i, a in enumerate(args)
     ]
 
@@ -54,9 +63,12 @@
         extra.append(pltpu.SemaphoreType.DMA((len(fetched),)))
     return pl.pallas_call(
         body,
-        out_shape=outs,
+        out_shape=[pltpu.HBM(o.shape, o.dtype) if i in hbm_outs else o for i, o in enumerate(outs)],
         in_specs=specs,
-        out_specs=[pl.BlockSpec(memory_space=pltpu.VMEM) for _ in outs],
+        out_specs=[
+            pl.BlockSpec(memory_space=pltpu.HBM if i in hbm_outs else pltpu.VMEM)
+            for i in range(len(outs))
+        ],
         scratch_shapes=list(scratch) + extra,
         compiler_params=pltpu.CompilerParams(vmem_limit_bytes=32 * 1024 * 1024),
         cost_estimate=pl.CostEstimate(flops=flops, bytes_accessed=moved, transcendentals=0),
@@ -123,7 +135,7 @@
     blocks = tiles.shape[0]
     halves = []
     for half in range(2):
-        parts = [tiles[:, half * 4 + part].astype(F32) for part in range(4)]
+        parts = [tiles[:, 2 * part + half].astype(F32) for part in range(4)]
         rows = jnp.stack(swap_groups(parts), axis=1)
         halves.append(rows.reshape(blocks * T, CH))
     return jnp.concatenate(halves, axis=1)
@@ -131,11 +143,11 @@
 
 def from_matrix(matrix):
     blocks = matrix.shape[0] // T
-    parts = []
+    halves = []
     for half in range(2):
         rows = matrix[:, half * CH : (half + 1) * CH].reshape(blocks, GROUPS, SUB, CH)
-        parts += list(swap_groups([rows[:, g] for g in range(GROUPS)]))
-    return jnp.stack(parts, axis=1)
+        halves.append(swap_groups([rows[:, g] for g in range(GROUPS)]))
+    return jnp.stack([halves[half][part] for part in range(4) for half in range(2)], axis=1)
 
 
 def normalise(pair, gain, bias):
@@ -176,23 +188,23 @@
     tangent[...] = dot(w_out[...], d_out_proj, 1, 0) * column(x_gain[...])
 
 
-def product_rows(tiles, mine):
-    return to_matrix(tiles[:, pl.ds(mine, 1), :, SUB:].reshape(8, 8, SUB, CH)).astype(BF16)
-
-
-def product_own_kernel(parity, own, left_out, right_out, partial):
-    mine = lax.bitwise_and(parity[0], 1)
-    left = to_matrix(own[:, :, :, :SUB].reshape(16, 8, SUB, CH)).astype(BF16)
+def product_theirs_kernel(parity, own, left_out, theirs):
+    other = 1 - lax.bitwise_and(parity[0], 1)
+    left = to_matrix(own[:, :, :, :, :SUB].reshape(16, 8, SUB, CH)).astype(BF16)
     left_out[...] = left
-    right_out[...] = to_matrix(own[:, :, :, SUB:].reshape(16, 8, SUB, CH)).astype(BF16)
-    partial[...] = dot(left, product_rows(own, mine), 1, 1)
-
-
-def product_kernel(parity, other, partial, send):
-    mine = lax.bitwise_and(parity[0], 1)
-    left = to_matrix(other[:, :, :, :SUB].reshape(16, 8, SUB, CH)).astype(BF16)
-    x = partial[...] + dot(left, product_rows(other, mine), 1, 1)
-    send[...] = from_matrix(x).reshape(CH, SUB, CH).astype(BF16)
+    right = to_matrix(own[:, pl.ds(other, 1), :, :, SUB:].reshape(8, 8, SUB, CH)).astype(BF16)
+    theirs[...] = from_matrix(dot(left, right, 1, 1)).reshape(CH, SUB, CH).astype(BF16)
+
+
+def product_mine_kernel(parity, own, left, right_out, mine):
+    place = lax.bitwise_and(parity[0], 1)
+    right_out[...] = to_matrix(own[:, :, :, :, SUB:].reshape(16, 8, SUB, CH)).astype(BF16)
+    right = to_matrix(own[:, pl.ds(place, 1), :, :, SUB:].reshape(8, 8, SUB, CH)).astype(BF16)
+    mine[...] = from_matrix(dot(left[...], right, 1, 1)).reshape(CH, SUB, CH)
+
+
+def product_kernel(mine, got, send):
+    send[...] = (mine[...] + got[...].astype(F32)).astype(BF16)
 
 
 def inner_kernel(recv, tangent, send, scratch):
@@ -247,21 +259,26 @@
     partial[...] = dot(w_gate[...], d_gate_pre, 1, 0)
 
 
-def back_kernel(dx, left, right, send):
-    pairs = right[...].reshape(8, 2, T, 2 * CH)
-    da = None
-    dbs = []
-    for half in range(2):
-        grad = to_matrix(dx[half].reshape(16, 8, SUB, CH)).astype(BF16)
-        term = dot(grad, pairs[:, half].reshape(8 * T, 2 * CH), 1, 0)
-        da = term if da is None else da + term
-        dbs.append(dot(grad, left[...], 0, 0).reshape(8, T, 2 * CH))
-    db = jnp.stack(dbs, axis=1).reshape(16 * T, 2 * CH)
-    send[:, :SUB] = from_matrix(da).reshape(CH, SUB, CH).astype(BF16)
-    send[:, SUB:] = from_matrix(db).reshape(CH, SUB, CH).astype(BF16)
-
-
-def project_kernel(recv, in_proj, coef, normed, zhat, partial, early, send, d_normed, scratch, packed):
+def back_mine_kernel(parity, own, left, right, da, db):
+    place = lax.bitwise_and(parity[0], 1)
+    grad = to_matrix(own[...].reshape(16, 8, SUB, CH)).astype(BF16)
+    da[...] = dot(grad, right[:, pl.ds(place, 1)].reshape(8 * T, 2 * CH), 1, 0)
+    db[...] = from_matrix(dot(grad, left[...], 0, 0)).astype(BF16)
+
+
+def back_kernel(parity, other, left, right, da_mine, db_mine, send):
+    place = lax.bitwise_and(parity[0], 1)
+    grad = to_matrix(other[...].reshape(16, 8, SUB, CH)).astype(BF16)
+    da = da_mine[...] + dot(grad, right[:, pl.ds(1 - place, 1)].reshape(8 * T, 2 * CH), 1, 0)
+    db = from_matrix(dot(grad, left[...], 0, 0)).astype(BF16)
+    send[:, :, :, :, :SUB] = from_matrix(da).reshape(2, 2, 4, 8, SUB, CH).astype(BF16)
+    send[:, pl.ds(place, 1), :, :, SUB:] = db_mine[...].reshape(2, 1, 4, 8, SUB, CH)
+    send[:, pl.ds(1 - place, 1), :, :, SUB:] = db.reshape(2, 1, 4, 8, SUB, CH)
+
+
+def project_kernel(
+    recv, in_proj, coef, normed, zhat, partial, early, send, d_normed, scratch, packed, kept, sem
+):
     scratch[...] = recv[...].astype(F32).reshape(2 * CELLS, CH)
     da = from_tiles(scratch, 0, 2 * SUB)
     db = from_tiles(scratch, SUB, 2 * SUB)
@@ -274,7 +291,9 @@
     )
     g_in = dot(normed[...], d_proj, 1, 1)
     grad = dot(in_proj[...], d_proj, 1, 0) + partial[...]
-    d_normed[...] = grad
+    kept[...] = grad
+    copy = pltpu.make_async_copy(kept, d_normed, sem)
+    copy.start()
     for part in range(4):
         packed[pl.ds(part, CH, stride=SUB), :] = g_in[:, part * CH : (part + 1) * CH]
     packed[pl.ds(4, CH, stride=SUB), :] = early[0:CH]
@@ -284,6 +303,7 @@
     )
     packed[pl.ds(7, CH, stride=SUB), :] = jnp.zeros((CH, CH), F32)
     send[...] = packed[...].reshape(CH, SUB, CH).astype(BF16)
+    copy.wait()
 
 
 def pair_kernel(d_normed, pair, gain, out):
@@ -297,27 +317,22 @@
 
 def total_kernel(recv, after, send):
     total = jnp.sum(recv[...].astype(F32), axis=0, keepdims=True)
-    total = total + pltpu.roll(total, HALF, 1)
-    send[...] = jnp.broadcast_to(total, (CH // 2, SUB, CH)).astype(BF16)
+    send[...] = jnp.broadcast_to(total, send.shape).astype(BF16)
 
 
 def unpack_kernel(totals, g_in, g_gate, g_out, ln_in, inner, scratch):
     scratch[...] = totals[...].astype(F32).reshape(CELLS, CH)
-    for part in range(HALF):
-        g_in[:, part * CH : (part + 1) * CH] = scratch[pl.ds(part, CH, stride=HALF), :]
-    g_gate[...] = scratch[pl.ds(CELLS // 2, CH, stride=HALF), :]
-    g_out[...] = scratch[pl.ds(CELLS // 2 + 1, CH, stride=HALF), :]
-    norms = jnp.transpose(scratch[pl.ds(CELLS // 2 + 2, CH, stride=HALF), :])
+    for part in range(4):
+        g_in[:, part * CH : (part + 1) * CH] = scratch[pl.ds(part, CH, stride=SUB), :]
+    g_gate[...] = scratch[pl.ds(4, CH, stride=SUB), :]
+    g_out[...] = scratch[pl.ds(5, CH, stride=SUB), :]
+    norms = jnp.transpose(scratch[pl.ds(6, CH, stride=SUB), :])
     ln_in[...] = norms[0:2]
     inner[...] = norms[2:4]
 
 
 def swap_cores(value):
     return lax.ppermute(value, "depth", [(0, 1), (1, 0)])
-
-
-def both_cores(value):
-    return lax.all_gather(value, "depth", axis=0, tiled=False)
 
 
 def exchange(value, axes=PLANE):
@@ -361,17 +376,22 @@
         scratch=[pairs_of_tiles],
         fetched=range(5),
     )
-    factors = exchange(factors).reshape(8, 2, 8, 2 * SUB, CH)
-    left, right, partial = call(
-        product_own_kernel,
-        [matrix, matrix, struct((16 * T, 2 * CH), F32)],
+    factors, parity = lax.optimization_barrier((factors, parity))
+    factors = exchange(factors).reshape(2, 2, 4, 8, 2 * SUB, CH)
+    left, x_theirs = call(
+        product_theirs_kernel, [matrix, one], parity, factors, spaces={0: pltpu.SMEM}
+    )
+    x_got = swap_cores(x_theirs)
+    right, x_mine = call(
+        product_mine_kernel,
+        [matrix, struct((CH, SUB, CH), F32)],
         parity,
         factors,
+        left,
         spaces={0: pltpu.SMEM},
     )
-    (x_send,) = call(
-        product_kernel, [one], parity, swap_cores(factors), partial, spaces={0: pltpu.SMEM}
-    )
+    right = right.reshape(2, 2, 4 * T, 2 * CH)
+    (x_send,) = call(product_kernel, [one], x_mine, x_got)
     x_recv = exchange(x_send)
     (tangent,) = call(
         tangent_kernel,
@@ -387,7 +407,28 @@
         fetched=range(7),
     )
     (dx_send,) = call(inner_kernel, [one], x_recv, tangent, scratch=[tiles])
-    (back_send,) = call(back_kernel, [two], both_cores(exchange(dx_send)), left, right)
+    dx = exchange(dx_send)
+    da, db = call(
+        back_mine_kernel,
+        [struct((16 * T, 2 * CH), F32), struct((8, 8, SUB, CH), BF16)],
+        parity,
+        dx,
+        left,
+        right,
+        spaces={0: pltpu.SMEM},
+    )
+    (back_send,) = call(
+        back_kernel,
+        [struct((2, 2, 4, 8, 2 * SUB, CH), BF16)],
+        parity,
+        swap_cores(dx),
+        left,
+        right,
+        da,
+        db,
+        spaces={0: pltpu.SMEM},
+    )
+    back_send = back_send.reshape(CH, 2 * SUB, CH)
     back = exchange(back_send)
     coef, normed, zhat, partial, early = call(
         output_kernel,
@@ -407,7 +448,7 @@
         scratch=[tiles],
         flops=500_000_000,
         fetched=range(10),
-        spaces={11: pl.ANY},
+        hbm=(11,),
     )
     weights, d_normed = call(
         project_kernel,
@@ -419,9 +460,15 @@
         zhat,
         partial,
         early,
-        scratch=[pairs_of_tiles, tiles],
-    )
-    weights = exchange(weights.reshape(2 * CH, HALF, CH), ("row", "col", "depth"))
+        scratch=[
+            pairs_of_tiles,
+            tiles,
+            pltpu.VMEM((CH, CELLS), F32),
+            pltpu.SemaphoreType.DMA,
+        ],
+        hbm_outs=(1,),
+    )
+    weights = exchange(weights.reshape(PARTS, PART, CH), FLAT)
     (grad_pair,) = call(
         pair_kernel,
         [struct((T, T, CH), BF16)],
@@ -429,31 +476,32 @@
         pair,
         in_gain,
         flops=500_000_000,
-        fetched=(1, 2),
+        fetched=range(3),
     )
     (totals,) = call(
-        total_kernel,
-        [struct((CH // 2, SUB, CH), BF16)],
-        weights.reshape(CH, SUB, CH),
-        grad_pair,
-        spaces={1: pl.ANY},
-    )
-    totals = exchange(totals.reshape(CH, HALF, CH))
+        total_kernel, [struct((PEERS, PART, CH), BF16)], weights, grad_pair, hbm=(1,)
+    )
+    totals = exchange(totals, UPRIGHT)
+    (totals,) = call(
+        total_kernel, [struct((PARTS, PART, CH), BF16)], totals, grad_pair, hbm=(1,)
+    )
+    totals = exchange(totals, FLAT).reshape(CH, SUB, CH)
     g_in, g_gate, g_out, ln_in, inner = call(
         unpack_kernel,
         [struct((CH, 4 * CH), F32), square, square, struct((2, CH), F32), struct((2, CH), F32)],
-        both_cores(totals.reshape(CH // 2, SUB, CH)),
+        totals,
         scratch=[tiles],
     )
     return grad_pair, g_in, g_gate, g_out, ln_in, inner
 
 
 def solution(mesh):
-    cells = P("row", ("col", "depth"), None)
+    fine = Mesh(mesh.devices.reshape(SIZES), ROW + COL + ("depth",))
+    cells = P(ROW, COL + ("depth",), None)
     return jax.shard_map(
         per_device,
-        mesh=mesh,
-        in_specs=(cells, cells, P("row", ("col", "depth"))) + (P(),) * 7,
+        mesh=fine,
+        in_specs=(cells, cells, P(ROW, COL + ("depth",))) + (P(),) * 7,
         out_specs=(cells,) + (P(),) * 5,
         check_vma=False,
     )

time: 162 us -> 152 us (0.938)
  waiting for transfers between devices: 40.9 us -> 31.9 us
  blocking collectives: 77.9 us -> 75.5 us
  starting transfers between devices: 23.4 us -> 25.8 us
  local copies, waits for them, and re-layouts: 1.75 us -> 0.01 us
    all_gather x2 -> x0, blocking collectives: 9 us -> none  [both_cores(): return lax.all_gather(value, 'depth', axis=0, tiled=False)]
    all_to_all x3, waiting for transfers between devices: 40.2 us -> 31.4 us  [exchange(): return lax.all_to_all(value, axes, 0, 0, tiled=True)]
    all_to_all x3 -> x4, blocking collectives: 68.9 us -> 75.5 us  [exchange(): return lax.all_to_all(value, axes, 0, 0, tiled=True)]
    ppermute x1 -> x2, starting transfers between devices: 2.98 us -> 6.33 us  [swap_cores(): return lax.ppermute(value, 'depth', [(0, 1), (1, 0)])]
    unnamed x8 -> x2, local copies, waits for them, and re-layouts: 1.75 us -> 0.01 us
    pallas_call x11 -> x14, Pallas kernels: 16.7 us -> 17.8 us  [call(): pl.pallas_call(body, out_shape=[pltpu.HBM(o.shape, o.dtype) if i in hbm_o...]
  transfers between devices with their start and end apart: 4 -> 5, of which waited for: 4 -> 5; matrix products, arithmetic and copies ran while one was open for 0% -> 0% of each run, Pallas kernels for 5% -> 6%
where the time goes in v3:
time: 152 us
  blocking collectives  75.5 us (50%)
  waiting for transfers between devices  31.9 us (21%)
  starting transfers between devices  25.8 us (17%)
  Pallas kernels  17.8 us (12%)
    all_to_all x4, blocking collectives, exchange(): return lax.all_to_all(value, axes, 0, 0, tiled=True)  75.5 us
    all_to_all x3, waiting for transfers between devices, exchange(): return lax.all_to_all(value, axes, 0, 0, tiled=True)  31.4 us
    all_to_all x3, starting transfers between devices, exchange(): return lax.all_to_all(value, axes, 0, 0, tiled=True)  19.5 us
    pallas_call x14, Pallas kernels, call(): pl.pallas_call(body, out_shape=[pltpu.HBM(o.shape, o.dtype) if i in hbm_o...  17.8 us
    ppermute x2, starting transfers between devices, swap_cores(): return lax.ppermute(value, 'depth', [(0, 1), (1, 0)])  6.33 us
  transfers between devices with their start and end apart: 5, of which 5 were waited for; matrix products, arithmetic and copies ran while one was open for 0% of the time, Pallas kernels for 6%

profile of v3, /device:TPU:1, one launch (start us, length us, event | category | flops | bytes accessed | tf_op | source)
XLA Modules:
  0.0 151.8 jit_solution(16497404163778817088)
XLA Ops:
  0.6 1.9 %shard_map.145 = bf16[128,16,128]{2,1,0:T(8,128)(2,1)S(1)} custom-call(bf16[32,32,128]{2,1,0:T(8,128)(2,1)} %refs_1_.9, s32[32,32]{1,0:T(8,128)} %refs_2_.1, f32[1,128]{1,0:T(1,128)} %bitcast.18, f32[1,128]{1,0:T(1,128)} %bitcast.15, bf16[128,512]{1,0:T(8,128)(2,1)} %refs_1_.8), custom_call_target="tpu_custom_call" | custom-call | flops 2000000 | bytes 922624 | tf_op jit(solution)/shard_map/pallas_call | solution.py:64
  2.6 33.6 %all_to_all.35 = bf16[128,16,128]{2,1,0:T(8,128)(2,1)S(1)} all-to-all(bf16[128,16,128]{2,1,0:T(8,128)(2,1)S(1)} %shard_map.145), channel_id=1, replica_groups=mesh['y'=4,'z_lo'=4,'x'=4,'z_hi'=2,'depth'=2] {'z_lo','y','x','z_hi'}, dimensions={0} | all-to-all | bytes 1048576 | tf_op jit(solution)/shard_map/all_to_all | solution.py:339
  36.2 0.9 shard_map.146
  37.1 2.9 %collective-permute-start = (bf16[128,8,128]{2,1,0:T(8,128)(2,1)S(1)}, bf16[128,8,128]{2,1,0:T(8,128)(2,1)S(1)}, u32[]{:S(2)}, u32[]{:S(2)}) collective-permute-start(bf16[128,8,128]{2,1,0:T(8,128)(2,1)S(1)} %get-tuple-element.30), channel_id=1, source_target_pairs={{0,1},{1,0},{2,3},{3,2},{4,5},{5,4},{6,7},{7,6},{8,9},{9,8},{10,11... | collective-permute-start | bytes 786440 | tf_op jit(solution)/shard_map/ppermute | solution.py:335
  40.0 1.0 shard_map.147
  41.0 0.2 collective-permute-done.refs_1_
  41.2 0.8 shard_map.148
  41.9 6.6 %all-to-all-start.1 = ((bf16[128,8,128]{2,1,0:T(8,128)(2,1)}), bf16[128,8,128]{2,1,0:T(8,128)(2,1)S(1)}, u32[]{:S(2)}, u32[]{:S(2)}) async-start(bf16[128,8,128]{2,1,0:T(8,128)(2,1)} %shard_map.148), calls=%async_computation.1 | async-start | bytes 524288 | tf_op jit(solution)/shard_map/all_to_all | solution.py:339
  48.6 1.8 %shard_map.149.refs_1_ = f32[128,1024]{1,0:T(8,128)S(1)} custom-call(bf16[32,32,128]{2,1,0:T(8,128)(2,1)} %refs_1_.9, bf16[32,32,128]{2,1,0:T(8,128)(2,1)} %refs_1_.7, f32[1,128]{1,0:T(1,128)} %bitcast.19, f32[1,128]{1,0:T(1,128)} %bitcast.16, f32[1,128]{1,0:T(1,128)} %bitcast.22, bf16[128,128]{1,0:T(8,128)(2,1)} %refs_8_.1, bf16[128,128]{1,0:T(8,128)(2,1)} %refs_9_.1), custom_call_target="tpu_custom_call" | custom-call | flops 500000000 | bytes 1115648 | tf_op jit(solution)/shard_map/pallas_call | solution.py:64
  50.3 10.7 %all-to-all-done.1.refs_0_.refs_10_ = bf16[128,8,128]{2,1,0:T(8,128)(2,1)S(1)} async-done(((bf16[128,8,128]{2,1,0:T(8,128)(2,1)}), bf16[128,8,128]{2,1,0:T(8,128)(2,1)S(1)}, u32[]{:S(2)}, u32[]{:S(2)}) %all-to-all-start.1) | async-done | bytes 262176 | tf_op jit(solution)/shard_map/all_to_all | solution.py:339
  61.0 0.5 shard_map.150
  61.5 18.8 %all_to_all.36.refs_1_ = bf16[128,8,128]{2,1,0:T(8,128)(2,1)S(1)} all-to-all(bf16[128,8,128]{2,1,0:T(8,128)(2,1)S(1)} %shard_map.150), channel_id=1, replica_groups=mesh['y'=4,'z_lo'=4,'x'=4,'z_hi'=2,'depth'=2] {'z_lo','y','x','z_hi'}, dimensions={0} | all-to-all | bytes 524288 | tf_op jit(solution)/shard_map/all_to_all | solution.py:339
  80.3 3.4 %collective-permute-start.1 = (bf16[128,8,128]{2,1,0:T(8,128)(2,1)S(1)}, bf16[128,8,128]{2,1,0:T(8,128)(2,1)S(1)}, u32[]{:S(2)}, u32[]{:S(2)}) collective-permute-start(bf16[128,8,128]{2,1,0:T(8,128)(2,1)S(1)} %all_to_all.36.refs_1_), channel_id=1, source_target_pairs={{0,1},{1,0},{2,3},{3,2},{4,5},{5,4},{6,7},{7,6},{8,9},{9,8},{10,11... | collective-permute-start | bytes 786440 | tf_op jit(solution)/shard_map/ppermute | solution.py:335
  83.8 0.8 shard_map.151
  84.6 0.4 collective-permute-done.1.refs_1_
  85.0 1.6 %shard_map.152 = bf16[2,2,4,8,16,128]{5,4,3,2,1,0:T(8,128)(2,1)} custom-call(s32[1]{0:T(128)} %bitcast.2.refs_0_, bf16[128,8,128]{2,1,0:T(8,128)(2,1)S(1)} %collective-permute-done.1.refs_1_, bf16[512,256]{1,0:T(8,128)(2,1)S(1)} %get-tuple-element.28.refs_2_, bf16[2,2,128,256]{3,2,1,0:T(8,128)(2,1)S(1)} %bitcast.13, ...), custom_call_target="tpu_custom_call" | custom-call | flops 2000000 | bytes 1966084 | tf_op jit(solution)/shard_map/pallas_call | solution.py:64
  86.5 6.7 %all-to-all-start.3 = ((bf16[128,16,128]{2,1,0:T(8,128)(2,1)}), bf16[128,16,128]{2,1,0:T(8,128)(2,1)S(1)}, u32[]{:S(2)}, u32[]{:S(2)}) async-start(bf16[128,16,128]{2,1,0:T(8,128)(2,1)} %bitcast.6.refs_11_), calls=%async_computation.3 | async-start | bytes 1048576 | tf_op jit(solution)/shard_map/all_to_all | solution.py:339
  93.2 0.0 copy-start
  93.2 2.9 %shard_map.153 = (bf16[512,1024]{1,0:T(8,128)(2,1)S(1)}, bf16[128,1024]{1,0:T(8,128)(2,1)S(1)}, bf16[128,1024]{1,0:T(8,128)(2,1)S(1)}, f32[128,1024]{1,0:T(8,128)S(1)}, f32[384,128]{1,0:T(8,128)S(1)}) custom-call(bf16[32,32,128]{2,1,0:T(8,128)(2,1)} %refs_1_.9, bf16[32,32,128]{2,1,0:T(8,128)(2,1)} %refs_1_.7, s32[32,32]{1,0:T(8,128)} %refs_2_.1, ...), custom_call_target="tpu_custom_call" | custom-call | flops 500000000 | bytes 3807232 | tf_op jit(solution)/shard_map/pallas_call | solution.py:64
  96.2 14.8 %all-to-all-done.3.refs_0_ = bf16[128,16,128]{2,1,0:T(8,128)(2,1)S(1)} async-done(((bf16[128,16,128]{2,1,0:T(8,128)(2,1)}), bf16[128,16,128]{2,1,0:T(8,128)(2,1)S(1)}, u32[]{:S(2)}, u32[]{:S(2)}) %all-to-all-start.3) | async-done | bytes 524320 | tf_op jit(solution)/shard_map/all_to_all | solution.py:339
  111.0 0.0 copy-done
  111.0 2.4 %shard_map.154 = (bf16[128,8,128]{2,1,0:T(8,128)(2,1)}, f32[128,1024]{1,0:T(8,128)}) custom-call(bf16[128,16,128]{2,1,0:T(8,128)(2,1)S(1)} %all-to-all-done.3.refs_0_, bf16[128,512]{1,0:T(8,128)(2,1)S(1)} %copy-done, bf16[512,1024]{1,0:T(8,128)(2,1)S(1)} %get-tuple-element.34.refs_2_, bf16[128,1024]{1,0:T(8,128)(2,1)S(1)} %get-tuple-element.35.refs_3_, ...), custom_call_target="tpu_custom_call" | custom-call | flops 2000000 | bytes 3735552 | tf_op jit(solution)/shard_map/pallas_call | solution.py:64
  113.3 6.2 %all-to-all-start.4 = ((bf16[32,32,128]{2,1,0:T(8,128)(2,1)}), bf16[32,32,128]{2,1,0:T(8,128)(2,1)S(1)}, u32[]{:S(2)}, u32[]{:S(2)}) async-start(bf16[32,32,128]{2,1,0:T(8,128)(2,1)} %bitcast.8), calls=%async_computation.4 | async-start | bytes 524288 | tf_op jit(solution)/shard_map/all_to_all | solution.py:339
  119.6 2.4 %shard_map.155.refs_1_ = bf16[32,32,128]{2,1,0:T(8,128)(2,1)} custom-call(f32[128,1024]{1,0:T(8,128)} %get-tuple-element.39.refs_0_, bf16[32,32,128]{2,1,0:T(8,128)(2,1)} %refs_1_.9, f32[1,128]{1,0:T(1,128)} %bitcast.21), custom_call_target="tpu_custom_call" | custom-call | flops 500000000 | bytes 1049088 | tf_op jit(solution)/shard_map/pallas_call | solution.py:64
  121.9 5.9 %all-to-all-done.4.refs_0_ = bf16[32,32,128]{2,1,0:T(8,128)(2,1)S(1)} async-done(((bf16[32,32,128]{2,1,0:T(8,128)(2,1)}), bf16[32,32,128]{2,1,0:T(8,128)(2,1)S(1)}, u32[]{:S(2)}, u32[]{:S(2)}) %all-to-all-start.4) | async-done | bytes 262176 | tf_op jit(solution)/shard_map/all_to_all | solution.py:339
  127.9 9.2 %all_to_all.37.refs_0_ = bf16[8,32,128]{2,1,0:T(8,128)(2,1)S(1)} all-to-all(bf16[8,32,128]{2,1,0:T(8,128)(2,1)S(1)} %shard_map.156), channel_id=1, replica_groups=mesh['y'=4,'z_lo'=4,'x'=4,'z_hi'=2,'depth'=2] {'z_lo','z_hi'}, dimensions={0} | all-to-all | bytes 131072 | tf_op jit(solution)/shard_map/all_to_all | solution.py:339
  137.1 13.8 %all_to_all.38 = bf16[32,32,128]{2,1,0:T(8,128)(2,1)S(1)} all-to-all(bf16[32,32,128]{2,1,0:T(8,128)(2,1)S(1)} %shard_map.157), channel_id=1, replica_groups=mesh['y'=4,'z_lo'=4,'x'=4,'z_hi'=2,'depth'=2] {'depth','y','x'}, dimensions={0} | all-to-all | bytes 524288 | tf_op jit(solution)/shard_map/all_to_all | solution.py:339
  150.9 0.8 shard_map.158
  (2 shorter events, 0.1 us)
Async XLA Ops:
  37.1 4.0 %collective-permute-start = (bf16[128,8,128]{2,1,0:T(8,128)(2,1)S(1)}, bf16[128,8,128]{2,1,0:T(8,128)(2,1)S(1)}, u32[]{:S(2)}, u32[]{:S(2)}) collective-permute-start(bf16[128,8,128]{2,1,0:T(8,128)(2,1)S(1)} %get-tuple-element.30), channel_id=1, source_target_pairs={{0,1},{1,0},{2,3},{3,2},{4,5},{5,4},{6,7},{7,6},{8,9},{9,8},{10,11... | collective-permute-start | bytes 786440 | tf_op jit(solution)/shard_map/ppermute | solution.py:335
  41.9 19.1 %all-to-all-start.1 = ((bf16[128,8,128]{2,1,0:T(8,128)(2,1)}), bf16[128,8,128]{2,1,0:T(8,128)(2,1)S(1)}, u32[]{:S(2)}, u32[]{:S(2)}) async-start(bf16[128,8,128]{2,1,0:T(8,128)(2,1)} %shard_map.148), calls=%async_computation.1 | async-start | bytes 524288 | tf_op jit(solution)/shard_map/all_to_all | solution.py:339
  80.3 4.6 %collective-permute-start.1 = (bf16[128,8,128]{2,1,0:T(8,128)(2,1)S(1)}, bf16[128,8,128]{2,1,0:T(8,128)(2,1)S(1)}, u32[]{:S(2)}, u32[]{:S(2)}) collective-permute-start(bf16[128,8,128]{2,1,0:T(8,128)(2,1)S(1)} %all_to_all.36.refs_1_), channel_id=1, source_target_pairs={{0,1},{1,0},{2,3},{3,2},{4,5},{5,4},{6,7},{7,6},{8,9},{9,8},{10,11... | collective-permute-start | bytes 786440 | tf_op jit(solution)/shard_map/ppermute | solution.py:335
  86.5 24.4 %all-to-all-start.3 = ((bf16[128,16,128]{2,1,0:T(8,128)(2,1)}), bf16[128,16,128]{2,1,0:T(8,128)(2,1)S(1)}, u32[]{:S(2)}, u32[]{:S(2)}) async-start(bf16[128,16,128]{2,1,0:T(8,128)(2,1)} %bitcast.6.refs_11_), calls=%async_computation.3 | async-start | bytes 1048576 | tf_op jit(solution)/shard_map/all_to_all | solution.py:339
  93.2 17.7 %copy-start = (bf16[128,512]{1,0:T(8,128)(2,1)S(1)}, bf16[128,512]{1,0:T(8,128)(2,1)}, u32[]{:S(2)}) copy-start(bf16[128,512]{1,0:T(8,128)(2,1)} %refs_1_.8) | copy-start | bytes 393220
  113.3 14.5 %all-to-all-start.4 = ((bf16[32,32,128]{2,1,0:T(8,128)(2,1)}), bf16[32,32,128]{2,1,0:T(8,128)(2,1)S(1)}, u32[]{:S(2)}, u32[]{:S(2)}) async-start(bf16[32,32,128]{2,1,0:T(8,128)(2,1)} %bitcast.8), calls=%async_computation.4 | async-start | bytes 524288 | tf_op jit(solution)/shard_map/all_to_all | solution.py:339

commit v4 on v3

--- a/solution.py
+++ b/solution.py
@@ -1,3 +1,5 @@
+import itertools
+
 import jax
 import jax.numpy as jnp
 from jax import lax
@@ -16,12 +18,32 @@
 ROW = ("y", "z_lo")
 COL = ("x", "z_hi")
 SIZES = (4, 4, 4, 2, 2)
-PLANE = ("z_lo", "y") + COL
+AXES = ROW + COL + ("depth",)
+ORIGIN = {"z_lo": 2, "y": 3, "x": 3, "z_hi": 1, "depth": 0}
+PLANE = ("z_lo", "y", "x", "z_hi")
 FLAT = ("depth", "y", "x")
 UPRIGHT = ("z_lo", "z_hi")
 PARTS = 32
 PEERS = 8
 PART = CELLS // PARTS
+
+
+def groups(axes):
+    sizes = dict(zip(AXES, SIZES))
+    rest = [axis for axis in AXES if axis not in axes]
+    listed = []
+    for outer in itertools.product(*(range(sizes[axis]) for axis in rest)):
+        members = []
+        for inner in itertools.product(*(range(sizes[axis]) for axis in axes)):
+            place = dict(zip(rest, outer))
+            for axis, index in zip(axes, inner):
+                place[axis] = (index + ORIGIN[axis]) % sizes[axis]
+            member = 0
+            for axis in AXES:
+                member = member * sizes[axis] + place[axis]
+            members.append(member)
+        listed.append(members)
+    return listed
 
 
 def call(kernel, outs, *args, scratch=(), flops=2_000_000, spaces=None, fetched=(), hbm=(), hbm_outs=()):
@@ -336,7 +358,7 @@
 
 
 def exchange(value, axes=PLANE):
-    return lax.all_to_all(value, axes, 0, 0, tiled=True)
+    return lax.all_to_all(value, AXES, 0, 0, tiled=True, axis_index_groups=groups(axes))
 
 
 def per_device(
@@ -496,7 +518,7 @@
 
 
 def solution(mesh):
-    fine = Mesh(mesh.devices.reshape(SIZES), ROW + COL + ("depth",))
+    fine = Mesh(mesh.devices.reshape(SIZES), AXES)
     cells = P(ROW, COL + ("depth",), None)
     return jax.shard_map(
         per_device,

time: 152 us -> 147 us (0.967)
  waiting for transfers between devices: 31.9 us -> 19 us
  starting transfers between devices: 25.8 us -> 38.5 us
  blocking collectives: 75.5 us -> 70.7 us
    all_to_all x3, starting transfers between devices: 19.5 us -> 33.3 us  [exchange(): lax.all_to_all(value, AXES, 0, 0, tiled=True, axis_index_groups=groups(ax...]
    all_to_all x3, waiting for transfers between devices: 31.4 us -> 18.5 us  [exchange(): lax.all_to_all(value, AXES, 0, 0, tiled=True, axis_index_groups=groups(ax...]
    all_to_all x4, blocking collectives: 75.5 us -> 70.7 us  [exchange(): lax.all_to_all(value, AXES, 0, 0, tiled=True, axis_index_groups=groups(ax...]
where the time goes in v4:
time: 147 us
  blocking collectives  70.7 us (48%)
  starting transfers between devices  38.5 us (26%)
  waiting for transfers between devices  19 us (13%)
  Pallas kernels  17.8 us (12%)
    all_to_all x4, blocking collectives, exchange(): lax.all_to_all(value, AXES, 0, 0, tiled=True, axis_index_groups=groups(ax...  70.7 us
    all_to_all x3, starting transfers between devices, exchange(): lax.all_to_all(value, AXES, 0, 0, tiled=True, axis_index_groups=groups(ax...  33.3 us
    all_to_all x3, waiting for transfers between devices, exchange(): lax.all_to_all(value, AXES, 0, 0, tiled=True, axis_index_groups=groups(ax...  18.5 us
    pallas_call x14, Pallas kernels, call(): pl.pallas_call(body, out_shape=[pltpu.HBM(o.shape, o.dtype) if i in hbm_o...  17.8 us
    ppermute x2, starting transfers between devices, swap_cores(): return lax.ppermute(value, 'depth', [(0, 1), (1, 0)])  5.19 us
  transfers between devices with their start and end apart: 5, of which 5 were waited for; matrix products, arithmetic and copies ran while one was open for 0% of the time, Pallas kernels for 6%

profile of v4, /device:TPU:1, one launch (start us, length us, event | category | flops | bytes accessed | tf_op | source)
XLA Modules:
  0.0 146.8 jit_solution(12357110604291857800)
XLA Ops:
  0.6 1.9 %shard_map.145 = bf16[128,16,128]{2,1,0:T(8,128)(2,1)S(1)} custom-call(bf16[32,32,128]{2,1,0:T(8,128)(2,1)} %refs_1_.9, s32[32,32]{1,0:T(8,128)} %refs_2_.1, f32[1,128]{1,0:T(1,128)} %bitcast.18, f32[1,128]{1,0:T(1,128)} %bitcast.15, bf16[128,512]{1,0:T(8,128)(2,1)} %refs_1_.8), custom_call_target="tpu_custom_call" | custom-call | flops 2000000 | bytes 922624 | tf_op jit(solution)/shard_map/pallas_call | solution.py:86
  2.6 29.7 %all_to_all.35 = bf16[128,16,128]{2,1,0:T(8,128)(2,1)S(1)} all-to-all(bf16[128,16,128]{2,1,0:T(8,128)(2,1)S(1)} %shard_map.145), channel_id=1, replica_groups={{238,236,226,224,230,228,234,232,46,44,34,32,38,36,42,40,110,108,98,96,..., dimensions={0} | all-to-all | bytes 1048576 | tf_op jit(solution)/shard_map/all_to_all | solution.py:361
  32.2 0.9 shard_map.146
  33.1 2.0 %collective-permute-start = (bf16[128,8,128]{2,1,0:T(8,128)(2,1)S(1)}, bf16[128,8,128]{2,1,0:T(8,128)(2,1)S(1)}, u32[]{:S(2)}, u32[]{:S(2)}) collective-permute-start(bf16[128,8,128]{2,1,0:T(8,128)(2,1)S(1)} %get-tuple-element.30), channel_id=1, source_target_pairs={{0,1},{1,0},{2,3},{3,2},{4,5},{5,4},{6,7},{7,6},{8,9},{9,8},{10,11... | collective-permute-start | bytes 786440 | tf_op jit(solution)/shard_map/ppermute | solution.py:357
  35.1 1.0 shard_map.147
  36.1 0.2 collective-permute-done.refs_1_
  36.3 0.8 shard_map.148
  37.1 12.2 %all-to-all-start.1 = ((bf16[128,8,128]{2,1,0:T(8,128)(2,1)}), bf16[128,8,128]{2,1,0:T(8,128)(2,1)S(1)}, u32[]{:S(2)}, u32[]{:S(2)}) async-start(bf16[128,8,128]{2,1,0:T(8,128)(2,1)} %shard_map.148), calls=%async_computation.1 | async-start | bytes 524288 | tf_op jit(solution)/shard_map/all_to_all | solution.py:361
  49.3 1.8 %shard_map.149.refs_1_ = f32[128,1024]{1,0:T(8,128)S(1)} custom-call(bf16[32,32,128]{2,1,0:T(8,128)(2,1)} %refs_1_.9, bf16[32,32,128]{2,1,0:T(8,128)(2,1)} %refs_1_.7, f32[1,128]{1,0:T(1,128)} %bitcast.19, f32[1,128]{1,0:T(1,128)} %bitcast.16, f32[1,128]{1,0:T(1,128)} %bitcast.22, bf16[128,128]{1,0:T(8,128)(2,1)} %refs_8_.1, bf16[128,128]{1,0:T(8,128)(2,1)} %refs_9_.1), custom_call_target="tpu_custom_call" | custom-call | flops 500000000 | bytes 1115648 | tf_op jit(solution)/shard_map/pallas_call | solution.py:86
  51.1 5.7 %all-to-all-done.1.refs_0_.refs_10_ = bf16[128,8,128]{2,1,0:T(8,128)(2,1)S(1)} async-done(((bf16[128,8,128]{2,1,0:T(8,128)(2,1)}), bf16[128,8,128]{2,1,0:T(8,128)(2,1)S(1)}, u32[]{:S(2)}, u32[]{:S(2)}) %all-to-all-start.1) | async-done | bytes 262176 | tf_op jit(solution)/shard_map/all_to_all | solution.py:361
  56.7 0.5 shard_map.150
  57.3 18.2 %all_to_all.36.refs_1_ = bf16[128,8,128]{2,1,0:T(8,128)(2,1)S(1)} all-to-all(bf16[128,8,128]{2,1,0:T(8,128)(2,1)S(1)} %shard_map.150), channel_id=1, replica_groups={{238,236,226,224,230,228,234,232,46,44,34,32,38,36,42,40,110,108,98,96,..., dimensions={0} | all-to-all | bytes 524288 | tf_op jit(solution)/shard_map/all_to_all | solution.py:361
  75.5 3.2 %collective-permute-start.1 = (bf16[128,8,128]{2,1,0:T(8,128)(2,1)S(1)}, bf16[128,8,128]{2,1,0:T(8,128)(2,1)S(1)}, u32[]{:S(2)}, u32[]{:S(2)}) collective-permute-start(bf16[128,8,128]{2,1,0:T(8,128)(2,1)S(1)} %all_to_all.36.refs_1_), channel_id=1, source_target_pairs={{0,1},{1,0},{2,3},{3,2},{4,5},{5,4},{6,7},{7,6},{8,9},{9,8},{10,11... | collective-permute-start | bytes 786440 | tf_op jit(solution)/shard_map/ppermute | solution.py:357
  78.7 0.8 shard_map.151
  79.5 0.4 collective-permute-done.1.refs_1_
  79.8 1.6 %shard_map.152 = bf16[2,2,4,8,16,128]{5,4,3,2,1,0:T(8,128)(2,1)} custom-call(s32[1]{0:T(128)} %bitcast.2.refs_0_, bf16[128,8,128]{2,1,0:T(8,128)(2,1)S(1)} %collective-permute-done.1.refs_1_, bf16[512,256]{1,0:T(8,128)(2,1)S(1)} %get-tuple-element.28.refs_2_, bf16[2,2,128,256]{3,2,1,0:T(8,128)(2,1)S(1)} %bitcast.13, ...), custom_call_target="tpu_custom_call" | custom-call | flops 2000000 | bytes 1966084 | tf_op jit(solution)/shard_map/pallas_call | solution.py:86
  81.4 12.2 %all-to-all-start.3 = ((bf16[128,16,128]{2,1,0:T(8,128)(2,1)}), bf16[128,16,128]{2,1,0:T(8,128)(2,1)S(1)}, u32[]{:S(2)}, u32[]{:S(2)}) async-start(bf16[128,16,128]{2,1,0:T(8,128)(2,1)} %bitcast.6.refs_11_), calls=%async_computation.3 | async-start | bytes 1048576 | tf_op jit(solution)/shard_map/all_to_all | solution.py:361
  93.6 0.0 copy-start
  93.6 2.9 %shard_map.153 = (bf16[512,1024]{1,0:T(8,128)(2,1)S(1)}, bf16[128,1024]{1,0:T(8,128)(2,1)S(1)}, bf16[128,1024]{1,0:T(8,128)(2,1)S(1)}, f32[128,1024]{1,0:T(8,128)S(1)}, f32[384,128]{1,0:T(8,128)S(1)}) custom-call(bf16[32,32,128]{2,1,0:T(8,128)(2,1)} %refs_1_.9, bf16[32,32,128]{2,1,0:T(8,128)(2,1)} %refs_1_.7, s32[32,32]{1,0:T(8,128)} %refs_2_.1, ...), custom_call_target="tpu_custom_call" | custom-call | flops 500000000 | bytes 3807232 | tf_op jit(solution)/shard_map/pallas_call | solution.py:86
  96.6 10.2 %all-to-all-done.3.refs_0_ = bf16[128,16,128]{2,1,0:T(8,128)(2,1)S(1)} async-done(((bf16[128,16,128]{2,1,0:T(8,128)(2,1)}), bf16[128,16,128]{2,1,0:T(8,128)(2,1)S(1)}, u32[]{:S(2)}, u32[]{:S(2)}) %all-to-all-start.3) | async-done | bytes 524320 | tf_op jit(solution)/shard_map/all_to_all | solution.py:361
  106.8 0.0 copy-done
  106.8 2.4 %shard_map.154 = (bf16[128,8,128]{2,1,0:T(8,128)(2,1)}, f32[128,1024]{1,0:T(8,128)}) custom-call(bf16[128,16,128]{2,1,0:T(8,128)(2,1)S(1)} %all-to-all-done.3.refs_0_, bf16[128,512]{1,0:T(8,128)(2,1)S(1)} %copy-done, bf16[512,1024]{1,0:T(8,128)(2,1)S(1)} %get-tuple-element.34.refs_2_, bf16[128,1024]{1,0:T(8,128)(2,1)S(1)} %get-tuple-element.35.refs_3_, ...), custom_call_target="tpu_custom_call" | custom-call | flops 2000000 | bytes 3735552 | tf_op jit(solution)/shard_map/pallas_call | solution.py:86
  109.2 8.9 %all-to-all-start.4 = ((bf16[32,32,128]{2,1,0:T(8,128)(2,1)}), bf16[32,32,128]{2,1,0:T(8,128)(2,1)S(1)}, u32[]{:S(2)}, u32[]{:S(2)}) async-start(bf16[32,32,128]{2,1,0:T(8,128)(2,1)} %bitcast.8), calls=%async_computation.4 | async-start | bytes 524288 | tf_op jit(solution)/shard_map/all_to_all | solution.py:361
  118.1 2.4 %shard_map.155.refs_1_ = bf16[32,32,128]{2,1,0:T(8,128)(2,1)} custom-call(f32[128,1024]{1,0:T(8,128)} %get-tuple-element.39.refs_0_, bf16[32,32,128]{2,1,0:T(8,128)(2,1)} %refs_1_.9, f32[1,128]{1,0:T(1,128)} %bitcast.21), custom_call_target="tpu_custom_call" | custom-call | flops 500000000 | bytes 1049088 | tf_op jit(solution)/shard_map/pallas_call | solution.py:86
  120.4 2.6 %all-to-all-done.4.refs_0_ = bf16[32,32,128]{2,1,0:T(8,128)(2,1)S(1)} async-done(((bf16[32,32,128]{2,1,0:T(8,128)(2,1)}), bf16[32,32,128]{2,1,0:T(8,128)(2,1)S(1)}, u32[]{:S(2)}, u32[]{:S(2)}) %all-to-all-start.4) | async-done | bytes 262176 | tf_op jit(solution)/shard_map/all_to_all | solution.py:361
  123.1 9.2 %all_to_all.37.refs_0_ = bf16[8,32,128]{2,1,0:T(8,128)(2,1)S(1)} all-to-all(bf16[8,32,128]{2,1,0:T(8,128)(2,1)S(1)} %shard_map.156), channel_id=1, replica_groups={{34,32,50,48,2,0,18,16},{35,33,51,49,3,1,19,17},{38,36,54,52,6,4,22,20}..., dimensions={0} | all-to-all | bytes 131072 | tf_op jit(solution)/shard_map/all_to_all | solution.py:361
  132.3 13.6 %all_to_all.38 = bf16[32,32,128]{2,1,0:T(8,128)(2,1)S(1)} all-to-all(bf16[32,32,128]{2,1,0:T(8,128)(2,1)S(1)} %shard_map.157), channel_id=1, replica_groups={{204,192,196,200,12,0,4,8,76,64,68,72,140,128,132,136,205,193,197,201,1..., dimensions={0} | all-to-all | bytes 524288 | tf_op jit(solution)/shard_map/all_to_all | solution.py:361
  145.9 0.8 shard_map.158
  (2 shorter events, 0.1 us)
Async XLA Ops:
  33.1 3.2 %collective-permute-start = (bf16[128,8,128]{2,1,0:T(8,128)(2,1)S(1)}, bf16[128,8,128]{2,1,0:T(8,128)(2,1)S(1)}, u32[]{:S(2)}, u32[]{:S(2)}) collective-permute-start(bf16[128,8,128]{2,1,0:T(8,128)(2,1)S(1)} %get-tuple-element.30), channel_id=1, source_target_pairs={{0,1},{1,0},{2,3},{3,2},{4,5},{5,4},{6,7},{7,6},{8,9},{9,8},{10,11... | collective-permute-start | bytes 786440 | tf_op jit(solution)/shard_map/ppermute | solution.py:357
  37.1 19.7 %all-to-all-start.1 = ((bf16[128,8,128]{2,1,0:T(8,128)(2,1)}), bf16[128,8,128]{2,1,0:T(8,128)(2,1)S(1)}, u32[]{:S(2)}, u32[]{:S(2)}) async-start(bf16[128,8,128]{2,1,0:T(8,128)(2,1)} %shard_map.148), calls=%async_computation.1 | async-start | bytes 524288 | tf_op jit(solution)/shard_map/all_to_all | solution.py:361
  75.5 4.3 %collective-permute-start.1 = (bf16[128,8,128]{2,1,0:T(8,128)(2,1)S(1)}, bf16[128,8,128]{2,1,0:T(8,128)(2,1)S(1)}, u32[]{:S(2)}, u32[]{:S(2)}) collective-permute-start(bf16[128,8,128]{2,1,0:T(8,128)(2,1)S(1)} %all_to_all.36.refs_1_), channel_id=1, source_target_pairs={{0,1},{1,0},{2,3},{3,2},{4,5},{5,4},{6,7},{7,6},{8,9},{9,8},{10,11... | collective-permute-start | bytes 786440 | tf_op jit(solution)/shard_map/ppermute | solution.py:357
  81.4 25.4 %all-to-all-start.3 = ((bf16[128,16,128]{2,1,0:T(8,128)(2,1)}), bf16[128,16,128]{2,1,0:T(8,128)(2,1)S(1)}, u32[]{:S(2)}, u32[]{:S(2)}) async-start(bf16[128,16,128]{2,1,0:T(8,128)(2,1)} %bitcast.6.refs_11_), calls=%async_computation.3 | async-start | bytes 1048576 | tf_op jit(solution)/shard_map/all_to_all | solution.py:361
  93.6 13.2 %copy-start = (bf16[128,512]{1,0:T(8,128)(2,1)S(1)}, bf16[128,512]{1,0:T(8,128)(2,1)}, u32[]{:S(2)}) copy-start(bf16[128,512]{1,0:T(8,128)(2,1)} %refs_1_.8) | copy-start | bytes 393220
  109.2 13.8 %all-to-all-start.4 = ((bf16[32,32,128]{2,1,0:T(8,128)(2,1)}), bf16[32,32,128]{2,1,0:T(8,128)(2,1)S(1)}, u32[]{:S(2)}, u32[]{:S(2)}) async-start(bf16[32,32,128]{2,1,0:T(8,128)(2,1)} %bitcast.8), calls=%async_computation.4 | async-start | bytes 524288 | tf_op jit(solution)/shard_map/all_to_all | solution.py:361

commit v5 on v4

--- a/solution.py
+++ b/solution.py
@@ -19,10 +19,10 @@
 COL = ("x", "z_hi")
 SIZES = (4, 4, 4, 2, 2)
 AXES = ROW + COL + ("depth",)
-ORIGIN = {"z_lo": 2, "y": 3, "x": 3, "z_hi": 1, "depth": 0}
 PLANE = ("z_lo", "y", "x", "z_hi")
 FLAT = ("depth", "y", "x")
 UPRIGHT = ("z_lo", "z_hi")
+ORIGINS = {PLANE: (2, 2, 2, 1, 0), FLAT: (2, 0, 2, 0, 1), UPRIGHT: (0, 0, 0, 1, 0)}
 PARTS = 32
 PEERS = 8
 PART = CELLS // PARTS
@@ -30,6 +30,7 @@
 
 def groups(axes):
     sizes = dict(zip(AXES, SIZES))
+    origin = dict(zip(AXES, ORIGINS[axes]))
     rest = [axis for axis in AXES if axis not in axes]
     listed = []
     for outer in itertools.product(*(range(sizes[axis]) for axis in rest)):
@@ -37,7 +38,7 @@
         for inner in itertools.product(*(range(sizes[axis]) for axis in axes)):
             place = dict(zip(rest, outer))
             for axis, index in zip(axes, inner):
-                place[axis] = (index + ORIGIN[axis]) % sizes[axis]
+                place[axis] = (index + origin[axis]) % sizes[axis]
             member = 0
             for axis in AXES:
                 member = member * sizes[axis] + place[axis]

time: 147 us -> 145 us (0.986)
  waiting for transfers between devices: 19 us -> 16.4 us
  starting transfers between devices: 38.5 us -> 40.2 us
    all_to_all x3, waiting for transfers between devices: 18.5 us -> 15.8 us  [exchange(): lax.all_to_all(value, AXES, 0, 0, tiled=True, axis_index_groups=groups(ax...]
    all_to_all x3, starting transfers between devices: 33.3 us -> 35.4 us  [exchange(): lax.all_to_all(value, AXES, 0, 0, tiled=True, axis_index_groups=groups(ax...]
where the time goes in v5:
time: 145 us
  blocking collectives  69.6 us (48%)
  starting transfers between devices  40.2 us (28%)
  Pallas kernels  17.8 us (12%)
  waiting for transfers between devices  16.4 us (11%)
    all_to_all x4, blocking collectives, exchange(): lax.all_to_all(value, AXES, 0, 0, tiled=True, axis_index_groups=groups(ax...  69.6 us
    all_to_all x3, starting transfers between devices, exchange(): lax.all_to_all(value, AXES, 0, 0, tiled=True, axis_index_groups=groups(ax...  35.4 us
    pallas_call x14, Pallas kernels, call(): pl.pallas_call(body, out_shape=[pltpu.HBM(o.shape, o.dtype) if i in hbm_o...  17.8 us
    all_to_all x3, waiting for transfers between devices, exchange(): lax.all_to_all(value, AXES, 0, 0, tiled=True, axis_index_groups=groups(ax...  15.8 us
    ppermute x2, starting transfers between devices, swap_cores(): return lax.ppermute(value, 'depth', [(0, 1), (1, 0)])  4.81 us
  transfers between devices with their start and end apart: 5, of which 5 were waited for; matrix products, arithmetic and copies ran while one was open for 0% of the time, Pallas kernels for 6%

profile of v5, /device:TPU:1, one launch (start us, length us, event | category | flops | bytes accessed | tf_op | source)
XLA Modules:
  0.0 144.7 jit_solution(7578686225684700508)
XLA Ops:
  0.6 1.9 %shard_map.145 = bf16[128,16,128]{2,1,0:T(8,128)(2,1)S(1)} custom-call(bf16[32,32,128]{2,1,0:T(8,128)(2,1)} %refs_1_.9, s32[32,32]{1,0:T(8,128)} %refs_2_.1, f32[1,128]{1,0:T(1,128)} %bitcast.18, f32[1,128]{1,0:T(1,128)} %bitcast.15, bf16[128,512]{1,0:T(8,128)(2,1)} %refs_1_.8), custom_call_target="tpu_custom_call" | custom-call | flops 2000000 | bytes 922624 | tf_op jit(solution)/shard_map/pallas_call | solution.py:87
  2.6 29.1 %all_to_all.35 = bf16[128,16,128]{2,1,0:T(8,128)(2,1)S(1)} all-to-all(bf16[128,16,128]{2,1,0:T(8,128)(2,1)S(1)} %shard_map.145), channel_id=1, replica_groups={{170,168,174,172,162,160,166,164,234,232,238,236,226,224,230,228,42,40,..., dimensions={0} | all-to-all | bytes 1048576 | tf_op jit(solution)/shard_map/all_to_all | solution.py:362
  31.7 0.9 shard_map.146
  32.6 2.1 %collective-permute-start = (bf16[128,8,128]{2,1,0:T(8,128)(2,1)S(1)}, bf16[128,8,128]{2,1,0:T(8,128)(2,1)S(1)}, u32[]{:S(2)}, u32[]{:S(2)}) collective-permute-start(bf16[128,8,128]{2,1,0:T(8,128)(2,1)S(1)} %get-tuple-element.30), channel_id=1, source_target_pairs={{0,1},{1,0},{2,3},{3,2},{4,5},{5,4},{6,7},{7,6},{8,9},{9,8},{10,11... | collective-permute-start | bytes 786440 | tf_op jit(solution)/shard_map/ppermute | solution.py:358
  34.7 1.0 shard_map.147
  35.6 0.2 collective-permute-done.refs_1_
  35.8 0.8 shard_map.148
  36.6 13.0 %all-to-all-start.1 = ((bf16[128,8,128]{2,1,0:T(8,128)(2,1)}), bf16[128,8,128]{2,1,0:T(8,128)(2,1)S(1)}, u32[]{:S(2)}, u32[]{:S(2)}) async-start(bf16[128,8,128]{2,1,0:T(8,128)(2,1)} %shard_map.148), calls=%async_computation.1 | async-start | bytes 524288 | tf_op jit(solution)/shard_map/all_to_all | solution.py:362
  49.6 1.8 %shard_map.149.refs_1_ = f32[128,1024]{1,0:T(8,128)S(1)} custom-call(bf16[32,32,128]{2,1,0:T(8,128)(2,1)} %refs_1_.9, bf16[32,32,128]{2,1,0:T(8,128)(2,1)} %refs_1_.7, f32[1,128]{1,0:T(1,128)} %bitcast.19, f32[1,128]{1,0:T(1,128)} %bitcast.16, f32[1,128]{1,0:T(1,128)} %bitcast.22, bf16[128,128]{1,0:T(8,128)(2,1)} %refs_8_.1, bf16[128,128]{1,0:T(8,128)(2,1)} %refs_9_.1), custom_call_target="tpu_custom_call" | custom-call | flops 500000000 | bytes 1115648 | tf_op jit(solution)/shard_map/pallas_call | solution.py:87
  51.4 4.7 %all-to-all-done.1.refs_0_.refs_10_ = bf16[128,8,128]{2,1,0:T(8,128)(2,1)S(1)} async-done(((bf16[128,8,128]{2,1,0:T(8,128)(2,1)}), bf16[128,8,128]{2,1,0:T(8,128)(2,1)S(1)}, u32[]{:S(2)}, u32[]{:S(2)}) %all-to-all-start.1) | async-done | bytes 262176 | tf_op jit(solution)/shard_map/all_to_all | solution.py:362
  56.1 0.5 shard_map.150
  56.6 18.8 %all_to_all.36.refs_1_ = bf16[128,8,128]{2,1,0:T(8,128)(2,1)S(1)} all-to-all(bf16[128,8,128]{2,1,0:T(8,128)(2,1)S(1)} %shard_map.150), channel_id=1, replica_groups={{170,168,174,172,162,160,166,164,234,232,238,236,226,224,230,228,42,40,..., dimensions={0} | all-to-all | bytes 524288 | tf_op jit(solution)/shard_map/all_to_all | solution.py:362
  75.4 2.7 %collective-permute-start.1 = (bf16[128,8,128]{2,1,0:T(8,128)(2,1)S(1)}, bf16[128,8,128]{2,1,0:T(8,128)(2,1)S(1)}, u32[]{:S(2)}, u32[]{:S(2)}) collective-permute-start(bf16[128,8,128]{2,1,0:T(8,128)(2,1)S(1)} %all_to_all.36.refs_1_), channel_id=1, source_target_pairs={{0,1},{1,0},{2,3},{3,2},{4,5},{5,4},{6,7},{7,6},{8,9},{9,8},{10,11... | collective-permute-start | bytes 786440 | tf_op jit(solution)/shard_map/ppermute | solution.py:358
  78.1 0.8 shard_map.151
  78.9 0.4 collective-permute-done.1.refs_1_
  79.3 1.6 %shard_map.152 = bf16[2,2,4,8,16,128]{5,4,3,2,1,0:T(8,128)(2,1)} custom-call(s32[1]{0:T(128)} %bitcast.2.refs_0_, bf16[128,8,128]{2,1,0:T(8,128)(2,1)S(1)} %collective-permute-done.1.refs_1_, bf16[512,256]{1,0:T(8,128)(2,1)S(1)} %get-tuple-element.28.refs_2_, bf16[2,2,128,256]{3,2,1,0:T(8,128)(2,1)S(1)} %bitcast.13, ...), custom_call_target="tpu_custom_call" | custom-call | flops 2000000 | bytes 1966084 | tf_op jit(solution)/shard_map/pallas_call | solution.py:87
  80.9 13.3 %all-to-all-start.3 = ((bf16[128,16,128]{2,1,0:T(8,128)(2,1)}), bf16[128,16,128]{2,1,0:T(8,128)(2,1)S(1)}, u32[]{:S(2)}, u32[]{:S(2)}) async-start(bf16[128,16,128]{2,1,0:T(8,128)(2,1)} %bitcast.6.refs_11_), calls=%async_computation.3 | async-start | bytes 1048576 | tf_op jit(solution)/shard_map/all_to_all | solution.py:362
  94.2 0.0 copy-start
  94.2 2.9 %shard_map.153 = (bf16[512,1024]{1,0:T(8,128)(2,1)S(1)}, bf16[128,1024]{1,0:T(8,128)(2,1)S(1)}, bf16[128,1024]{1,0:T(8,128)(2,1)S(1)}, f32[128,1024]{1,0:T(8,128)S(1)}, f32[384,128]{1,0:T(8,128)S(1)}) custom-call(bf16[32,32,128]{2,1,0:T(8,128)(2,1)} %refs_1_.9, bf16[32,32,128]{2,1,0:T(8,128)(2,1)} %refs_1_.7, s32[32,32]{1,0:T(8,128)} %refs_2_.1, ...), custom_call_target="tpu_custom_call" | custom-call | flops 500000000 | bytes 3807232 | tf_op jit(solution)/shard_map/pallas_call | solution.py:87
  97.1 9.3 %all-to-all-done.3.refs_0_ = bf16[128,16,128]{2,1,0:T(8,128)(2,1)S(1)} async-done(((bf16[128,16,128]{2,1,0:T(8,128)(2,1)}), bf16[128,16,128]{2,1,0:T(8,128)(2,1)S(1)}, u32[]{:S(2)}, u32[]{:S(2)}) %all-to-all-start.3) | async-done | bytes 524320 | tf_op jit(solution)/shard_map/all_to_all | solution.py:362
  106.5 0.0 copy-done
  106.5 2.4 %shard_map.154 = (bf16[128,8,128]{2,1,0:T(8,128)(2,1)}, f32[128,1024]{1,0:T(8,128)}) custom-call(bf16[128,16,128]{2,1,0:T(8,128)(2,1)S(1)} %all-to-all-done.3.refs_0_, bf16[128,512]{1,0:T(8,128)(2,1)S(1)} %copy-done, bf16[512,1024]{1,0:T(8,128)(2,1)S(1)} %get-tuple-element.34.refs_2_, bf16[128,1024]{1,0:T(8,128)(2,1)S(1)} %get-tuple-element.35.refs_3_, ...), custom_call_target="tpu_custom_call" | custom-call | flops 2000000 | bytes 3735552 | tf_op jit(solution)/shard_map/pallas_call | solution.py:87
  108.8 9.0 %all-to-all-start.4 = ((bf16[32,32,128]{2,1,0:T(8,128)(2,1)}), bf16[32,32,128]{2,1,0:T(8,128)(2,1)S(1)}, u32[]{:S(2)}, u32[]{:S(2)}) async-start(bf16[32,32,128]{2,1,0:T(8,128)(2,1)} %bitcast.8), calls=%async_computation.4 | async-start | bytes 524288 | tf_op jit(solution)/shard_map/all_to_all | solution.py:362
  117.9 2.4 %shard_map.155.refs_1_ = bf16[32,32,128]{2,1,0:T(8,128)(2,1)} custom-call(f32[128,1024]{1,0:T(8,128)} %get-tuple-element.39.refs_0_, bf16[32,32,128]{2,1,0:T(8,128)(2,1)} %refs_1_.9, f32[1,128]{1,0:T(1,128)} %bitcast.21), custom_call_target="tpu_custom_call" | custom-call | flops 500000000 | bytes 1049088 | tf_op jit(solution)/shard_map/pallas_call | solution.py:87
  120.3 1.8 %all-to-all-done.4.refs_0_ = bf16[32,32,128]{2,1,0:T(8,128)(2,1)S(1)} async-done(((bf16[32,32,128]{2,1,0:T(8,128)(2,1)}), bf16[32,32,128]{2,1,0:T(8,128)(2,1)S(1)}, u32[]{:S(2)}, u32[]{:S(2)}) %all-to-all-start.4) | async-done | bytes 262176 | tf_op jit(solution)/shard_map/all_to_all | solution.py:362
  122.1 8.8 %all_to_all.37.refs_0_ = bf16[8,32,128]{2,1,0:T(8,128)(2,1)S(1)} all-to-all(bf16[8,32,128]{2,1,0:T(8,128)(2,1)S(1)} %shard_map.156), channel_id=1, replica_groups={{2,0,18,16,34,32,50,48},{3,1,19,17,35,33,51,49},{6,4,22,20,38,36,54,52}..., dimensions={0} | all-to-all | bytes 131072 | tf_op jit(solution)/shard_map/all_to_all | solution.py:362
  130.9 13.0 %all_to_all.38 = bf16[32,32,128]{2,1,0:T(8,128)(2,1)S(1)} all-to-all(bf16[32,32,128]{2,1,0:T(8,128)(2,1)S(1)} %shard_map.157), channel_id=1, replica_groups={{137,141,129,133,201,205,193,197,9,13,1,5,73,77,65,69,136,140,128,132,2..., dimensions={0} | all-to-all | bytes 524288 | tf_op jit(solution)/shard_map/all_to_all | solution.py:362
  143.9 0.8 shard_map.158
  (2 shorter events, 0.1 us)
Async XLA Ops:
  32.6 3.3 %collective-permute-start = (bf16[128,8,128]{2,1,0:T(8,128)(2,1)S(1)}, bf16[128,8,128]{2,1,0:T(8,128)(2,1)S(1)}, u32[]{:S(2)}, u32[]{:S(2)}) collective-permute-start(bf16[128,8,128]{2,1,0:T(8,128)(2,1)S(1)} %get-tuple-element.30), channel_id=1, source_target_pairs={{0,1},{1,0},{2,3},{3,2},{4,5},{5,4},{6,7},{7,6},{8,9},{9,8},{10,11... | collective-permute-start | bytes 786440 | tf_op jit(solution)/shard_map/ppermute | solution.py:358
  36.6 19.5 %all-to-all-start.1 = ((bf16[128,8,128]{2,1,0:T(8,128)(2,1)}), bf16[128,8,128]{2,1,0:T(8,128)(2,1)S(1)}, u32[]{:S(2)}, u32[]{:S(2)}) async-start(bf16[128,8,128]{2,1,0:T(8,128)(2,1)} %shard_map.148), calls=%async_computation.1 | async-start | bytes 524288 | tf_op jit(solution)/shard_map/all_to_all | solution.py:362
  75.4 3.9 %collective-permute-start.1 = (bf16[128,8,128]{2,1,0:T(8,128)(2,1)S(1)}, bf16[128,8,128]{2,1,0:T(8,128)(2,1)S(1)}, u32[]{:S(2)}, u32[]{:S(2)}) collective-permute-start(bf16[128,8,128]{2,1,0:T(8,128)(2,1)S(1)} %all_to_all.36.refs_1_), channel_id=1, source_target_pairs={{0,1},{1,0},{2,3},{3,2},{4,5},{5,4},{6,7},{7,6},{8,9},{9,8},{10,11... | collective-permute-start | bytes 786440 | tf_op jit(solution)/shard_map/ppermute | solution.py:358
  80.9 25.6 %all-to-all-start.3 = ((bf16[128,16,128]{2,1,0:T(8,128)(2,1)}), bf16[128,16,128]{2,1,0:T(8,128)(2,1)S(1)}, u32[]{:S(2)}, u32[]{:S(2)}) async-start(bf16[128,16,128]{2,1,0:T(8,128)(2,1)} %bitcast.6.refs_11_), calls=%async_computation.3 | async-start | bytes 1048576 | tf_op jit(solution)/shard_map/all_to_all | solution.py:362
  94.2 12.3 %copy-start = (bf16[128,512]{1,0:T(8,128)(2,1)S(1)}, bf16[128,512]{1,0:T(8,128)(2,1)}, u32[]{:S(2)}) copy-start(bf16[128,512]{1,0:T(8,128)(2,1)} %refs_1_.8) | copy-start | bytes 393220
  108.8 13.2 %all-to-all-start.4 = ((bf16[32,32,128]{2,1,0:T(8,128)(2,1)}), bf16[32,32,128]{2,1,0:T(8,128)(2,1)S(1)}, u32[]{:S(2)}, u32[]{:S(2)}) async-start(bf16[32,32,128]{2,1,0:T(8,128)(2,1)} %bitcast.8), calls=%async_computation.4 | async-start | bytes 524288 | tf_op jit(solution)/shard_map/all_to_all | solution.py:362

commit v6 on v5

--- a/solution.py
+++ b/solution.py
@@ -192,23 +192,21 @@
     return sides
 
 
-def factors_kernel(pair, mask, gain, bias, in_proj, send, scratch):
+def factors_kernel(
+    pair, grad_out, mask, gain, bias, x_gain, in_proj, w_gate, w_out, send, tangent, scratch
+):
     normed = normalise(pair, gain, bias)[2]
     for side, (_, factor, _) in enumerate(factors_of(normed, mask, in_proj)):
         to_tiles(factor, scratch, side * SUB, 2 * SUB)
     send[...] = scratch[...].reshape(CH, 2 * SUB, CH).astype(BF16)
+    d_out_proj, _ = gated_grad(grad_out, normed, w_gate)
+    tangent[...] = dot(w_out[...], d_out_proj, 1, 0) * column(x_gain[...])
 
 
 def gated_grad(grad_out, normed, w_gate):
     gate = jax.nn.sigmoid(dot(w_gate[...], normed, 0, 0))
     moved = channel_major(grad_out) * gate
     return moved.astype(BF16), moved * (1.0 - gate)
-
-
-def tangent_kernel(pair, grad_out, gain, bias, x_gain, w_gate, w_out, tangent):
-    normed = normalise(pair, gain, bias)[2]
-    d_out_proj, _ = gated_grad(grad_out, normed, w_gate)
-    tangent[...] = dot(w_out[...], d_out_proj, 1, 0) * column(x_gain[...])
 
 
 def product_theirs_kernel(parity, own, left_out, theirs):
@@ -338,7 +336,8 @@
             out[SUB * g + s] = block[g * T : (g + 1) * T]
 
 
-def total_kernel(recv, after, send):
+def total_kernel(recv, *refs):
+    send = refs[-1]
     total = jnp.sum(recv[...].astype(F32), axis=0, keepdims=True)
     send[...] = jnp.broadcast_to(total, send.shape).astype(BF16)
 
@@ -388,16 +387,20 @@
     tiles = pltpu.VMEM((CELLS, CH), F32)
     pairs_of_tiles = pltpu.VMEM((2 * CELLS, CH), F32)
 
-    (factors,) = call(
+    factors, tangent = call(
         factors_kernel,
-        [two],
+        [two, wide],
         pair,
+        grad_out,
         pair_mask,
         in_gain,
         in_bias,
+        x_gain,
         in_proj,
+        w_gate,
+        w_out,
         scratch=[pairs_of_tiles],
-        fetched=range(5),
+        fetched=range(9),
     )
     factors, parity = lax.optimization_barrier((factors, parity))
     factors = exchange(factors).reshape(2, 2, 4, 8, 2 * SUB, CH)
@@ -416,19 +419,6 @@
     right = right.reshape(2, 2, 4 * T, 2 * CH)
     (x_send,) = call(product_kernel, [one], x_mine, x_got)
     x_recv = exchange(x_send)
-    (tangent,) = call(
-        tangent_kernel,
-        [wide],
-        pair,
-        grad_out,
-        in_gain,
-        in_bias,
-        x_gain,
-        w_gate,
-        w_out,
-        flops=500_000_000,
-        fetched=range(7),
-    )
     (dx_send,) = call(inner_kernel, [one], x_recv, tangent, scratch=[tiles])
     dx = exchange(dx_send)
     da, db = call(
@@ -502,7 +492,7 @@
         fetched=range(3),
     )
     (totals,) = call(
-        total_kernel, [struct((PEERS, PART, CH), BF16)], weights, grad_pair, hbm=(1,)
+        total_kernel, [struct((PEERS, PART, CH), BF16)], weights
     )
     totals = exchange(totals, UPRIGHT)
     (totals,) = call(

time: 145 us -> 144 us (level)
  blocking collectives: 69.6 us -> 92.8 us
  starting transfers between devices: 40.2 us -> 24.9 us
  waiting for transfers between devices: 16.4 us -> 9.91 us
  Pallas kernels: 17.8 us -> 15.7 us
    all_to_all x4 -> x5, blocking collectives: 69.6 us -> 92.8 us  [exchange(): lax.all_to_all(value, AXES, 0, 0, tiled=True, axis_index_groups=groups(ax...]
    all_to_all x3 -> x2, starting transfers between devices: 35.4 us -> 20 us  [exchange(): lax.all_to_all(value, AXES, 0, 0, tiled=True, axis_index_groups=groups(ax...]
    all_to_all x3 -> x2, waiting for transfers between devices: 15.8 us -> 9.36 us  [exchange(): lax.all_to_all(value, AXES, 0, 0, tiled=True, axis_index_groups=groups(ax...]
    pallas_call x14 -> x13, Pallas kernels: 17.8 us -> 15.7 us  [call(): pl.pallas_call(body, out_shape=[pltpu.HBM(o.shape, o.dtype) if i in hbm_o...]
  transfers between devices with their start and end apart: 5 -> 4, of which waited for: 5 -> 3; matrix products, arithmetic and copies ran while one was open for 0% -> 0% of each run, Pallas kernels for 6% -> 5%
where the time goes in v6:
time: 144 us
  blocking collectives  92.8 us (64%)
  starting transfers between devices  24.9 us (17%)
  Pallas kernels  15.7 us (11%)
  waiting for transfers between devices  9.91 us (7%)
    all_to_all x5, blocking collectives, exchange(): lax.all_to_all(value, AXES, 0, 0, tiled=True, axis_index_groups=groups(ax...  92.8 us
    all_to_all x2, starting transfers between devices, exchange(): lax.all_to_all(value, AXES, 0, 0, tiled=True, axis_index_groups=groups(ax...  20 us
    pallas_call x13, Pallas kernels, call(): pl.pallas_call(body, out_shape=[pltpu.HBM(o.shape, o.dtype) if i in hbm_o...  15.7 us
    all_to_all x2, waiting for transfers between devices, exchange(): lax.all_to_all(value, AXES, 0, 0, tiled=True, axis_index_groups=groups(ax...  9.36 us
    ppermute x2, starting transfers between devices, swap_cores(): return lax.ppermute(value, 'depth', [(0, 1), (1, 0)])  4.9 us
  transfers between devices with their start and end apart: 4, of which 3 were waited for; matrix products, arithmetic and copies ran while one was open for 0% of the time, Pallas kernels for 5%

profile of v6, /device:TPU:1, one launch (start us, length us, event | category | flops | bytes accessed | tf_op | source)
XLA Modules:
  0.0 144.0 jit_solution(116757761576977523)
XLA Ops:
  0.6 2.4 %shard_map.145 = (bf16[128,16,128]{2,1,0:T(8,128)(2,1)S(1)}, f32[128,1024]{1,0:T(8,128)S(1)}) custom-call(bf16[32,32,128]{2,1,0:T(8,128)(2,1)} %refs_1_.7, bf16[32,32,128]{2,1,0:T(8,128)(2,1)} %refs_1_.5, s32[32,32]{1,0:T(8,128)} %refs_2_.3, f32[1,128]{1,0:T(1,128)} %bitcast.20, f32[1,128]{1,0:T(1,128)} %bitcast.16, f32[1,128]{1,0:T(1,128)} %bitcast.18, ...), custom_call_target="tpu_custom_call" | custom-call | flops 2000000 | bytes 1775104 | tf_op jit(solution)/shard_map/pallas_call | solution.py:87
  3.1 29.1 %all_to_all.35 = bf16[128,16,128]{2,1,0:T(8,128)(2,1)S(1)} all-to-all(bf16[128,16,128]{2,1,0:T(8,128)(2,1)S(1)} %get-tuple-element.30), channel_id=1, replica_groups={{170,168,174,172,162,160,166,164,234,232,238,236,226,224,230,228,42,40,..., dimensions={0} | all-to-all | bytes 1048576 | tf_op jit(solution)/shard_map/all_to_all | solution.py:361
  32.2 0.9 shard_map.146
  33.0 2.1 %collective-permute-start = (bf16[128,8,128]{2,1,0:T(8,128)(2,1)S(1)}, bf16[128,8,128]{2,1,0:T(8,128)(2,1)S(1)}, u32[]{:S(2)}, u32[]{:S(2)}) collective-permute-start(bf16[128,8,128]{2,1,0:T(8,128)(2,1)S(1)} %get-tuple-element.33), channel_id=1, source_target_pairs={{0,1},{1,0},{2,3},{3,2},{4,5},{5,4},{6,7},{7,6},{8,9},{9,8},{10,11... | collective-permute-start | bytes 786440 | tf_op jit(solution)/shard_map/ppermute | solution.py:357
  35.1 1.0 shard_map.147
  36.1 0.2 collective-permute-done.refs_1_
  36.3 0.1 shard_map.148
  36.4 19.2 %all_to_all.36.refs_0_.refs_10_ = bf16[128,8,128]{2,1,0:T(8,128)(2,1)S(1)} all-to-all(bf16[128,8,128]{2,1,0:T(8,128)(2,1)S(1)} %shard_map.148), channel_id=1, replica_groups={{170,168,174,172,162,160,166,164,234,232,238,236,226,224,230,228,42,40,..., dimensions={0} | all-to-all | bytes 524288 | tf_op jit(solution)/shard_map/all_to_all | solution.py:361
  55.6 0.5 shard_map.149
  56.1 18.7 %all_to_all.37.refs_1_ = bf16[128,8,128]{2,1,0:T(8,128)(2,1)S(1)} all-to-all(bf16[128,8,128]{2,1,0:T(8,128)(2,1)S(1)} %shard_map.149), channel_id=1, replica_groups={{170,168,174,172,162,160,166,164,234,232,238,236,226,224,230,228,42,40,..., dimensions={0} | all-to-all | bytes 524288 | tf_op jit(solution)/shard_map/all_to_all | solution.py:361
  74.9 2.8 %collective-permute-start.1 = (bf16[128,8,128]{2,1,0:T(8,128)(2,1)S(1)}, bf16[128,8,128]{2,1,0:T(8,128)(2,1)S(1)}, u32[]{:S(2)}, u32[]{:S(2)}) collective-permute-start(bf16[128,8,128]{2,1,0:T(8,128)(2,1)S(1)} %all_to_all.37.refs_1_), channel_id=1, source_target_pairs={{0,1},{1,0},{2,3},{3,2},{4,5},{5,4},{6,7},{7,6},{8,9},{9,8},{10,11... | collective-permute-start | bytes 786440 | tf_op jit(solution)/shard_map/ppermute | solution.py:357
  77.7 0.8 shard_map.150
  78.5 0.4 collective-permute-done.1.refs_1_
  78.8 1.6 %shard_map.151 = bf16[2,2,4,8,16,128]{5,4,3,2,1,0:T(8,128)(2,1)} custom-call(s32[1]{0:T(128)} %bitcast.3.refs_0_, bf16[128,8,128]{2,1,0:T(8,128)(2,1)S(1)} %collective-permute-done.1.refs_1_, bf16[512,256]{1,0:T(8,128)(2,1)S(1)} %get-tuple-element.31.refs_2_, bf16[2,2,128,256]{3,2,1,0:T(8,128)(2,1)S(1)} %bitcast.13, ...), custom_call_target="tpu_custom_call" | custom-call | flops 2000000 | bytes 1966084 | tf_op jit(solution)/shard_map/pallas_call | solution.py:87
  80.4 13.1 %all-to-all-start.3 = ((bf16[128,16,128]{2,1,0:T(8,128)(2,1)}), bf16[128,16,128]{2,1,0:T(8,128)(2,1)S(1)}, u32[]{:S(2)}, u32[]{:S(2)}) async-start(bf16[128,16,128]{2,1,0:T(8,128)(2,1)} %bitcast.6.refs_11_), calls=%async_computation.3 | async-start | bytes 1048576 | tf_op jit(solution)/shard_map/all_to_all | solution.py:361
  93.6 0.0 copy-start
  93.6 2.9 %shard_map.152 = (bf16[512,1024]{1,0:T(8,128)(2,1)S(1)}, bf16[128,1024]{1,0:T(8,128)(2,1)S(1)}, bf16[128,1024]{1,0:T(8,128)(2,1)S(1)}, f32[128,1024]{1,0:T(8,128)S(1)}, f32[384,128]{1,0:T(8,128)S(1)}) custom-call(bf16[32,32,128]{2,1,0:T(8,128)(2,1)} %refs_1_.7, bf16[32,32,128]{2,1,0:T(8,128)(2,1)} %refs_1_.5, s32[32,32]{1,0:T(8,128)} %refs_2_.3, ...), custom_call_target="tpu_custom_call" | custom-call | flops 500000000 | bytes 3807232 | tf_op jit(solution)/shard_map/pallas_call | solution.py:87
  96.5 9.3 %all-to-all-done.3.refs_0_ = bf16[128,16,128]{2,1,0:T(8,128)(2,1)S(1)} async-done(((bf16[128,16,128]{2,1,0:T(8,128)(2,1)}), bf16[128,16,128]{2,1,0:T(8,128)(2,1)S(1)}, u32[]{:S(2)}, u32[]{:S(2)}) %all-to-all-start.3) | async-done | bytes 524320 | tf_op jit(solution)/shard_map/all_to_all | solution.py:361
  105.8 0.0 copy-done
  105.8 1.7 %shard_map.153 = (bf16[128,8,128]{2,1,0:T(8,128)(2,1)S(1)}, f32[128,1024]{1,0:T(8,128)}) custom-call(bf16[128,16,128]{2,1,0:T(8,128)(2,1)S(1)} %all-to-all-done.3.refs_0_, bf16[128,512]{1,0:T(8,128)(2,1)S(1)} %copy-done, bf16[512,1024]{1,0:T(8,128)(2,1)S(1)} %get-tuple-element.38.refs_2_, bf16[128,1024]{1,0:T(8,128)(2,1)S(1)} %get-tuple-element.39.refs_3_, ...), custom_call_target="tpu_custom_call" | custom-call | flops 2000000 | bytes 3735552 | tf_op jit(solution)/shard_map/pallas_call | solution.py:87
  107.5 13.0 %all_to_all.38.refs_0_ = bf16[32,32,128]{2,1,0:T(8,128)(2,1)S(1)} all-to-all(bf16[32,32,128]{2,1,0:T(8,128)(2,1)S(1)} %bitcast.15), channel_id=1, replica_groups={{137,141,129,133,201,205,193,197,9,13,1,5,73,77,65,69,136,140,128,132,2..., dimensions={0} | all-to-all | bytes 524288 | tf_op jit(solution)/shard_map/all_to_all | solution.py:361
  120.5 0.7 shard_map.155
  121.2 6.8 %all-to-all-start.5 = ((bf16[8,32,128]{2,1,0:T(8,128)(2,1)}), bf16[8,32,128]{2,1,0:T(8,128)(2,1)S(1)}, u32[]{:S(2)}, u32[]{:S(2)}) async-start(bf16[8,32,128]{2,1,0:T(8,128)(2,1)} %shard_map.155), calls=%async_computation.5 | async-start | bytes 131072 | tf_op jit(solution)/shard_map/all_to_all | solution.py:361
  128.0 2.3 %shard_map.154.refs_1_ = bf16[32,32,128]{2,1,0:T(8,128)(2,1)} custom-call(f32[128,1024]{1,0:T(8,128)} %get-tuple-element.43.refs_0_, bf16[32,32,128]{2,1,0:T(8,128)(2,1)} %refs_1_.7, f32[1,128]{1,0:T(1,128)} %bitcast.22), custom_call_target="tpu_custom_call" | custom-call | flops 500000000 | bytes 1049088 | tf_op jit(solution)/shard_map/pallas_call | solution.py:87
  130.3 0.0 all-to-all-done.5.refs_0_
  130.4 12.7 %all_to_all.39 = bf16[32,32,128]{2,1,0:T(8,128)(2,1)S(1)} all-to-all(bf16[32,32,128]{2,1,0:T(8,128)(2,1)S(1)} %shard_map.156), channel_id=1, replica_groups={{137,141,129,133,201,205,193,197,9,13,1,5,73,77,65,69,136,140,128,132,2..., dimensions={0} | all-to-all | bytes 524288 | tf_op jit(solution)/shard_map/all_to_all | solution.py:361
  143.1 0.8 shard_map.157
  (1 shorter events, 0.0 us)
Async XLA Ops:
  33.0 3.3 %collective-permute-start = (bf16[128,8,128]{2,1,0:T(8,128)(2,1)S(1)}, bf16[128,8,128]{2,1,0:T(8,128)(2,1)S(1)}, u32[]{:S(2)}, u32[]{:S(2)}) collective-permute-start(bf16[128,8,128]{2,1,0:T(8,128)(2,1)S(1)} %get-tuple-element.33), channel_id=1, source_target_pairs={{0,1},{1,0},{2,3},{3,2},{4,5},{5,4},{6,7},{7,6},{8,9},{9,8},{10,11... | collective-permute-start | bytes 786440 | tf_op jit(solution)/shard_map/ppermute | solution.py:357
  74.9 4.0 %collective-permute-start.1 = (bf16[128,8,128]{2,1,0:T(8,128)(2,1)S(1)}, bf16[128,8,128]{2,1,0:T(8,128)(2,1)S(1)}, u32[]{:S(2)}, u32[]{:S(2)}) collective-permute-start(bf16[128,8,128]{2,1,0:T(8,128)(2,1)S(1)} %all_to_all.37.refs_1_), channel_id=1, source_target_pairs={{0,1},{1,0},{2,3},{3,2},{4,5},{5,4},{6,7},{7,6},{8,9},{9,8},{10,11... | collective-permute-start | bytes 786440 | tf_op jit(solution)/shard_map/ppermute | solution.py:357
  80.4 25.4 %all-to-all-start.3 = ((bf16[128,16,128]{2,1,0:T(8,128)(2,1)}), bf16[128,16,128]{2,1,0:T(8,128)(2,1)S(1)}, u32[]{:S(2)}, u32[]{:S(2)}) async-start(bf16[128,16,128]{2,1,0:T(8,128)(2,1)} %bitcast.6.refs_11_), calls=%async_computation.3 | async-start | bytes 1048576 | tf_op jit(solution)/shard_map/all_to_all | solution.py:361
  93.6 12.3 %copy-start = (bf16[128,512]{1,0:T(8,128)(2,1)S(1)}, bf16[128,512]{1,0:T(8,128)(2,1)}, u32[]{:S(2)}) copy-start(bf16[128,512]{1,0:T(8,128)(2,1)} %refs_1_.6) | copy-start | bytes 393220
  121.2 9.2 %all-to-all-start.5 = ((bf16[8,32,128]{2,1,0:T(8,128)(2,1)}), bf16[8,32,128]{2,1,0:T(8,128)(2,1)S(1)}, u32[]{:S(2)}, u32[]{:S(2)}) async-start(bf16[8,32,128]{2,1,0:T(8,128)(2,1)} %shard_map.155), calls=%async_computation.5 | async-start | bytes 131072 | tf_op jit(solution)/shard_map/all_to_all | solution.py:361

commit v7 on v6

--- a/solution.py
+++ b/solution.py
@@ -22,7 +22,7 @@
 PLANE = ("z_lo", "y", "x", "z_hi")
 FLAT = ("depth", "y", "x")
 UPRIGHT = ("z_lo", "z_hi")
-ORIGINS = {PLANE: (2, 2, 2, 1, 0), FLAT: (2, 0, 2, 0, 1), UPRIGHT: (0, 0, 0, 1, 0)}
+ORIGINS = {PLANE: (3, 2, 3, 1, 0), FLAT: (2, 0, 2, 0, 1), UPRIGHT: (0, 0, 0, 1, 0)}
 PARTS = 32
 PEERS = 8
 PART = CELLS // PARTS
@@ -298,7 +298,7 @@
 
 
 def project_kernel(
-    recv, in_proj, coef, normed, zhat, partial, early, send, d_normed, scratch, packed, kept, sem
+    recv, in_proj, coef, normed, zhat, partial, early, send, d_normed, scratch, packed
 ):
     scratch[...] = recv[...].astype(F32).reshape(2 * CELLS, CH)
     da = from_tiles(scratch, 0, 2 * SUB)
@@ -312,9 +312,7 @@
     )
     g_in = dot(normed[...], d_proj, 1, 1)
     grad = dot(in_proj[...], d_proj, 1, 0) + partial[...]
-    kept[...] = grad
-    copy = pltpu.make_async_copy(kept, d_normed, sem)
-    copy.start()
+    d_normed[...] = grad
     for part in range(4):
         packed[pl.ds(part, CH, stride=SUB), :] = g_in[:, part * CH : (part + 1) * CH]
     packed[pl.ds(4, CH, stride=SUB), :] = early[0:CH]
@@ -324,7 +322,6 @@
     )
     packed[pl.ds(7, CH, stride=SUB), :] = jnp.zeros((CH, CH), F32)
     send[...] = packed[...].reshape(CH, SUB, CH).astype(BF16)
-    copy.wait()
 
 
 def pair_kernel(d_normed, pair, gain, out):
@@ -476,10 +473,7 @@
         scratch=[
             pairs_of_tiles,
             tiles,
-            pltpu.VMEM((CH, CELLS), F32),
-            pltpu.SemaphoreType.DMA,
         ],
-        hbm_outs=(1,),
     )
     weights = exchange(weights.reshape(PARTS, PART, CH), FLAT)
     (grad_pair,) = call(
@@ -489,7 +483,7 @@
         pair,
         in_gain,
         flops=500_000_000,
-        fetched=range(3),
+        fetched=(1, 2),
     )
     (totals,) = call(
         total_kernel, [struct((PEERS, PART, CH), BF16)], weights

time: 144 us -> 144 us (level)
  transfers between devices with their start and end apart: 4 -> 4, of which waited for: 3 -> 4; matrix products, arithmetic and copies ran while one was open for 0% -> 0% of each run, Pallas kernels for 5% -> 5%
where the time goes in v7:
time: 144 us
  blocking collectives  92.5 us (64%)
  starting transfers between devices  24 us (17%)
  Pallas kernels  14.9 us (10%)
  waiting for transfers between devices  11 us (8%)
    all_to_all x5, blocking collectives, exchange(): lax.all_to_all(value, AXES, 0, 0, tiled=True, axis_index_groups=groups(ax...  92.5 us
    all_to_all x2, starting transfers between devices, exchange(): lax.all_to_all(value, AXES, 0, 0, tiled=True, axis_index_groups=groups(ax...  18.9 us
    pallas_call x13, Pallas kernels, call(): pl.pallas_call(body, out_shape=[pltpu.HBM(o.shape, o.dtype) if i in hbm_o...  14.9 us
    all_to_all x2, waiting for transfers between devices, exchange(): lax.all_to_all(value, AXES, 0, 0, tiled=True, axis_index_groups=groups(ax...  10.4 us
    ppermute x2, starting transfers between devices, swap_cores(): return lax.ppermute(value, 'depth', [(0, 1), (1, 0)])  5.08 us
  transfers between devices with their start and end apart: 4, of which 4 were waited for; matrix products, arithmetic and copies ran while one was open for 0% of the time, Pallas kernels for 5%

profile of v7, /device:TPU:1, one launch (start us, length us, event | category | flops | bytes accessed | tf_op | source)
XLA Modules:
  0.0 143.9 jit_solution(9441571146392095397)
XLA Ops:
  0.6 2.4 %shard_map.145 = (bf16[128,16,128]{2,1,0:T(8,128)(2,1)S(1)}, f32[128,1024]{1,0:T(8,128)S(1)}) custom-call(bf16[32,32,128]{2,1,0:T(8,128)(2,1)} %refs_1_.7, bf16[32,32,128]{2,1,0:T(8,128)(2,1)} %refs_1_.5, s32[32,32]{1,0:T(8,128)} %refs_2_.3, f32[1,128]{1,0:T(1,128)} %bitcast.20, f32[1,128]{1,0:T(1,128)} %bitcast.16, f32[1,128]{1,0:T(1,128)} %bitcast.18, ...), custom_call_target="tpu_custom_call" | custom-call | flops 2000000 | bytes 1775104 | tf_op jit(solution)/shard_map/pallas_call | solution.py:87
  3.1 29.7 %all_to_all.35 = bf16[128,16,128]{2,1,0:T(8,128)(2,1)S(1)} all-to-all(bf16[128,16,128]{2,1,0:T(8,128)(2,1)S(1)} %get-tuple-element.30), channel_id=1, replica_groups={{238,236,226,224,230,228,234,232,46,44,34,32,38,36,42,40,110,108,98,96,..., dimensions={0} | all-to-all | bytes 1048576 | tf_op jit(solution)/shard_map/all_to_all | solution.py:358
  32.8 0.9 shard_map.146
  33.7 1.9 %collective-permute-start = (bf16[128,8,128]{2,1,0:T(8,128)(2,1)S(1)}, bf16[128,8,128]{2,1,0:T(8,128)(2,1)S(1)}, u32[]{:S(2)}, u32[]{:S(2)}) collective-permute-start(bf16[128,8,128]{2,1,0:T(8,128)(2,1)S(1)} %get-tuple-element.33), channel_id=1, source_target_pairs={{0,1},{1,0},{2,3},{3,2},{4,5},{5,4},{6,7},{7,6},{8,9},{9,8},{10,11... | collective-permute-start | bytes 786440 | tf_op jit(solution)/shard_map/ppermute | solution.py:354
  35.6 1.0 shard_map.147
  36.6 0.2 collective-permute-done.refs_1_
  36.8 0.1 shard_map.148
  36.9 19.4 %all_to_all.36.refs_0_.refs_10_ = bf16[128,8,128]{2,1,0:T(8,128)(2,1)S(1)} all-to-all(bf16[128,8,128]{2,1,0:T(8,128)(2,1)S(1)} %shard_map.148), channel_id=1, replica_groups={{238,236,226,224,230,228,234,232,46,44,34,32,38,36,42,40,110,108,98,96,..., dimensions={0} | all-to-all | bytes 524288 | tf_op jit(solution)/shard_map/all_to_all | solution.py:358
  56.3 0.5 shard_map.149
  56.8 18.3 %all_to_all.37.refs_1_ = bf16[128,8,128]{2,1,0:T(8,128)(2,1)S(1)} all-to-all(bf16[128,8,128]{2,1,0:T(8,128)(2,1)S(1)} %shard_map.149), channel_id=1, replica_groups={{238,236,226,224,230,228,234,232,46,44,34,32,38,36,42,40,110,108,98,96,..., dimensions={0} | all-to-all | bytes 524288 | tf_op jit(solution)/shard_map/all_to_all | solution.py:358
  75.1 3.1 %collective-permute-start.1 = (bf16[128,8,128]{2,1,0:T(8,128)(2,1)S(1)}, bf16[128,8,128]{2,1,0:T(8,128)(2,1)S(1)}, u32[]{:S(2)}, u32[]{:S(2)}) collective-permute-start(bf16[128,8,128]{2,1,0:T(8,128)(2,1)S(1)} %all_to_all.37.refs_1_), channel_id=1, source_target_pairs={{0,1},{1,0},{2,3},{3,2},{4,5},{5,4},{6,7},{7,6},{8,9},{9,8},{10,11... | collective-permute-start | bytes 786440 | tf_op jit(solution)/shard_map/ppermute | solution.py:354
  78.2 0.8 shard_map.150
  79.0 0.4 collective-permute-done.1.refs_1_
  79.4 1.6 %shard_map.151 = bf16[2,2,4,8,16,128]{5,4,3,2,1,0:T(8,128)(2,1)} custom-call(s32[1]{0:T(128)} %bitcast.3.refs_0_, bf16[128,8,128]{2,1,0:T(8,128)(2,1)S(1)} %collective-permute-done.1.refs_1_, bf16[512,256]{1,0:T(8,128)(2,1)S(1)} %get-tuple-element.31.refs_2_, bf16[2,2,128,256]{3,2,1,0:T(8,128)(2,1)S(1)} %bitcast.13, ...), custom_call_target="tpu_custom_call" | custom-call | flops 2000000 | bytes 1966084 | tf_op jit(solution)/shard_map/pallas_call | solution.py:87
  81.0 12.0 %all-to-all-start.3 = ((bf16[128,16,128]{2,1,0:T(8,128)(2,1)}), bf16[128,16,128]{2,1,0:T(8,128)(2,1)S(1)}, u32[]{:S(2)}, u32[]{:S(2)}) async-start(bf16[128,16,128]{2,1,0:T(8,128)(2,1)} %bitcast.6.refs_11_), calls=%async_computation.3 | async-start | bytes 1048576 | tf_op jit(solution)/shard_map/all_to_all | solution.py:358
  93.0 0.0 copy-start
  93.0 2.9 %shard_map.152 = (bf16[512,1024]{1,0:T(8,128)(2,1)S(1)}, bf16[128,1024]{1,0:T(8,128)(2,1)S(1)}, bf16[128,1024]{1,0:T(8,128)(2,1)S(1)}, f32[128,1024]{1,0:T(8,128)S(1)}, f32[384,128]{1,0:T(8,128)S(1)}) custom-call(bf16[32,32,128]{2,1,0:T(8,128)(2,1)} %refs_1_.7, bf16[32,32,128]{2,1,0:T(8,128)(2,1)} %refs_1_.5, s32[32,32]{1,0:T(8,128)} %refs_2_.3, ...), custom_call_target="tpu_custom_call" | custom-call | flops 500000000 | bytes 3807232 | tf_op jit(solution)/shard_map/pallas_call | solution.py:87
  96.0 10.2 %all-to-all-done.3.refs_0_ = bf16[128,16,128]{2,1,0:T(8,128)(2,1)S(1)} async-done(((bf16[128,16,128]{2,1,0:T(8,128)(2,1)}), bf16[128,16,128]{2,1,0:T(8,128)(2,1)S(1)}, u32[]{:S(2)}, u32[]{:S(2)}) %all-to-all-start.3) | async-done | bytes 524320 | tf_op jit(solution)/shard_map/all_to_all | solution.py:358
  106.2 0.0 copy-done
  106.2 0.9 shard_map.153
  107.2 0.0 copy-start.1
  107.2 0.8 copy-done.1
  107.9 0.0 copy-start.2
  107.9 12.4 %all_to_all.38.refs_0_ = bf16[32,32,128]{2,1,0:T(8,128)(2,1)S(1)} all-to-all(bf16[32,32,128]{2,1,0:T(8,128)(2,1)S(1)} %bitcast.15), channel_id=1, replica_groups={{137,141,129,133,201,205,193,197,9,13,1,5,73,77,65,69,136,140,128,132,2..., dimensions={0} | all-to-all | bytes 524288 | tf_op jit(solution)/shard_map/all_to_all | solution.py:358
  120.3 0.7 shard_map.155
  121.0 6.8 %all-to-all-start.5 = ((bf16[8,32,128]{2,1,0:T(8,128)(2,1)}), bf16[8,32,128]{2,1,0:T(8,128)(2,1)S(1)}, u32[]{:S(2)}, u32[]{:S(2)}) async-start(bf16[8,32,128]{2,1,0:T(8,128)(2,1)} %shard_map.155), calls=%async_computation.5 | async-start | bytes 131072 | tf_op jit(solution)/shard_map/all_to_all | solution.py:358
  127.9 0.0 copy-done.2
  127.9 2.2 %shard_map.154.refs_1_ = bf16[32,32,128]{2,1,0:T(8,128)(2,1)} custom-call(f32[128,1024]{1,0:T(8,128)S(1)} %copy-done.2, bf16[32,32,128]{2,1,0:T(8,128)(2,1)} %refs_1_.7, f32[1,128]{1,0:T(1,128)} %bitcast.22), custom_call_target="tpu_custom_call" | custom-call | flops 500000000 | bytes 1049088 | tf_op jit(solution)/shard_map/pallas_call | solution.py:87
  130.0 0.2 all-to-all-done.5.refs_0_
  130.3 12.7 %all_to_all.39 = bf16[32,32,128]{2,1,0:T(8,128)(2,1)S(1)} all-to-all(bf16[32,32,128]{2,1,0:T(8,128)(2,1)S(1)} %shard_map.156), channel_id=1, replica_groups={{137,141,129,133,201,205,193,197,9,13,1,5,73,77,65,69,136,140,128,132,2..., dimensions={0} | all-to-all | bytes 524288 | tf_op jit(solution)/shard_map/all_to_all | solution.py:358
  143.0 0.8 shard_map.157
  (1 shorter events, 0.0 us)
Async XLA Ops:
  33.7 3.1 %collective-permute-start = (bf16[128,8,128]{2,1,0:T(8,128)(2,1)S(1)}, bf16[128,8,128]{2,1,0:T(8,128)(2,1)S(1)}, u32[]{:S(2)}, u32[]{:S(2)}) collective-permute-start(bf16[128,8,128]{2,1,0:T(8,128)(2,1)S(1)} %get-tuple-element.33), channel_id=1, source_target_pairs={{0,1},{1,0},{2,3},{3,2},{4,5},{5,4},{6,7},{7,6},{8,9},{9,8},{10,11... | collective-permute-start | bytes 786440 | tf_op jit(solution)/shard_map/ppermute | solution.py:354
  75.1 4.3 %collective-permute-start.1 = (bf16[128,8,128]{2,1,0:T(8,128)(2,1)S(1)}, bf16[128,8,128]{2,1,0:T(8,128)(2,1)S(1)}, u32[]{:S(2)}, u32[]{:S(2)}) collective-permute-start(bf16[128,8,128]{2,1,0:T(8,128)(2,1)S(1)} %all_to_all.37.refs_1_), channel_id=1, source_target_pairs={{0,1},{1,0},{2,3},{3,2},{4,5},{5,4},{6,7},{7,6},{8,9},{9,8},{10,11... | collective-permute-start | bytes 786440 | tf_op jit(solution)/shard_map/ppermute | solution.py:354
  81.0 25.2 %all-to-all-start.3 = ((bf16[128,16,128]{2,1,0:T(8,128)(2,1)}), bf16[128,16,128]{2,1,0:T(8,128)(2,1)S(1)}, u32[]{:S(2)}, u32[]{:S(2)}) async-start(bf16[128,16,128]{2,1,0:T(8,128)(2,1)} %bitcast.6.refs_11_), calls=%async_computation.3 | async-start | bytes 1048576 | tf_op jit(solution)/shard_map/all_to_all | solution.py:358
  93.0 13.2 %copy-start = (bf16[128,512]{1,0:T(8,128)(2,1)S(1)}, bf16[128,512]{1,0:T(8,128)(2,1)}, u32[]{:S(2)}) copy-start(bf16[128,512]{1,0:T(8,128)(2,1)} %refs_1_.6) | copy-start | bytes 393220
  107.2 0.8 copy-start.1
  107.9 19.9 %copy-start.2 = (f32[128,1024]{1,0:T(8,128)S(1)}, f32[128,1024]{1,0:T(8,128)}, u32[]{:S(2)}) copy-start(f32[128,1024]{1,0:T(8,128)} %copy-done.1) | copy-start | bytes 1572868
  121.0 9.2 %all-to-all-start.5 = ((bf16[8,32,128]{2,1,0:T(8,128)(2,1)}), bf16[8,32,128]{2,1,0:T(8,128)(2,1)S(1)}, u32[]{:S(2)}, u32[]{:S(2)}) async-start(bf16[8,32,128]{2,1,0:T(8,128)(2,1)} %shard_map.155), calls=%async_computation.5 | async-start | bytes 131072 | tf_op jit(solution)/shard_map/all_to_all | solution.py:358

commit v8 on v6

--- a/solution.py
+++ b/solution.py
@@ -22,7 +22,7 @@
 PLANE = ("z_lo", "y", "x", "z_hi")
 FLAT = ("depth", "y", "x")
 UPRIGHT = ("z_lo", "z_hi")
-ORIGINS = {PLANE: (2, 2, 2, 1, 0), FLAT: (2, 0, 2, 0, 1), UPRIGHT: (0, 0, 0, 1, 0)}
+ORIGINS = {PLANE: (3, 2, 3, 1, 0), FLAT: (2, 0, 2, 0, 1), UPRIGHT: (0, 0, 0, 1, 0)}
 PARTS = 32
 PEERS = 8
 PART = CELLS // PARTS

time: 144 us -> 144 us (level)
  no operation moved by 1% of the time
where the time goes in v8:
time: 144 us
  blocking collectives  92.4 us (64%)
  starting transfers between devices  24 us (17%)
  Pallas kernels  15.7 us (11%)
  waiting for transfers between devices  10.8 us (8%)
    all_to_all x5, blocking collectives, exchange(): lax.all_to_all(value, AXES, 0, 0, tiled=True, axis_index_groups=groups(ax...  92.4 us
    all_to_all x2, starting transfers between devices, exchange(): lax.all_to_all(value, AXES, 0, 0, tiled=True, axis_index_groups=groups(ax...  18.9 us
    pallas_call x13, Pallas kernels, call(): pl.pallas_call(body, out_shape=[pltpu.HBM(o.shape, o.dtype) if i in hbm_o...  15.7 us
    all_to_all x2, waiting for transfers between devices, exchange(): lax.all_to_all(value, AXES, 0, 0, tiled=True, axis_index_groups=groups(ax...  10.3 us
    ppermute x2, starting transfers between devices, swap_cores(): return lax.ppermute(value, 'depth', [(0, 1), (1, 0)])  5.08 us
  transfers between devices with their start and end apart: 4, of which 3 were waited for; matrix products, arithmetic and copies ran while one was open for 0% of the time, Pallas kernels for 5%

profile of v8, /device:TPU:1, one launch (start us, length us, event | category | flops | bytes accessed | tf_op | source)
XLA Modules:
  0.0 143.7 jit_solution(14905037508333145163)
XLA Ops:
  0.6 2.4 %shard_map.145 = (bf16[128,16,128]{2,1,0:T(8,128)(2,1)S(1)}, f32[128,1024]{1,0:T(8,128)S(1)}) custom-call(bf16[32,32,128]{2,1,0:T(8,128)(2,1)} %refs_1_.7, bf16[32,32,128]{2,1,0:T(8,128)(2,1)} %refs_1_.5, s32[32,32]{1,0:T(8,128)} %refs_2_.3, f32[1,128]{1,0:T(1,128)} %bitcast.20, f32[1,128]{1,0:T(1,128)} %bitcast.16, f32[1,128]{1,0:T(1,128)} %bitcast.18, ...), custom_call_target="tpu_custom_call" | custom-call | flops 2000000 | bytes 1775104 | tf_op jit(solution)/shard_map/pallas_call | solution.py:87
  3.1 29.7 %all_to_all.35 = bf16[128,16,128]{2,1,0:T(8,128)(2,1)S(1)} all-to-all(bf16[128,16,128]{2,1,0:T(8,128)(2,1)S(1)} %get-tuple-element.30), channel_id=1, replica_groups={{238,236,226,224,230,228,234,232,46,44,34,32,38,36,42,40,110,108,98,96,..., dimensions={0} | all-to-all | bytes 1048576 | tf_op jit(solution)/shard_map/all_to_all | solution.py:361
  32.8 0.9 shard_map.146
  33.7 1.9 %collective-permute-start = (bf16[128,8,128]{2,1,0:T(8,128)(2,1)S(1)}, bf16[128,8,128]{2,1,0:T(8,128)(2,1)S(1)}, u32[]{:S(2)}, u32[]{:S(2)}) collective-permute-start(bf16[128,8,128]{2,1,0:T(8,128)(2,1)S(1)} %get-tuple-element.33), channel_id=1, source_target_pairs={{0,1},{1,0},{2,3},{3,2},{4,5},{5,4},{6,7},{7,6},{8,9},{9,8},{10,11... | collective-permute-start | bytes 786440 | tf_op jit(solution)/shard_map/ppermute | solution.py:357
  35.6 1.0 shard_map.147
  36.6 0.2 collective-permute-done.refs_1_
  36.8 0.1 shard_map.148
  36.9 19.4 %all_to_all.36.refs_0_.refs_10_ = bf16[128,8,128]{2,1,0:T(8,128)(2,1)S(1)} all-to-all(bf16[128,8,128]{2,1,0:T(8,128)(2,1)S(1)} %shard_map.148), channel_id=1, replica_groups={{238,236,226,224,230,228,234,232,46,44,34,32,38,36,42,40,110,108,98,96,..., dimensions={0} | all-to-all | bytes 524288 | tf_op jit(solution)/shard_map/all_to_all | solution.py:361
  56.3 0.5 shard_map.149
  56.8 18.3 %all_to_all.37.refs_1_ = bf16[128,8,128]{2,1,0:T(8,128)(2,1)S(1)} all-to-all(bf16[128,8,128]{2,1,0:T(8,128)(2,1)S(1)} %shard_map.149), channel_id=1, replica_groups={{238,236,226,224,230,228,234,232,46,44,34,32,38,36,42,40,110,108,98,96,..., dimensions={0} | all-to-all | bytes 524288 | tf_op jit(solution)/shard_map/all_to_all | solution.py:361
  75.1 3.1 %collective-permute-start.1 = (bf16[128,8,128]{2,1,0:T(8,128)(2,1)S(1)}, bf16[128,8,128]{2,1,0:T(8,128)(2,1)S(1)}, u32[]{:S(2)}, u32[]{:S(2)}) collective-permute-start(bf16[128,8,128]{2,1,0:T(8,128)(2,1)S(1)} %all_to_all.37.refs_1_), channel_id=1, source_target_pairs={{0,1},{1,0},{2,3},{3,2},{4,5},{5,4},{6,7},{7,6},{8,9},{9,8},{10,11... | collective-permute-start | bytes 786440 | tf_op jit(solution)/shard_map/ppermute | solution.py:357
  78.2 0.8 shard_map.150
  79.0 0.4 collective-permute-done.1.refs_1_
  79.4 1.6 %shard_map.151 = bf16[2,2,4,8,16,128]{5,4,3,2,1,0:T(8,128)(2,1)} custom-call(s32[1]{0:T(128)} %bitcast.3.refs_0_, bf16[128,8,128]{2,1,0:T(8,128)(2,1)S(1)} %collective-permute-done.1.refs_1_, bf16[512,256]{1,0:T(8,128)(2,1)S(1)} %get-tuple-element.31.refs_2_, bf16[2,2,128,256]{3,2,1,0:T(8,128)(2,1)S(1)} %bitcast.13, ...), custom_call_target="tpu_custom_call" | custom-call | flops 2000000 | bytes 1966084 | tf_op jit(solution)/shard_map/pallas_call | solution.py:87
  81.0 12.0 %all-to-all-start.3 = ((bf16[128,16,128]{2,1,0:T(8,128)(2,1)}), bf16[128,16,128]{2,1,0:T(8,128)(2,1)S(1)}, u32[]{:S(2)}, u32[]{:S(2)}) async-start(bf16[128,16,128]{2,1,0:T(8,128)(2,1)} %bitcast.6.refs_11_), calls=%async_computation.3 | async-start | bytes 1048576 | tf_op jit(solution)/shard_map/all_to_all | solution.py:361
  93.0 0.0 copy-start
  93.0 2.9 %shard_map.152 = (bf16[512,1024]{1,0:T(8,128)(2,1)S(1)}, bf16[128,1024]{1,0:T(8,128)(2,1)S(1)}, bf16[128,1024]{1,0:T(8,128)(2,1)S(1)}, f32[128,1024]{1,0:T(8,128)S(1)}, f32[384,128]{1,0:T(8,128)S(1)}) custom-call(bf16[32,32,128]{2,1,0:T(8,128)(2,1)} %refs_1_.7, bf16[32,32,128]{2,1,0:T(8,128)(2,1)} %refs_1_.5, s32[32,32]{1,0:T(8,128)} %refs_2_.3, ...), custom_call_target="tpu_custom_call" | custom-call | flops 500000000 | bytes 3807232 | tf_op jit(solution)/shard_map/pallas_call | solution.py:87
  96.0 10.2 %all-to-all-done.3.refs_0_ = bf16[128,16,128]{2,1,0:T(8,128)(2,1)S(1)} async-done(((bf16[128,16,128]{2,1,0:T(8,128)(2,1)}), bf16[128,16,128]{2,1,0:T(8,128)(2,1)S(1)}, u32[]{:S(2)}, u32[]{:S(2)}) %all-to-all-start.3) | async-done | bytes 524320 | tf_op jit(solution)/shard_map/all_to_all | solution.py:361
  106.2 0.0 copy-done
  106.2 1.6 %shard_map.153 = (bf16[128,8,128]{2,1,0:T(8,128)(2,1)S(1)}, f32[128,1024]{1,0:T(8,128)}) custom-call(bf16[128,16,128]{2,1,0:T(8,128)(2,1)S(1)} %all-to-all-done.3.refs_0_, bf16[128,512]{1,0:T(8,128)(2,1)S(1)} %copy-done, bf16[512,1024]{1,0:T(8,128)(2,1)S(1)} %get-tuple-element.38.refs_2_, bf16[128,1024]{1,0:T(8,128)(2,1)S(1)} %get-tuple-element.39.refs_3_, ...), custom_call_target="tpu_custom_call" | custom-call | flops 2000000 | bytes 3735552 | tf_op jit(solution)/shard_map/pallas_call | solution.py:87
  107.9 12.3 %all_to_all.38.refs_0_ = bf16[32,32,128]{2,1,0:T(8,128)(2,1)S(1)} all-to-all(bf16[32,32,128]{2,1,0:T(8,128)(2,1)S(1)} %bitcast.15), channel_id=1, replica_groups={{137,141,129,133,201,205,193,197,9,13,1,5,73,77,65,69,136,140,128,132,2..., dimensions={0} | all-to-all | bytes 524288 | tf_op jit(solution)/shard_map/all_to_all | solution.py:361
  120.1 0.7 shard_map.155
  120.8 6.9 %all-to-all-start.5 = ((bf16[8,32,128]{2,1,0:T(8,128)(2,1)}), bf16[8,32,128]{2,1,0:T(8,128)(2,1)S(1)}, u32[]{:S(2)}, u32[]{:S(2)}) async-start(bf16[8,32,128]{2,1,0:T(8,128)(2,1)} %shard_map.155), calls=%async_computation.5 | async-start | bytes 131072 | tf_op jit(solution)/shard_map/all_to_all | solution.py:361
  127.7 2.3 %shard_map.154.refs_1_ = bf16[32,32,128]{2,1,0:T(8,128)(2,1)} custom-call(f32[128,1024]{1,0:T(8,128)} %get-tuple-element.43.refs_0_, bf16[32,32,128]{2,1,0:T(8,128)(2,1)} %refs_1_.7, f32[1,128]{1,0:T(1,128)} %bitcast.22), custom_call_target="tpu_custom_call" | custom-call | flops 500000000 | bytes 1049088 | tf_op jit(solution)/shard_map/pallas_call | solution.py:87
  130.0 0.0 all-to-all-done.5.refs_0_
  130.1 12.7 %all_to_all.39 = bf16[32,32,128]{2,1,0:T(8,128)(2,1)S(1)} all-to-all(bf16[32,32,128]{2,1,0:T(8,128)(2,1)S(1)} %shard_map.156), channel_id=1, replica_groups={{137,141,129,133,201,205,193,197,9,13,1,5,73,77,65,69,136,140,128,132,2..., dimensions={0} | all-to-all | bytes 524288 | tf_op jit(solution)/shard_map/all_to_all | solution.py:361
  142.8 0.8 shard_map.157
  (1 shorter events, 0.0 us)
Async XLA Ops:
  33.7 3.1 %collective-permute-start = (bf16[128,8,128]{2,1,0:T(8,128)(2,1)S(1)}, bf16[128,8,128]{2,1,0:T(8,128)(2,1)S(1)}, u32[]{:S(2)}, u32[]{:S(2)}) collective-permute-start(bf16[128,8,128]{2,1,0:T(8,128)(2,1)S(1)} %get-tuple-element.33), channel_id=1, source_target_pairs={{0,1},{1,0},{2,3},{3,2},{4,5},{5,4},{6,7},{7,6},{8,9},{9,8},{10,11... | collective-permute-start | bytes 786440 | tf_op jit(solution)/shard_map/ppermute | solution.py:357
  75.1 4.3 %collective-permute-start.1 = (bf16[128,8,128]{2,1,0:T(8,128)(2,1)S(1)}, bf16[128,8,128]{2,1,0:T(8,128)(2,1)S(1)}, u32[]{:S(2)}, u32[]{:S(2)}) collective-permute-start(bf16[128,8,128]{2,1,0:T(8,128)(2,1)S(1)} %all_to_all.37.refs_1_), channel_id=1, source_target_pairs={{0,1},{1,0},{2,3},{3,2},{4,5},{5,4},{6,7},{7,6},{8,9},{9,8},{10,11... | collective-permute-start | bytes 786440 | tf_op jit(solution)/shard_map/ppermute | solution.py:357
  81.0 25.2 %all-to-all-start.3 = ((bf16[128,16,128]{2,1,0:T(8,128)(2,1)}), bf16[128,16,128]{2,1,0:T(8,128)(2,1)S(1)}, u32[]{:S(2)}, u32[]{:S(2)}) async-start(bf16[128,16,128]{2,1,0:T(8,128)(2,1)} %bitcast.6.refs_11_), calls=%async_computation.3 | async-start | bytes 1048576 | tf_op jit(solution)/shard_map/all_to_all | solution.py:361
  93.0 13.2 %copy-start = (bf16[128,512]{1,0:T(8,128)(2,1)S(1)}, bf16[128,512]{1,0:T(8,128)(2,1)}, u32[]{:S(2)}) copy-start(bf16[128,512]{1,0:T(8,128)(2,1)} %refs_1_.6) | copy-start | bytes 393220
  120.8 9.2 %all-to-all-start.5 = ((bf16[8,32,128]{2,1,0:T(8,128)(2,1)}), bf16[8,32,128]{2,1,0:T(8,128)(2,1)S(1)}, u32[]{:S(2)}, u32[]{:S(2)}) async-start(bf16[8,32,128]{2,1,0:T(8,128)(2,1)} %shard_map.155), calls=%async_computation.5 | async-start | bytes 131072 | tf_op jit(solution)/shard_map/all_to_all | solution.py:361
